TPU v7x, 512 devices: a whole 4x8x8 slice. The times are simulated.
512 devices in a mesh: fsdp: 32 (over z, y_hi, core), expert: 16 (over x, y_lo).
Axes of the slice: x: 4, y: 8 (y_hi: 2, y_lo: 4; y = y_hi * 4 + y_lo), z: 8, core: 2. Of those that a mesh axis runs over, the one named last changes fastest.
Arguments:
- latent: bfloat16 [65536, 512], P(('fsdp', 'expert')), may hold values from -6 to 6
- routes: int32 [65536, 2], P(('fsdp', 'expert')), may hold values from 0 to 15, all different within a row; in each aligned block of 128 rows (0 to 127, 128 to 255, ...) at most 32 rows name the same one
- scores: float32 [65536, 2], P(('fsdp', 'expert')), may hold values from 0.2 to 1
- cotangent: bfloat16 [65536, 512], P(('fsdp', 'expert')), may hold values from -6 to 6
- w_gate: bfloat16 [16, 1344, 512], P('expert', 'fsdp'), may hold values from -0.25 to 0.25
- w_up: bfloat16 [16, 1344, 512], P('expert', 'fsdp'), may hold values from -0.25 to 0.25
- w_down: bfloat16 [16, 1344, 512], P('expert', 'fsdp'), may hold values from -0.15625 to 0.15625
Outputs:
- mixed: bfloat16 [65536, 512], P(('fsdp', 'expert'))
- latent_grad: bfloat16 [65536, 512], P(('fsdp', 'expert'))
- score_grad: float32 [65536, 2], P(('fsdp', 'expert'))
- gate_grad: float32 [16, 1344, 512], P('expert', 'fsdp')
- up_grad: float32 [16, 1344, 512], P('expert', 'fsdp')
- down_grad: float32 [16, 1344, 512], P('expert', 'fsdp')
Inputs may be any that keep to these rules, and one draw needn't show every extreme that they name: `routes`: each row names two different experts. Among the 128 rows of one device no expert is named more than 32 times; in some device's rows some expert is named exactly 32 times.
All inputs are finite; a program needn't handle non-finite values.
Results may differ from a plain program's by a relative error of at most 0.023.
Values may be sent and summed in bfloat16 or wider, within the bound.
No kernel may reach another device: no remote copies, remote signals or barrier semaphores. Data moves between devices by JAX's collectives and lax.ppermute only.
A program may use at most 64 MiB of HBM per device.

v0:
```python
import jax
import jax.numpy as jnp
from jax import lax
from jax.sharding import PartitionSpec as P

grad_scale = 0.015625


def slot_tables(routes, experts, capacity):
    tok_rows = routes.shape[0]
    flat = routes.reshape(-1)
    onehot = (flat[:, None] == jnp.arange(experts, dtype=jnp.int32)[None, :]).astype(jnp.int32)
    ranks = jnp.sum((jnp.cumsum(onehot, axis=0) - 1) * onehot, axis=1)
    slots = (flat * capacity + ranks).reshape(tok_rows, 2)
    positions = jnp.arange(experts * capacity, dtype=jnp.int32)
    first = (slots[:, 0:1] == positions[None, :]).astype(jnp.bfloat16)
    second = (slots[:, 1:2] == positions[None, :]).astype(jnp.bfloat16)
    return (first, second)


def place_rows(table, rows):
    return lax.dot_general(
        table, rows, (((0,), (0,)), ((), ())), preferred_element_type=jnp.float32
    )


def against(left, right):
    return lax.dot_general(
        left, right, (((1,), (1,)), ((), ())), preferred_element_type=jnp.float32
    )


def outer_sum(left, right):
    return (
        lax.dot_general(left, right, (((0,), (0,)), ((), ())), preferred_element_type=jnp.float32)
        * grad_scale
    )


def shards(latent, routes, scores, cotangent, w_gate, w_up, w_down):
    experts = lax.axis_size("expert")
    tok_rows = latent.shape[0]
    capacity = 4 * tok_rows // experts
    first, second = slot_tables(routes, experts, capacity)
    merged = first + second
    send = place_rows(merged, latent).astype(jnp.bfloat16)
    arrived = lax.all_to_all(send, "expert", split_axis=0, concat_axis=0, tiled=True)
    full_gate, full_up, full_down = (
        lax.all_gather(w_gate, "fsdp", axis=1, tiled=True),
        lax.all_gather(w_up, "fsdp", axis=1, tiled=True),
        lax.all_gather(w_down, "fsdp", axis=1, tiled=True),
    )
    wg, wu, wd = (full_gate[0], full_up[0], full_down[0])
    gate = against(arrived, wg)
    up = against(arrived, wu)
    sig = jax.nn.sigmoid(gate)
    act = gate * sig
    hidden = (act * up).astype(jnp.bfloat16)
    outs = jnp.dot(hidden, wd, preferred_element_type=jnp.float32).astype(jnp.bfloat16)
    back = lax.all_to_all(outs, "expert", split_axis=0, concat_axis=0, tiled=True)
    out_first = jnp.dot(first, back, preferred_element_type=jnp.float32)
    out_second = jnp.dot(second, back, preferred_element_type=jnp.float32)
    score_first = scores[:, 0:1]
    score_second = scores[:, 1:2]
    mixed = (score_first * out_first + score_second * out_second).astype(jnp.bfloat16)
    cot_f = cotangent.astype(jnp.float32)
    score_grad = jnp.stack(
        [jnp.sum(cot_f * out_first, axis=1), jnp.sum(cot_f * out_second, axis=1)], axis=1
    )
    grad_first = (score_first * cot_f).astype(jnp.bfloat16)
    grad_second = (score_second * cot_f).astype(jnp.bfloat16)
    grad_send = (place_rows(first, grad_first) + place_rows(second, grad_second)).astype(
        jnp.bfloat16
    )
    grad_arrived = lax.all_to_all(grad_send, "expert", split_axis=0, concat_axis=0, tiled=True)
    again_gate, again_up, again_down = (
        lax.all_gather(w_gate, "fsdp", axis=1, tiled=True),
        lax.all_gather(w_up, "fsdp", axis=1, tiled=True),
        lax.all_gather(w_down, "fsdp", axis=1, tiled=True),
    )
    wg, wu, wd = (again_gate[0], again_up[0], again_down[0])
    hidden_grad = against(grad_arrived, wd)
    down_term = outer_sum(hidden, grad_arrived)
    gate_back = (hidden_grad * up * sig * (1.0 + gate * (1.0 - sig))).astype(jnp.bfloat16)
    up_back = (hidden_grad * act).astype(jnp.bfloat16)
    token_back = (
        jnp.dot(gate_back, wg, preferred_element_type=jnp.float32)
        + jnp.dot(up_back, wu, preferred_element_type=jnp.float32)
    ).astype(jnp.bfloat16)
    returned = lax.all_to_all(token_back, "expert", split_axis=0, concat_axis=0, tiled=True)
    latent_grad = jnp.dot(merged, returned, preferred_element_type=jnp.float32).astype(jnp.bfloat16)
    gate_term = outer_sum(gate_back, arrived)
    up_term = outer_sum(up_back, arrived)
    gate_part, up_part, down_part = (
        lax.psum_scatter(
            gate_term.astype(jnp.bfloat16), "fsdp", scatter_dimension=0, tiled=True
        ).astype(jnp.float32),
        lax.psum_scatter(
            up_term.astype(jnp.bfloat16), "fsdp", scatter_dimension=0, tiled=True
        ).astype(jnp.float32),
        lax.psum_scatter(
            down_term.astype(jnp.bfloat16), "fsdp", scatter_dimension=0, tiled=True
        ).astype(jnp.float32),
    )
    return (mixed, latent_grad, score_grad, gate_part[None], up_part[None], down_part[None])


def solution(mesh):
    placed = (
        P(("fsdp", "expert"), None),
        P(("fsdp", "expert"), None),
        P(("fsdp", "expert"), None),
        P(("fsdp", "expert"), None),
        P("expert", "fsdp", None),
        P("expert", "fsdp", None),
        P("expert", "fsdp", None),
    )
    return jax.shard_map(
        shards,
        mesh=mesh,
        in_specs=placed,
        out_specs=(
            P(("fsdp", "expert"), None),
            P(("fsdp", "expert"), None),
            P(("fsdp", "expert"), None),
            P("expert", "fsdp", None),
            P("expert", "fsdp", None),
            P("expert", "fsdp", None),
        ),
        check_vma=False,
    )
```

profile of v0, /device:TPU:50, one launch (start us, length us, event | category | flops | bytes accessed | tf_op | source)
XLA Modules:
  0.0 541.3 jit_solution(5318642789219758416)
XLA Ops:
  18.2 6.8 %all-to-all-start.2 = ((bf16[16,32,512]{2,1,0:T(8,128)(2,1)}), bf16[16,32,512]{2,1,0:T(8,128)(2,1)S(1)}, u32[]{:S(2)}, u32[]{:S(2)}) async-start(bf16[16,32,512]{2,1,0:T(8,128)(2,1)} %bitcast.9), calls=%async_computation.2 | async-start | bytes 1048576 | tf_op jit(solution)/shard_map/all_to_all | solution.py:75
  26.2 13.3 %all-to-all-done.2 = bf16[16,32,512]{2,1,0:T(8,128)(2,1)S(1)} async-done(((bf16[16,32,512]{2,1,0:T(8,128)(2,1)}), bf16[16,32,512]{2,1,0:T(8,128)(2,1)S(1)}, u32[]{:S(2)}, u32[]{:S(2)}) %all-to-all-start.2) | async-done | bytes 524320 | tf_op jit(solution)/shard_map/all_to_all | solution.py:75
  39.5 7.3 %all-to-all-start = ((bf16[16,32,512]{2,1,0:T(8,128)(2,1)}), bf16[16,32,512]{2,1,0:T(8,128)(2,1)S(1)}, u32[]{:S(2)}, u32[]{:S(2)}) async-start(bf16[16,32,512]{2,1,0:T(8,128)(2,1)} %bitcast.4), calls=%async_computation | async-start | bytes 1048576 | tf_op jit(solution)/shard_map/all_to_all | solution.py:47
  46.8 66.9 %all-gather.8.cloned.1.call-done = bf16[1,1344,512]{2,0,1:T(2,128)(2,1)} async-done(((bf16[1,42,512]{2,0,1:T(2,128)(2,1)}), bf16[1,1344,512]{2,0,1:T(2,128)(2,1)}) %all-gather.8.cloned.1.call-update) | async-done | bytes 1376272 | tf_op jit(solution)/shard_map/all_gather | solution.py:51
  113.7 2.9 fusion.7
  116.6 92.5 %all-gather.6.cloned.1.call-done = bf16[1,1344,512]{2,0,1:T(2,128)(2,1)} async-done(((bf16[1,42,512]{2,0,1:T(2,128)(2,1)}), bf16[1,1344,512]{2,0,1:T(2,128)(2,1)}) %all-gather.6.cloned.1.call-update) | async-done | bytes 1376272 | tf_op jit(solution)/shard_map/all_gather | solution.py:50
  209.1 4.3 fusion.13
  213.4 91.1 %all-gather.4.cloned.1.call-done = bf16[1,1344,512]{2,0,1:T(2,128)(2,1)} async-done(((bf16[1,42,512]{2,0,1:T(2,128)(2,1)}), bf16[1,1344,512]{2,0,1:T(2,128)(2,1)}) %all-gather.4.cloned.1.call-update) | async-done | bytes 1376272 | tf_op jit(solution)/shard_map/all_gather | solution.py:49
  304.5 6.0 %multiply_convert_fusion.1 = (bf16[512,1344]{0,1:T(8,128)(2,1)S(1)}, bf16[512,1344]{0,1:T(8,128)(2,1)}, bf16[512,1344]{0,1:T(8,128)(2,1)S(1)}) fusion(f32[512,1344]{0,1:T(8,128)S(1)} %fusion.7, f32[512,1344]{0,1:T(8,128)} %fusion.13, bf16[512,512]{1,0:T(8,128)(2,1)S(1)} %bitcast.96, bf16[1,1344,512]{2,0,1:T(2,128)(2,1)} %all-gather.4.cloned.1.call-done), kind=kOutput, calls=%fused_computation.7 | convolution fusion | flops 714964992 | bytes 11534336 | tf_op jit(solution)/shard_map/dot_general | solution.py:28
  311.5 2.0 fusion.3
  315.4 6.6 %all-to-all-start.1 = ((bf16[16,32,512]{2,1,0:T(8,128)(2,1)}), bf16[16,32,512]{2,1,0:T(8,128)(2,1)S(1)}, u32[]{:S(2)}, u32[]{:S(2)}) async-start(bf16[16,32,512]{2,1,0:T(8,128)(2,1)} %bitcast.6), calls=%async_computation.1 | async-start | bytes 1048576 | tf_op jit(solution)/shard_map/all_to_all | solution.py:60
  322.0 3.5 fusion.4
  329.5 5.9 %all-to-all-done.1 = bf16[16,32,512]{2,1,0:T(8,128)(2,1)S(1)} async-done(((bf16[16,32,512]{2,1,0:T(8,128)(2,1)}), bf16[16,32,512]{2,1,0:T(8,128)(2,1)S(1)}, u32[]{:S(2)}, u32[]{:S(2)}) %all-to-all-start.1) | async-done | bytes 524320 | tf_op jit(solution)/shard_map/all_to_all | solution.py:60
  335.4 7.1 %all-to-all-start.3 = ((bf16[16,32,512]{2,1,0:T(8,128)(2,1)}), bf16[16,32,512]{2,1,0:T(8,128)(2,1)S(1)}, u32[]{:S(2)}, u32[]{:S(2)}) async-start(bf16[16,32,512]{2,1,0:T(8,128)(2,1)} %bitcast.11), calls=%async_computation.3 | async-start | bytes 1048576 | tf_op jit(solution)/shard_map/all_to_all | solution.py:90
  342.4 130.8 %fusion.65 = (bf16[48,512]{1,0:T(8,128)(2,1)S(1)}, bf16[48,512]{1,0:T(8,128)(2,1)S(1)}, bf16[48,512]{1,0:T(8,128)(2,1)S(1)}) fusion(bf16[1344,512]{1,0:T(8,128)(2,1)} %fusion.3, bf16[1344,512]{1,0:T(8,128)(2,1)} %fusion.4, bf16[1344,512]{1,0:T(8,128)(2,1)S(1)} %fusion.5), kind=kCustom, calls=%all-reduce-scatter.3 | all-reduce-scatter fusion | flops 2359297 | bytes 4278272
  474.5 1.9 collective-permute-start.8
  477.8 8.0 %collective-permute-start.9 = (bf16[48,512]{1,0:T(8,128)(2,1)S(1)}, bf16[48,512]{1,0:T(8,128)(2,1)S(1)}, u32[]{:S(2)}, u32[]{:S(2)}) collective-permute-start(bf16[48,512]{1,0:T(8,128)(2,1)S(1)} %get-tuple-element.49), channel_id=1, source_target_pairs={{0,32},{16,48},{32,64},{48,80},{64,96},{80,112},{96,128},{112,144}... | collective-permute-start | bytes 147464
  487.8 6.7 %collective-permute-start.5 = (bf16[48,512]{1,0:T(8,128)(2,1)S(1)}, bf16[48,512]{1,0:T(8,128)(2,1)S(1)}, u32[]{:S(2)}, u32[]{:S(2)}) collective-permute-start(bf16[48,512]{1,0:T(8,128)(2,1)S(1)} %get-tuple-element.48), channel_id=1, source_target_pairs={{0,32},{16,48},{32,64},{48,80},{64,96},{80,112},{96,128},{112,144}... | collective-permute-start | bytes 147464
  494.6 5.7 %collective-permute-start.6 = (bf16[48,512]{1,0:T(8,128)(2,1)S(1)}, bf16[48,512]{1,0:T(8,128)(2,1)S(1)}, u32[]{:S(2)}, u32[]{:S(2)}) collective-permute-start(bf16[48,512]{1,0:T(8,128)(2,1)S(1)} %get-tuple-element.48), channel_id=1, source_target_pairs={{0,48},{16,64},{32,80},{48,96},{64,112},{80,128},{96,144},{112,160... | collective-permute-start | bytes 147464
  500.3 1.9 collective-permute-start.7
  504.2 1.9 collective-permute-start
  506.9 6.1 %collective-permute-start.1 = (bf16[48,512]{1,0:T(8,128)(2,1)S(1)}, bf16[48,512]{1,0:T(8,128)(2,1)S(1)}, u32[]{:S(2)}, u32[]{:S(2)}) collective-permute-start(bf16[48,512]{1,0:T(8,128)(2,1)S(1)} %get-tuple-element.47), channel_id=1, source_target_pairs={{0,32},{16,48},{32,64},{48,80},{64,96},{80,112},{96,128},{112,144}... | collective-permute-start | bytes 147464
  513.0 8.3 %collective-permute-start.2 = (bf16[48,512]{1,0:T(8,128)(2,1)S(1)}, bf16[48,512]{1,0:T(8,128)(2,1)S(1)}, u32[]{:S(2)}, u32[]{:S(2)}) collective-permute-start(bf16[48,512]{1,0:T(8,128)(2,1)S(1)} %get-tuple-element.47), channel_id=1, source_target_pairs={{0,48},{16,64},{32,80},{48,96},{64,112},{80,128},{96,144},{112,160... | collective-permute-start | bytes 147464
  521.4 6.8 %collective-permute-start.3 = (bf16[42,512]{1,0:T(8,128)(2,1)S(1)}, bf16[42,512]{1,0:T(8,128)(2,1)S(1)}, u32[]{:S(2)}, u32[]{:S(2)}) collective-permute-start(bf16[42,512]{1,0:T(8,128)(2,1)S(1)} %slice.25), channel_id=1, source_target_pairs={{0,64},{16,80},{32,96},{48,112},{64,128},{80,144},{96,160},{112,17... | collective-permute-start | bytes 129032
  (84 shorter events, 32.2 us)
Async XLA Ops:
  7.2 17.8 %copy-start = (bf16[128,512]{1,0:T(8,128)(2,1)S(1)}, bf16[128,512]{1,0:T(8,128)(2,1)}, u32[]{:S(2)}) copy-start(bf16[128,512]{1,0:T(8,128)(2,1)} %param.7) | copy-start | bytes 393220
  7.2 9.8 %copy-start.5 = (bf16[128,512]{1,0:T(8,128)(2,1)S(1)}, bf16[128,512]{1,0:T(8,128)(2,1)}, u32[]{:S(2)}) copy-start(bf16[128,512]{1,0:T(8,128)(2,1)} %param.10) | copy-start | bytes 393220
  7.2 106.5 %all-gather.8.cloned.1.call-start = ((), (), s32[]{:S(2)}) async-start(), calls=%async_computation.6 | async-start | bytes 2838528 | tf_op jit(solution)/shard_map/all_gather | solution.py:51
  8.8 200.3 %all-gather.6.cloned.1.call-start = ((), (), s32[]{:S(2)}) async-start(), calls=%async_computation.5 | async-start | bytes 2838528 | tf_op jit(solution)/shard_map/all_gather | solution.py:50
  10.4 294.1 %all-gather.4.cloned.1.call-start = ((), (), s32[]{:S(2)}) async-start(), calls=%async_computation.4 | async-start | bytes 2838528 | tf_op jit(solution)/shard_map/all_gather | solution.py:49
  18.2 21.3 %all-to-all-start.2 = ((bf16[16,32,512]{2,1,0:T(8,128)(2,1)}), bf16[16,32,512]{2,1,0:T(8,128)(2,1)S(1)}, u32[]{:S(2)}, u32[]{:S(2)}) async-start(bf16[16,32,512]{2,1,0:T(8,128)(2,1)} %bitcast.9), calls=%async_computation.2 | async-start | bytes 1048576 | tf_op jit(solution)/shard_map/all_to_all | solution.py:75
  39.5 74.2 %copy-start.1 = (bf16[16,32,512]{2,1,0:T(8,128)(2,1)}, bf16[16,32,512]{2,1,0:T(8,128)(2,1)S(1)}, u32[]{:S(2)}) copy-start(bf16[16,32,512]{2,1,0:T(8,128)(2,1)S(1)} %all-to-all-done.2) | copy-start | bytes 1572868
  39.5 77.1 %all-to-all-start = ((bf16[16,32,512]{2,1,0:T(8,128)(2,1)}), bf16[16,32,512]{2,1,0:T(8,128)(2,1)S(1)}, u32[]{:S(2)}, u32[]{:S(2)}) async-start(bf16[16,32,512]{2,1,0:T(8,128)(2,1)} %bitcast.4), calls=%async_computation | async-start | bytes 1048576 | tf_op jit(solution)/shard_map/all_to_all | solution.py:47
  304.5 6.0 %copy-start.2 = (bf16[16,32,512]{2,1,0:T(8,128)(2,1)S(1)}, bf16[16,32,512]{2,1,0:T(8,128)(2,1)}, u32[]{:S(2)}) copy-start(bf16[16,32,512]{2,1,0:T(8,128)(2,1)} %copy-done.1) | copy-start | bytes 1572868
  315.4 20.0 %all-to-all-start.1 = ((bf16[16,32,512]{2,1,0:T(8,128)(2,1)}), bf16[16,32,512]{2,1,0:T(8,128)(2,1)S(1)}, u32[]{:S(2)}, u32[]{:S(2)}) async-start(bf16[16,32,512]{2,1,0:T(8,128)(2,1)} %bitcast.6), calls=%async_computation.1 | async-start | bytes 1048576 | tf_op jit(solution)/shard_map/all_to_all | solution.py:60
  322.0 3.5 copy-start.4
  335.4 197.9 %all-to-all-start.3 = ((bf16[16,32,512]{2,1,0:T(8,128)(2,1)}), bf16[16,32,512]{2,1,0:T(8,128)(2,1)S(1)}, u32[]{:S(2)}, u32[]{:S(2)}) async-start(bf16[16,32,512]{2,1,0:T(8,128)(2,1)} %bitcast.11), calls=%async_computation.3 | async-start | bytes 1048576 | tf_op jit(solution)/shard_map/all_to_all | solution.py:90
  473.2 21.4 %collective-permute-start.10 = (bf16[48,512]{1,0:T(8,128)(2,1)S(1)}, bf16[48,512]{1,0:T(8,128)(2,1)S(1)}, u32[]{:S(2)}, u32[]{:S(2)}) collective-permute-start(bf16[48,512]{1,0:T(8,128)(2,1)S(1)} %get-tuple-element.49), channel_id=1, source_target_pairs={{0,48},{16,64},{32,80},{48,96},{64,112},{80,128},{96,144},{112,160... | collective-permute-start | bytes 147464
  474.5 25.8 %collective-permute-start.8 = (bf16[48,512]{1,0:T(8,128)(2,1)S(1)}, bf16[48,512]{1,0:T(8,128)(2,1)S(1)}, u32[]{:S(2)}, u32[]{:S(2)}) collective-permute-start(bf16[48,512]{1,0:T(8,128)(2,1)S(1)} %get-tuple-element.49), channel_id=1, source_target_pairs={{0,16},{16,32},{32,48},{48,64},{64,80},{80,96},{96,112},{112,128},... | collective-permute-start | bytes 147464
  476.4 11.4 %collective-permute-start.11 = (bf16[42,512]{1,0:T(8,128)(2,1)S(1)}, bf16[42,512]{1,0:T(8,128)(2,1)S(1)}, u32[]{:S(2)}, u32[]{:S(2)}) collective-permute-start(bf16[42,512]{1,0:T(8,128)(2,1)S(1)} %slice.27), channel_id=1, source_target_pairs={{0,64},{16,80},{32,96},{48,112},{64,128},{80,144},{96,160},{112,17... | collective-permute-start | bytes 129032
  477.8 26.4 %collective-permute-start.9 = (bf16[48,512]{1,0:T(8,128)(2,1)S(1)}, bf16[48,512]{1,0:T(8,128)(2,1)S(1)}, u32[]{:S(2)}, u32[]{:S(2)}) collective-permute-start(bf16[48,512]{1,0:T(8,128)(2,1)S(1)} %get-tuple-element.49), channel_id=1, source_target_pairs={{0,32},{16,48},{32,64},{48,80},{64,96},{80,112},{96,128},{112,144}... | collective-permute-start | bytes 147464
  485.9 27.2 %collective-permute-start.4 = (bf16[48,512]{1,0:T(8,128)(2,1)S(1)}, bf16[48,512]{1,0:T(8,128)(2,1)S(1)}, u32[]{:S(2)}, u32[]{:S(2)}) collective-permute-start(bf16[48,512]{1,0:T(8,128)(2,1)S(1)} %get-tuple-element.48), channel_id=1, source_target_pairs={{0,16},{16,32},{32,48},{48,64},{64,80},{80,96},{96,112},{112,128},... | collective-permute-start | bytes 147464
  487.8 33.5 %collective-permute-start.5 = (bf16[48,512]{1,0:T(8,128)(2,1)S(1)}, bf16[48,512]{1,0:T(8,128)(2,1)S(1)}, u32[]{:S(2)}, u32[]{:S(2)}) collective-permute-start(bf16[48,512]{1,0:T(8,128)(2,1)S(1)} %get-tuple-element.48), channel_id=1, source_target_pairs={{0,32},{16,48},{32,64},{48,80},{64,96},{80,112},{96,128},{112,144}... | collective-permute-start | bytes 147464
  494.6 33.6 %collective-permute-start.6 = (bf16[48,512]{1,0:T(8,128)(2,1)S(1)}, bf16[48,512]{1,0:T(8,128)(2,1)S(1)}, u32[]{:S(2)}, u32[]{:S(2)}) collective-permute-start(bf16[48,512]{1,0:T(8,128)(2,1)S(1)} %get-tuple-element.48), channel_id=1, source_target_pairs={{0,48},{16,64},{32,80},{48,96},{64,112},{80,128},{96,144},{112,160... | collective-permute-start | bytes 147464
  500.3 6.6 %collective-permute-start.7 = (bf16[42,512]{1,0:T(8,128)(2,1)S(1)}, bf16[42,512]{1,0:T(8,128)(2,1)S(1)}, u32[]{:S(2)}, u32[]{:S(2)}) collective-permute-start(bf16[42,512]{1,0:T(8,128)(2,1)S(1)} %slice.26), channel_id=1, source_target_pairs={{0,64},{16,80},{32,96},{48,112},{64,128},{80,144},{96,160},{112,17... | collective-permute-start | bytes 129032
  504.2 26.3 %collective-permute-start = (bf16[48,512]{1,0:T(8,128)(2,1)S(1)}, bf16[48,512]{1,0:T(8,128)(2,1)S(1)}, u32[]{:S(2)}, u32[]{:S(2)}) collective-permute-start(bf16[48,512]{1,0:T(8,128)(2,1)S(1)} %get-tuple-element.47), channel_id=1, source_target_pairs={{0,16},{16,32},{32,48},{48,64},{64,80},{80,96},{96,112},{112,128},... | collective-permute-start | bytes 147464
  506.9 23.6 %collective-permute-start.1 = (bf16[48,512]{1,0:T(8,128)(2,1)S(1)}, bf16[48,512]{1,0:T(8,128)(2,1)S(1)}, u32[]{:S(2)}, u32[]{:S(2)}) collective-permute-start(bf16[48,512]{1,0:T(8,128)(2,1)S(1)} %get-tuple-element.47), channel_id=1, source_target_pairs={{0,32},{16,48},{32,64},{48,80},{64,96},{80,112},{96,128},{112,144}... | collective-permute-start | bytes 147464
  513.0 17.4 %collective-permute-start.2 = (bf16[48,512]{1,0:T(8,128)(2,1)S(1)}, bf16[48,512]{1,0:T(8,128)(2,1)S(1)}, u32[]{:S(2)}, u32[]{:S(2)}) collective-permute-start(bf16[48,512]{1,0:T(8,128)(2,1)S(1)} %get-tuple-element.47), channel_id=1, source_target_pairs={{0,48},{16,64},{32,80},{48,96},{64,112},{80,128},{96,144},{112,160... | collective-permute-start | bytes 147464
  521.4 9.1 %collective-permute-start.3 = (bf16[42,512]{1,0:T(8,128)(2,1)S(1)}, bf16[42,512]{1,0:T(8,128)(2,1)S(1)}, u32[]{:S(2)}, u32[]{:S(2)}) collective-permute-start(bf16[42,512]{1,0:T(8,128)(2,1)S(1)} %slice.25), channel_id=1, source_target_pairs={{0,64},{16,80},{32,96},{48,112},{64,128},{80,144},{96,160},{112,17... | collective-permute-start | bytes 129032
  (5 other events, 10.6 us)
Sparse Core Ops, SparseCore 0:
  11.9 101.7 all-gather.7
  117.6 91.4 all-gather.5
  213.0 91.4 all-gather.3
where the time goes:
time: 542 us; the launch traced here: 541 us
  waiting for transfers between devices  270 us (50%)
  blocking collectives  131 us (24%)
  starting transfers between devices  80 us (15%)
  matrix products  30.1 us (6%)
  between operations  14.8 us (3%)
  local copies, waits for them, and re-layouts  13.9 us (3%)
    unnamed x1, blocking collectives  131 us
    all_gather x1, waiting for transfers between devices, shards(): lax.all_gather(w_up, 'fsdp', axis=1, tiled=True)  92.5 us
    all_gather x1, waiting for transfers between devices, shards(): lax.all_gather(w_gate, 'fsdp', axis=1, tiled=True)  91.1 us
    all_gather x1, waiting for transfers between devices, shards(): lax.all_gather(w_down, 'fsdp', axis=1, tiled=True)  66.9 us
    unnamed x12, starting transfers between devices  52.1 us
    all_to_all x1, waiting for transfers between devices, shards(): lax.all_to_all(grad_send, 'expert', split_axis=0, concat_axis=0, tiled=True)  13.3 us
    dot_general x3, matrix products, against(): lax.dot_general(left, right, (((1,), (1,)), ((), ())), preferred_element_...  13.1 us
    unnamed x34, local copies, waits for them, and re-layouts  12.4 us
  transfers between devices with their start and end apart: 19, of which 5 were waited for; matrix products, arithmetic and copies ran while one was open for 30% of the time, Pallas kernels for 0%

commit v1 on v0

v1 whole, which is shorter than its diff:
```python
import jax
import jax.numpy as jnp
from jax import lax
from jax.sharding import Mesh, PartitionSpec as P

grad_scale = 0.015625
PAD = 48
F32 = jnp.float32
BF16 = jnp.bfloat16


def partner_pairs(rounds, size):
    pairs = []
    for z in range(size):
        for core in range(2):
            odd_link = (rounds + core) % 2
            step = 1 if (z + odd_link) % 2 == 0 else -1
            pairs.append((z * 2 + core, (z + step) % size * 2 + core))
    return pairs


def swap_z(rows, rounds):
    size = lax.axis_size("z")
    return lax.ppermute(rows, ("z", "core"), partner_pairs(rounds, size))


def swap(rows, axis):
    return lax.ppermute(rows, axis, [(0, 1), (1, 0)])


def gather_z(block):
    got = swap_z(block, 0)
    pieces = [jnp.concatenate([block, got], axis=0)]
    for rounds in (1, 2, 3):
        pieces.append(swap_z(pieces[-1], rounds))
    return pieces


def add(one, two):
    return one.astype(F32) + two.astype(F32)


def sum_z(pieces):
    first, second, third, last = pieces
    third = add(third, swap_z(last, 3)).astype(BF16)
    second = add(second, swap_z(third, 2)).astype(BF16)
    first = add(first, swap_z(second, 1))
    return add(first[:1], swap_z(first[1:].astype(BF16), 0))


def against(left, right):
    return lax.dot_general(left, right, (((1,), (1,)), ((), ())), preferred_element_type=F32)


def outer_sum(left, right):
    return lax.dot_general(left, right, (((0,), (0,)), ((), ())), preferred_element_type=F32)


def slot_tables(routes, experts, capacity):
    rows = routes.shape[0]
    ids = jnp.arange(experts, dtype=jnp.int32)[None, :]
    named = ((routes[:, 0:1] == ids) | (routes[:, 1:2] == ids)).astype(BF16)
    earlier = (
        jnp.arange(rows)[:, None] > jnp.arange(rows)[None, :]
    ).astype(BF16)
    ranks = jnp.dot(earlier, named, preferred_element_type=F32)
    slots = ids.astype(F32) * capacity + ranks
    slot = [
        jnp.sum(jnp.where(routes[:, k : k + 1] == ids, slots, 0.0), axis=1, keepdims=True)
        for k in range(2)
    ]
    positions = jnp.arange(experts * capacity, dtype=jnp.int32).astype(F32)[None, :]
    return [s == positions for s in slot]


def shards(latent, routes, scores, cotangent, w_gate, w_up, w_down):
    experts = lax.axis_size("x") * lax.axis_size("yl")
    tok_rows, width = latent.shape
    capacity = 4 * tok_rows // experts
    slots = experts * capacity
    hidden_rows = w_gate.shape[1]
    own = jnp.pad(
        jnp.stack([w_gate[0], w_up[0], w_down[0]]), ((0, 0), (0, PAD - hidden_rows), (0, 0))
    )[None]
    other = swap(own, "yh")

    first, second = slot_tables(routes, experts, capacity)
    first_b, second_b = first.astype(BF16), second.astype(BF16)
    merged = first_b + second_b
    score_slot = jnp.sum(
        jnp.where(first, scores[:, 0:1], 0.0) + jnp.where(second, scores[:, 1:2], 0.0), axis=0
    )[:, None]
    send = outer_sum(merged, latent).astype(BF16)
    grad_send = (outer_sum(merged, cotangent) * score_slot).astype(BF16)
    shape = (experts, capacity, width)
    both = jnp.concatenate([send.reshape(shape), grad_send.reshape(shape)], axis=1)
    mine = lax.all_to_all(both, ("x", "yl"), 0, 0, tiled=True)
    theirs = swap(mine, "core")

    pieces = gather_z(own) + gather_z(other)
    weights = jnp.concatenate(pieces, axis=0)
    blocks = weights.shape[0]
    wg, wu, wd = [weights[:, i].reshape(blocks * PAD, width) for i in range(3)]

    def tokens(part):
        rows = slice(part * capacity, (part + 1) * capacity)
        return jnp.concatenate(
            [mine[:, rows].reshape(slots, width), theirs[:, rows].reshape(slots, width)], axis=0
        )

    arrived, out_grad = tokens(0), tokens(1)
    gate = against(arrived, wg)
    up = against(arrived, wu)
    sig = jax.nn.sigmoid(gate)
    act = gate * sig
    hidden = (act * up).astype(BF16)
    outs = jnp.dot(hidden, wd, preferred_element_type=F32)
    hidden_grad = against(out_grad, wd)
    gate_back = (hidden_grad * up * sig * (1.0 + gate * (1.0 - sig))).astype(BF16)
    up_back = (hidden_grad * act).astype(BF16)
    token_back = jnp.dot(gate_back, wg, preferred_element_type=F32) + jnp.dot(
        up_back, wu, preferred_element_type=F32
    )
    terms = jnp.stack(
        [
            (outer_sum(left, right) * grad_scale).astype(BF16).reshape(blocks, PAD, width)
            for left, right in ((gate_back, arrived), (up_back, arrived), (hidden, out_grad))
        ],
        axis=1,
    )
    quarter = blocks // 8
    parts = [terms[i * quarter : (i + 1) * quarter] for i in range(8)]
    far = sum_z(parts[4:]).astype(BF16)
    near = sum_z(parts[:4])
    grads = add(near, swap(far, "yh"))[0, :, :hidden_rows]

    rest = swap(
        jnp.concatenate(
            [outs[slots:].reshape(shape), token_back[slots:].reshape(shape)], axis=1
        ).astype(BF16),
        "core",
    )
    local = jnp.concatenate(
        [outs[:slots].reshape(shape), token_back[:slots].reshape(shape)], axis=1
    )
    back = lax.all_to_all(add(local, rest).astype(BF16), ("x", "yl"), 0, 0, tiled=True)
    outs_back = back[:, :capacity].reshape(slots, width)
    tokens_back = back[:, capacity:].reshape(slots, width)
    out_first = jnp.dot(first_b, outs_back, preferred_element_type=F32)
    out_second = jnp.dot(second_b, outs_back, preferred_element_type=F32)
    mixed = (scores[:, 0:1] * out_first + scores[:, 1:2] * out_second).astype(BF16)
    cot_f = cotangent.astype(F32)
    score_grad = jnp.stack(
        [jnp.sum(cot_f * out_first, axis=1), jnp.sum(cot_f * out_second, axis=1)], axis=1
    )
    latent_grad = jnp.dot(merged, tokens_back, preferred_element_type=F32).astype(BF16)
    return (mixed, latent_grad, score_grad, grads[0:1], grads[1:2], grads[2:3])


def solution(mesh):
    fine = Mesh(
        mesh.devices.reshape(8, 2, 2, 4, 4), ("z", "yh", "core", "x", "yl")
    )
    fsdp, expert = ("z", "yh", "core"), ("x", "yl")
    rows = P(fsdp + expert, None)
    weight = P(expert, fsdp, None)
    return jax.shard_map(
        shards,
        mesh=fine,
        in_specs=(rows,) * 4 + (weight,) * 3,
        out_specs=(rows,) * 3 + (weight,) * 3,
        check_vma=False,
    )
```

time: 542 us -> 182 us (0.34)
  the two profiles are of different devices: /device:TPU:50 before, /device:TPU:2 now
where the time goes in v1:
time: 182 us; the launch traced here: 181 us
  starting transfers between devices  96.7 us (53%)
  waiting for transfers between devices  46.2 us (25%)
  matrix products  14.9 us (8%)
  local copies, waits for them, and re-layouts  12.2 us (7%)
  other arithmetic  9.42 us (5%)
    ppermute x16, starting transfers between devices, swap_z(): return lax.ppermute(rows, ('z', 'core'), partner_pairs(rounds, size))  65.5 us
    ppermute x16, waiting for transfers between devices, swap_z(): return lax.ppermute(rows, ('z', 'core'), partner_pairs(rounds, size))  36.4 us
    ppermute x4, starting transfers between devices, swap(): return lax.ppermute(rows, axis, [(0, 1), (1, 0)])  13.5 us
    ppermute x4, waiting for transfers between devices, swap(): return lax.ppermute(rows, axis, [(0, 1), (1, 0)])  9.82 us
    all_to_all x1, starting transfers between devices, shards(): mine = lax.all_to_all(both, ('x', 'yl'), 0, 0, tiled=True)  9.37 us
    all_to_all x1, starting transfers between devices, shards(): lax.all_to_all(add(local, rest).astype(BF16), ('x', 'yl'), 0, 0, tiled=True)  8.32 us
    dot_general x3, matrix products, against(): lax.dot_general(left, right, (((1,), (1,)), ((), ())), preferred_element_...  4.94 us
    unnamed x32, local copies, waits for them, and re-layouts  4.85 us
  transfers between devices with their start and end apart: 22, of which 11 were waited for; matrix products, arithmetic and copies ran while one was open for 8% of the time, Pallas kernels for 0%

profile of v1, /device:TPU:2, one launch (start us, length us, event | category | flops | bytes accessed | tf_op | source)
XLA Modules:
  0.0 180.7 jit_solution(8782951386998828239)
XLA Ops:
  5.3 9.4 %all-to-all-start = ((bf16[16,64,512]{2,1,0:T(8,128)(2,1)}), bf16[16,64,512]{2,1,0:T(8,128)(2,1)S(1)}, u32[]{:S(2)}, u32[]{:S(2)}) async-start(bf16[16,64,512]{2,1,0:T(8,128)(2,1)} %pad_maximum_fusion), calls=%async_computation | async-start | bytes 2097152 | tf_op jit(solution)/shard_map/all_to_all | solution.py:97
  17.6 5.0 %collective-permute-start.5 = (bf16[1,3,48,512]{3,2,1,0:T(8,128)(2,1)S(1)}, bf16[1,3,48,512]{3,2,1,0:T(8,128)(2,1)S(1)}, u32[]{:S(2)}, u32[]{:S(2)}) collective-permute-start(bf16[1,3,48,512]{3,2,1,0:T(8,128)(2,1)S(1)} %fusion.19), channel_id=1, source_target_pairs={{0,32},{32,0},{1,33},{33,1},{2,34},{34,2},{3,35},{35,3},{4,36},{36... | collective-permute-start | bytes 442376 | tf_op jit(solution)/shard_map/ppermute | solution.py:28
  22.7 9.1 %collective-permute-start.2 = (bf16[2,3,48,512]{3,2,1,0:T(8,128)(2,1)S(1)}, bf16[2,3,48,512]{3,2,1,0:T(8,128)(2,1)S(1)}, u32[]{:S(2)}, u32[]{:S(2)}) collective-permute-start(bf16[2,3,48,512]{3,2,1,0:T(8,128)(2,1)S(1)} %pad_maximum_fusion.6), channel_id=1, source_target_pairs={{0,448},{16,80},{64,128},{80,16},{128,64},{144,208},{192,256},{208... | collective-permute-start | bytes 884744 | tf_op jit(solution)/shard_map/ppermute | solution.py:24
  31.8 8.2 %collective-permute-done.5 = bf16[1,3,48,512]{3,2,1,0:T(8,128)(2,1)S(1)} collective-permute-done((bf16[1,3,48,512]{3,2,1,0:T(8,128)(2,1)S(1)}, bf16[1,3,48,512]{3,2,1,0:T(8,128)(2,1)S(1)}, u32[]{:S(2)}, u32[]{:S(2)}) %collective-permute-start.5) | collective-permute-done | bytes 147488 | tf_op jit(solution)/shard_map/ppermute | solution.py:28
  40.0 4.3 %collective-permute-start.6 = (bf16[1,3,48,512]{3,2,1,0:T(8,128)(2,1)S(1)}, bf16[1,3,48,512]{3,2,1,0:T(8,128)(2,1)S(1)}, u32[]{:S(2)}, u32[]{:S(2)}) collective-permute-start(bf16[1,3,48,512]{3,2,1,0:T(8,128)(2,1)S(1)} %collective-permute-done.5), channel_id=1, source_target_pairs={{0,64},{16,464},{64,0},{80,144},{128,192},{144,80},{192,128},{208,... | collective-permute-start | bytes 442376 | tf_op jit(solution)/shard_map/ppermute | solution.py:24
  44.3 3.1 %collective-permute-done.6 = bf16[1,3,48,512]{3,2,1,0:T(8,128)(2,1)S(1)} collective-permute-done((bf16[1,3,48,512]{3,2,1,0:T(8,128)(2,1)S(1)}, bf16[1,3,48,512]{3,2,1,0:T(8,128)(2,1)S(1)}, u32[]{:S(2)}, u32[]{:S(2)}) %collective-permute-start.6) | collective-permute-done | bytes 147488 | tf_op jit(solution)/shard_map/ppermute | solution.py:24
  47.5 10.6 %collective-permute-start.7 = (bf16[2,3,48,512]{3,2,1,0:T(8,128)(2,1)S(1)}, bf16[2,3,48,512]{3,2,1,0:T(8,128)(2,1)S(1)}, u32[]{:S(2)}, u32[]{:S(2)}) collective-permute-start(bf16[2,3,48,512]{3,2,1,0:T(8,128)(2,1)S(1)} %pad_maximum_fusion.7), channel_id=1, source_target_pairs={{0,448},{16,80},{64,128},{80,16},{128,64},{144,208},{192,256},{208... | collective-permute-start | bytes 884744 | tf_op jit(solution)/shard_map/ppermute | solution.py:24
  60.9 5.0 %collective-permute-done.7 = bf16[2,3,48,512]{3,2,1,0:T(8,128)(2,1)S(1)} collective-permute-done((bf16[2,3,48,512]{3,2,1,0:T(8,128)(2,1)S(1)}, bf16[2,3,48,512]{3,2,1,0:T(8,128)(2,1)S(1)}, u32[]{:S(2)}, u32[]{:S(2)}) %collective-permute-start.7) | collective-permute-done | bytes 294944 | tf_op jit(solution)/shard_map/ppermute | solution.py:24
  67.8 4.9 %collective-permute-start.4 = (bf16[2,3,48,512]{3,2,1,0:T(8,128)(2,1)S(1)}, bf16[2,3,48,512]{3,2,1,0:T(8,128)(2,1)S(1)}, u32[]{:S(2)}, u32[]{:S(2)}) collective-permute-start(bf16[2,3,48,512]{3,2,1,0:T(8,128)(2,1)S(1)} %collective-permute-done.3), channel_id=1, source_target_pairs={{0,448},{16,80},{64,128},{80,16},{128,64},{144,208},{192,256},{208... | collective-permute-start | bytes 884744 | tf_op jit(solution)/shard_map/ppermute | solution.py:24
  72.8 5.0 %collective-permute-done.8 = bf16[2,3,48,512]{3,2,1,0:T(8,128)(2,1)} collective-permute-done((bf16[2,3,48,512]{3,2,1,0:T(8,128)(2,1)S(1)}, bf16[2,3,48,512]{3,2,1,0:T(8,128)(2,1)}, u32[]{:S(2)}, u32[]{:S(2)}) %collective-permute-start.8) | collective-permute-done | bytes 294944 | tf_op jit(solution)/shard_map/ppermute | solution.py:24
  77.8 4.3 %collective-permute-start.9 = (bf16[2,3,48,512]{3,2,1,0:T(8,128)(2,1)}, bf16[2,3,48,512]{3,2,1,0:T(8,128)(2,1)}, u32[]{:S(2)}, u32[]{:S(2)}) collective-permute-start(bf16[2,3,48,512]{3,2,1,0:T(8,128)(2,1)} %collective-permute-done.8), channel_id=1, source_target_pairs={{0,448},{16,80},{64,128},{80,16},{128,64},{144,208},{192,256},{208... | collective-permute-start | bytes 884744 | tf_op jit(solution)/shard_map/ppermute | solution.py:24
  91.4 2.9 %multiply_convert_fusion.2 = (bf16[1024,768]{1,0:T(8,128)(2,1)S(1)}, bf16[1024,768]{1,0:T(8,128)(2,1)S(1)}, bf16[1024,768]{1,0:T(8,128)(2,1)S(1)}) fusion(f32[1024,768]{1,0:T(8,128)S(1)} %fusion.44, f32[1024,768]{1,0:T(8,128)S(1)} %fusion.3, bf16[768,512]{1,0:T(8,128)(2,1)S(1)} %bitcast.78, bf16[512,512]{1,0:T(8,128)(2,1)S(1)} %bitcast.66, ...), kind=kOutput, calls=%fused_computation.2 | convolution fusion | flops 819200000 | bytes 12845056 | tf_op jit(solution)/shard_map/dot_general | solution.py:52
  103.1 4.3 %collective-permute-start.15 = (bf16[2,3,48,512]{3,0,2,1:T(2,128)(2,1)S(1)}, bf16[2,3,48,512]{3,0,2,1:T(2,128)(2,1)S(1)}, u32[]{:S(2)}, u32[]{:S(2)}) collective-permute-start(bf16[2,3,48,512]{3,0,2,1:T(2,128)(2,1)S(1)} %get-tuple-element.15), channel_id=1, source_target_pairs={{0,448},{16,80},{64,128},{80,16},{128,64},{144,208},{192,256},{208... | collective-permute-start | bytes 884744 | tf_op jit(solution)/shard_map/ppermute | solution.py:24
  109.4 3.5 %collective-permute-done.15 = bf16[2,3,48,512]{3,0,2,1:T(2,128)(2,1)S(1)} collective-permute-done((bf16[2,3,48,512]{3,0,2,1:T(2,128)(2,1)S(1)}, bf16[2,3,48,512]{3,0,2,1:T(2,128)(2,1)S(1)}, u32[]{:S(2)}, u32[]{:S(2)}) %collective-permute-start.15) | collective-permute-done | bytes 294944 | tf_op jit(solution)/shard_map/ppermute | solution.py:24
  115.5 4.3 %collective-permute-start.11 = (bf16[2,3,48,512]{3,0,2,1:T(2,128)(2,1)}, bf16[2,3,48,512]{3,0,2,1:T(2,128)(2,1)}, u32[]{:S(2)}, u32[]{:S(2)}) collective-permute-start(bf16[2,3,48,512]{3,0,2,1:T(2,128)(2,1)} %get-tuple-element.16), channel_id=1, source_target_pairs={{0,448},{16,80},{64,128},{80,16},{128,64},{144,208},{192,256},{208... | collective-permute-start | bytes 884744 | tf_op jit(solution)/shard_map/ppermute | solution.py:24
  119.8 5.4 %collective-permute-done.16 = bf16[2,3,48,512]{3,0,2,1:T(2,128)(2,1)S(1)} collective-permute-done((bf16[2,3,48,512]{3,0,2,1:T(2,128)(2,1)S(1)}, bf16[2,3,48,512]{3,0,2,1:T(2,128)(2,1)S(1)}, u32[]{:S(2)}, u32[]{:S(2)}) %collective-permute-start.16) | collective-permute-done | bytes 294944 | tf_op jit(solution)/shard_map/ppermute | solution.py:24
  126.3 4.3 %collective-permute-start.17 = (bf16[2,3,48,512]{3,0,2,1:T(2,128)(2,1)}, bf16[2,3,48,512]{3,0,2,1:T(2,128)(2,1)}, u32[]{:S(2)}, u32[]{:S(2)}) collective-permute-start(bf16[2,3,48,512]{3,0,2,1:T(2,128)(2,1)} %add_convert_fusion), channel_id=1, source_target_pairs={{0,448},{16,80},{64,128},{80,16},{128,64},{144,208},{192,256},{208... | collective-permute-start | bytes 884744 | tf_op jit(solution)/shard_map/ppermute | solution.py:24
  133.3 8.3 %all-to-all-start.1 = ((bf16[16,64,512]{2,1,0:T(8,128)(2,1)}), bf16[16,64,512]{2,1,0:T(8,128)(2,1)S(1)}, u32[]{:S(2)}, u32[]{:S(2)}) async-start(bf16[16,64,512]{2,1,0:T(8,128)(2,1)} %fusion.1), calls=%async_computation.1 | async-start | bytes 2097152 | tf_op jit(solution)/shard_map/all_to_all | solution.py:146
  145.6 3.9 %collective-permute-start.18 = (bf16[1,3,48,512]{3,0,2,1:T(2,128)(2,1)S(1)}, bf16[1,3,48,512]{3,0,2,1:T(2,128)(2,1)S(1)}, u32[]{:S(2)}, u32[]{:S(2)}) collective-permute-start(bf16[1,3,48,512]{3,0,2,1:T(2,128)(2,1)S(1)} %slice.205), channel_id=1, source_target_pairs={{0,64},{16,464},{64,0},{80,144},{128,192},{144,80},{192,128},{208,... | collective-permute-start | bytes 442376 | tf_op jit(solution)/shard_map/ppermute | solution.py:24
  149.5 4.9 %collective-permute-done.12 = bf16[2,3,48,512]{3,0,2,1:T(2,128)(2,1)S(1)} collective-permute-done((bf16[2,3,48,512]{3,0,2,1:T(2,128)(2,1)S(1)}, bf16[2,3,48,512]{3,0,2,1:T(2,128)(2,1)S(1)}, u32[]{:S(2)}, u32[]{:S(2)}) %collective-permute-start.12) | collective-permute-done | bytes 294944 | tf_op jit(solution)/shard_map/ppermute | solution.py:24
  154.9 2.9 %collective-permute-start.13 = (bf16[2,3,48,512]{3,0,2,1:T(2,128)(2,1)S(1)}, bf16[2,3,48,512]{3,0,2,1:T(2,128)(2,1)S(1)}, u32[]{:S(2)}, u32[]{:S(2)}) collective-permute-start(bf16[2,3,48,512]{3,0,2,1:T(2,128)(2,1)S(1)} %add_convert_fusion.2), channel_id=1, source_target_pairs={{0,448},{16,80},{64,128},{80,16},{128,64},{144,208},{192,256},{208... | collective-permute-start | bytes 884744 | tf_op jit(solution)/shard_map/ppermute | solution.py:24
  158.7 4.6 %collective-permute-start.19 = (bf16[1,3,48,512]{3,0,2,1:T(2,128)(2,1)S(1)}, bf16[1,3,48,512]{3,0,2,1:T(2,128)(2,1)S(1)}, u32[]{:S(2)}, u32[]{:S(2)}) collective-permute-start(bf16[1,3,48,512]{3,0,2,1:T(2,128)(2,1)S(1)} %fusion.8), channel_id=1, source_target_pairs={{0,32},{32,0},{1,33},{33,1},{2,34},{34,2},{3,35},{35,3},{4,36},{36... | collective-permute-start | bytes 442376 | tf_op jit(solution)/shard_map/ppermute | solution.py:28
  163.3 3.9 %collective-permute-done.13 = bf16[2,3,48,512]{3,0,2,1:T(2,128)(2,1)S(1)} collective-permute-done((bf16[2,3,48,512]{3,0,2,1:T(2,128)(2,1)S(1)}, bf16[2,3,48,512]{3,0,2,1:T(2,128)(2,1)S(1)}, u32[]{:S(2)}, u32[]{:S(2)}) %collective-permute-start.13) | collective-permute-done | bytes 294944 | tf_op jit(solution)/shard_map/ppermute | solution.py:24
  171.4 5.1 %collective-permute-done.14 = bf16[1,3,48,512]{3,0,2,1:T(2,128)(2,1)S(1)} collective-permute-done((bf16[1,3,48,512]{3,0,2,1:T(2,128)(2,1)S(1)}, bf16[1,3,48,512]{3,0,2,1:T(2,128)(2,1)S(1)}, u32[]{:S(2)}, u32[]{:S(2)}) %collective-permute-start.14) | collective-permute-done | bytes 147488 | tf_op jit(solution)/shard_map/ppermute | solution.py:24
  (102 shorter events, 52.1 us)
Async XLA Ops:
  5.3 76.9 %all-to-all-start = ((bf16[16,64,512]{2,1,0:T(8,128)(2,1)}), bf16[16,64,512]{2,1,0:T(8,128)(2,1)S(1)}, u32[]{:S(2)}, u32[]{:S(2)}) async-start(bf16[16,64,512]{2,1,0:T(8,128)(2,1)} %pad_maximum_fusion), calls=%async_computation | async-start | bytes 2097152 | tf_op jit(solution)/shard_map/all_to_all | solution.py:97
  14.8 7.8 %collective-permute-start.1 = (bf16[1,3,48,512]{3,2,1,0:T(8,128)(2,1)S(1)}, bf16[1,3,48,512]{3,2,1,0:T(8,128)(2,1)S(1)}, u32[]{:S(2)}, u32[]{:S(2)}) collective-permute-start(bf16[1,3,48,512]{3,2,1,0:T(8,128)(2,1)S(1)} %fusion.19), channel_id=1, source_target_pairs={{0,64},{16,464},{64,0},{80,144},{128,192},{144,80},{192,128},{208,... | collective-permute-start | bytes 442376 | tf_op jit(solution)/shard_map/ppermute | solution.py:24
  17.6 22.5 %collective-permute-start.5 = (bf16[1,3,48,512]{3,2,1,0:T(8,128)(2,1)S(1)}, bf16[1,3,48,512]{3,2,1,0:T(8,128)(2,1)S(1)}, u32[]{:S(2)}, u32[]{:S(2)}) collective-permute-start(bf16[1,3,48,512]{3,2,1,0:T(8,128)(2,1)S(1)} %fusion.19), channel_id=1, source_target_pairs={{0,32},{32,0},{1,33},{33,1},{2,34},{34,2},{3,35},{35,3},{4,36},{36... | collective-permute-start | bytes 442376 | tf_op jit(solution)/shard_map/ppermute | solution.py:28
  22.7 35.4 %collective-permute-start.2 = (bf16[2,3,48,512]{3,2,1,0:T(8,128)(2,1)S(1)}, bf16[2,3,48,512]{3,2,1,0:T(8,128)(2,1)S(1)}, u32[]{:S(2)}, u32[]{:S(2)}) collective-permute-start(bf16[2,3,48,512]{3,2,1,0:T(8,128)(2,1)S(1)} %pad_maximum_fusion.6), channel_id=1, source_target_pairs={{0,448},{16,80},{64,128},{80,16},{128,64},{144,208},{192,256},{208... | collective-permute-start | bytes 884744 | tf_op jit(solution)/shard_map/ppermute | solution.py:24
  40.0 42.1 %copy-start.2 = (bf16[1,3,48,512]{3,2,1,0:T(8,128)(2,1)}, bf16[1,3,48,512]{3,2,1,0:T(8,128)(2,1)S(1)}, u32[]{:S(2)}) copy-start(bf16[1,3,48,512]{3,2,1,0:T(8,128)(2,1)S(1)} %collective-permute-done.5) | copy-start | bytes 442372
  40.0 7.4 %collective-permute-start.6 = (bf16[1,3,48,512]{3,2,1,0:T(8,128)(2,1)S(1)}, bf16[1,3,48,512]{3,2,1,0:T(8,128)(2,1)S(1)}, u32[]{:S(2)}, u32[]{:S(2)}) collective-permute-start(bf16[1,3,48,512]{3,2,1,0:T(8,128)(2,1)S(1)} %collective-permute-done.5), channel_id=1, source_target_pairs={{0,64},{16,464},{64,0},{80,144},{128,192},{144,80},{192,128},{208,... | collective-permute-start | bytes 442376 | tf_op jit(solution)/shard_map/ppermute | solution.py:24
  47.4 34.7 %copy-start.3 = (bf16[1,3,48,512]{3,2,1,0:T(8,128)(2,1)}, bf16[1,3,48,512]{3,2,1,0:T(8,128)(2,1)S(1)}, u32[]{:S(2)}) copy-start(bf16[1,3,48,512]{3,2,1,0:T(8,128)(2,1)S(1)} %collective-permute-done.6) | copy-start | bytes 442372
  47.5 18.4 %collective-permute-start.7 = (bf16[2,3,48,512]{3,2,1,0:T(8,128)(2,1)S(1)}, bf16[2,3,48,512]{3,2,1,0:T(8,128)(2,1)S(1)}, u32[]{:S(2)}, u32[]{:S(2)}) collective-permute-start(bf16[2,3,48,512]{3,2,1,0:T(8,128)(2,1)S(1)} %pad_maximum_fusion.7), channel_id=1, source_target_pairs={{0,448},{16,80},{64,128},{80,16},{128,64},{144,208},{192,256},{208... | collective-permute-start | bytes 884744 | tf_op jit(solution)/shard_map/ppermute | solution.py:24
  58.1 9.7 %collective-permute-start.3 = (bf16[2,3,48,512]{3,2,1,0:T(8,128)(2,1)S(1)}, bf16[2,3,48,512]{3,2,1,0:T(8,128)(2,1)S(1)}, u32[]{:S(2)}, u32[]{:S(2)}) collective-permute-start(bf16[2,3,48,512]{3,2,1,0:T(8,128)(2,1)S(1)} %collective-permute-done.2), channel_id=1, source_target_pairs={{0,64},{16,464},{64,0},{80,144},{128,192},{144,80},{192,128},{208,... | collective-permute-start | bytes 884744 | tf_op jit(solution)/shard_map/ppermute | solution.py:24
  65.9 11.9 %collective-permute-start.8 = (bf16[2,3,48,512]{3,2,1,0:T(8,128)(2,1)S(1)}, bf16[2,3,48,512]{3,2,1,0:T(8,128)(2,1)}, u32[]{:S(2)}, u32[]{:S(2)}) collective-permute-start(bf16[2,3,48,512]{3,2,1,0:T(8,128)(2,1)S(1)} %collective-permute-done.7), channel_id=1, source_target_pairs={{0,64},{16,464},{64,0},{80,144},{128,192},{144,80},{192,128},{208,... | collective-permute-start | bytes 884744 | tf_op jit(solution)/shard_map/ppermute | solution.py:24
  67.8 14.4 %collective-permute-start.4 = (bf16[2,3,48,512]{3,2,1,0:T(8,128)(2,1)S(1)}, bf16[2,3,48,512]{3,2,1,0:T(8,128)(2,1)S(1)}, u32[]{:S(2)}, u32[]{:S(2)}) collective-permute-start(bf16[2,3,48,512]{3,2,1,0:T(8,128)(2,1)S(1)} %collective-permute-done.3), channel_id=1, source_target_pairs={{0,448},{16,80},{64,128},{80,16},{128,64},{144,208},{192,256},{208... | collective-permute-start | bytes 884744 | tf_op jit(solution)/shard_map/ppermute | solution.py:24
  77.8 10.2 %collective-permute-start.9 = (bf16[2,3,48,512]{3,2,1,0:T(8,128)(2,1)}, bf16[2,3,48,512]{3,2,1,0:T(8,128)(2,1)}, u32[]{:S(2)}, u32[]{:S(2)}) collective-permute-start(bf16[2,3,48,512]{3,2,1,0:T(8,128)(2,1)} %collective-permute-done.8), channel_id=1, source_target_pairs={{0,448},{16,80},{64,128},{80,16},{128,64},{144,208},{192,256},{208... | collective-permute-start | bytes 884744 | tf_op jit(solution)/shard_map/ppermute | solution.py:24
  82.2 7.0 %collective-permute-start = (bf16[16,64,512]{2,1,0:T(8,128)(2,1)S(1)}, bf16[16,64,512]{2,1,0:T(8,128)(2,1)S(1)}, u32[]{:S(2)}, u32[]{:S(2)}) collective-permute-start(bf16[16,64,512]{2,1,0:T(8,128)(2,1)S(1)} %all-to-all-done), channel_id=1, source_target_pairs={{0,16},{16,0},{1,17},{17,1},{2,18},{18,2},{3,19},{19,3},{4,20},{20... | collective-permute-start | bytes 3145736 | tf_op jit(solution)/shard_map/ppermute | solution.py:28
  103.1 9.8 %collective-permute-start.15 = (bf16[2,3,48,512]{3,0,2,1:T(2,128)(2,1)S(1)}, bf16[2,3,48,512]{3,0,2,1:T(2,128)(2,1)S(1)}, u32[]{:S(2)}, u32[]{:S(2)}) collective-permute-start(bf16[2,3,48,512]{3,0,2,1:T(2,128)(2,1)S(1)} %get-tuple-element.15), channel_id=1, source_target_pairs={{0,448},{16,80},{64,128},{80,16},{128,64},{144,208},{192,256},{208... | collective-permute-start | bytes 884744 | tf_op jit(solution)/shard_map/ppermute | solution.py:24
  107.5 23.3 %collective-permute-start.10 = (bf16[16,64,512]{2,1,0:T(8,128)(2,1)S(1)}, bf16[16,64,512]{2,1,0:T(8,128)(2,1)S(1)}, u32[]{:S(2)}, u32[]{:S(2)}) collective-permute-start(bf16[16,64,512]{2,1,0:T(8,128)(2,1)S(1)} %pad_maximum_fusion.3), channel_id=1, source_target_pairs={{0,16},{16,0},{1,17},{17,1},{2,18},{18,2},{3,19},{19,3},{4,20},{20... | collective-permute-start | bytes 3145736 | tf_op jit(solution)/shard_map/ppermute | solution.py:28
  113.4 11.8 %collective-permute-start.16 = (bf16[2,3,48,512]{3,0,2,1:T(2,128)(2,1)S(1)}, bf16[2,3,48,512]{3,0,2,1:T(2,128)(2,1)S(1)}, u32[]{:S(2)}, u32[]{:S(2)}) collective-permute-start(bf16[2,3,48,512]{3,0,2,1:T(2,128)(2,1)S(1)} %add_convert_fusion.1), channel_id=1, source_target_pairs={{0,64},{16,464},{64,0},{80,144},{128,192},{144,80},{192,128},{208,... | collective-permute-start | bytes 884744 | tf_op jit(solution)/shard_map/ppermute | solution.py:24
  115.5 26.1 %collective-permute-start.11 = (bf16[2,3,48,512]{3,0,2,1:T(2,128)(2,1)}, bf16[2,3,48,512]{3,0,2,1:T(2,128)(2,1)}, u32[]{:S(2)}, u32[]{:S(2)}) collective-permute-start(bf16[2,3,48,512]{3,0,2,1:T(2,128)(2,1)} %get-tuple-element.16), channel_id=1, source_target_pairs={{0,448},{16,80},{64,128},{80,16},{128,64},{144,208},{192,256},{208... | collective-permute-start | bytes 884744 | tf_op jit(solution)/shard_map/ppermute | solution.py:24
  126.3 15.3 %collective-permute-start.17 = (bf16[2,3,48,512]{3,0,2,1:T(2,128)(2,1)}, bf16[2,3,48,512]{3,0,2,1:T(2,128)(2,1)}, u32[]{:S(2)}, u32[]{:S(2)}) collective-permute-start(bf16[2,3,48,512]{3,0,2,1:T(2,128)(2,1)} %add_convert_fusion), channel_id=1, source_target_pairs={{0,448},{16,80},{64,128},{80,16},{128,64},{144,208},{192,256},{208... | collective-permute-start | bytes 884744 | tf_op jit(solution)/shard_map/ppermute | solution.py:24
  133.3 44.6 %all-to-all-start.1 = ((bf16[16,64,512]{2,1,0:T(8,128)(2,1)}), bf16[16,64,512]{2,1,0:T(8,128)(2,1)S(1)}, u32[]{:S(2)}, u32[]{:S(2)}) async-start(bf16[16,64,512]{2,1,0:T(8,128)(2,1)} %fusion.1), calls=%async_computation.1 | async-start | bytes 2097152 | tf_op jit(solution)/shard_map/all_to_all | solution.py:146
  143.3 11.1 %collective-permute-start.12 = (bf16[2,3,48,512]{3,0,2,1:T(2,128)(2,1)S(1)}, bf16[2,3,48,512]{3,0,2,1:T(2,128)(2,1)S(1)}, u32[]{:S(2)}, u32[]{:S(2)}) collective-permute-start(bf16[2,3,48,512]{3,0,2,1:T(2,128)(2,1)S(1)} %get-tuple-element.14), channel_id=1, source_target_pairs={{0,64},{16,464},{64,0},{80,144},{128,192},{144,80},{192,128},{208,... | collective-permute-start | bytes 884744 | tf_op jit(solution)/shard_map/ppermute | solution.py:24
  145.6 12.7 %collective-permute-start.18 = (bf16[1,3,48,512]{3,0,2,1:T(2,128)(2,1)S(1)}, bf16[1,3,48,512]{3,0,2,1:T(2,128)(2,1)S(1)}, u32[]{:S(2)}, u32[]{:S(2)}) collective-permute-start(bf16[1,3,48,512]{3,0,2,1:T(2,128)(2,1)S(1)} %slice.205), channel_id=1, source_target_pairs={{0,64},{16,464},{64,0},{80,144},{128,192},{144,80},{192,128},{208,... | collective-permute-start | bytes 442376 | tf_op jit(solution)/shard_map/ppermute | solution.py:24
  154.9 12.3 %collective-permute-start.13 = (bf16[2,3,48,512]{3,0,2,1:T(2,128)(2,1)S(1)}, bf16[2,3,48,512]{3,0,2,1:T(2,128)(2,1)S(1)}, u32[]{:S(2)}, u32[]{:S(2)}) collective-permute-start(bf16[2,3,48,512]{3,0,2,1:T(2,128)(2,1)S(1)} %add_convert_fusion.2), channel_id=1, source_target_pairs={{0,448},{16,80},{64,128},{80,16},{128,64},{144,208},{192,256},{208... | collective-permute-start | bytes 884744 | tf_op jit(solution)/shard_map/ppermute | solution.py:24
  158.7 12.7 %collective-permute-start.19 = (bf16[1,3,48,512]{3,0,2,1:T(2,128)(2,1)S(1)}, bf16[1,3,48,512]{3,0,2,1:T(2,128)(2,1)S(1)}, u32[]{:S(2)}, u32[]{:S(2)}) collective-permute-start(bf16[1,3,48,512]{3,0,2,1:T(2,128)(2,1)S(1)} %fusion.8), channel_id=1, source_target_pairs={{0,32},{32,0},{1,33},{33,1},{2,34},{34,2},{3,35},{35,3},{4,36},{36... | collective-permute-start | bytes 442376 | tf_op jit(solution)/shard_map/ppermute | solution.py:28
  167.9 8.6 %collective-permute-start.14 = (bf16[1,3,48,512]{3,0,2,1:T(2,128)(2,1)S(1)}, bf16[1,3,48,512]{3,0,2,1:T(2,128)(2,1)S(1)}, u32[]{:S(2)}, u32[]{:S(2)}) collective-permute-start(bf16[1,3,48,512]{3,0,2,1:T(2,128)(2,1)S(1)} %slice.206), channel_id=1, source_target_pairs={{0,64},{16,464},{64,0},{80,144},{128,192},{144,80},{192,128},{208,... | collective-permute-start | bytes 442376 | tf_op jit(solution)/shard_map/ppermute | solution.py:24
  (10 other events, 91.2 us)

commit v2 on v1

v2 whole, which is shorter than its diff:
```python
import functools

import jax
import jax.numpy as jnp
from jax import lax
from jax.experimental import pallas as pl
from jax.experimental.pallas import tpu as pltpu
from jax.sharding import Mesh, PartitionSpec as P

grad_scale = 0.015625
PAD = 48
F32 = jnp.float32
BF16 = jnp.bfloat16


def swap_z(rows, parity):
    size = lax.axis_size("z")
    pairs = [(z, (z + (1 if (z + parity) % 2 == 0 else -1)) % size) for z in range(size)]
    return lax.ppermute(rows, "z", pairs)


def swap(rows, axis):
    return lax.ppermute(rows, axis, [(0, 1), (1, 0)])


def add(one, two):
    return one.astype(F32) + two.astype(F32)


together = lax.optimization_barrier


def sum_z(pieces, parity):
    first, second, third, last = pieces
    third = add(third, swap_z(last, parity + 3)).astype(BF16)
    second = add(second, swap_z(third, parity + 2)).astype(BF16)
    first = add(first, swap_z(second, parity + 1))
    return add(first[:1], swap_z(first[1:].astype(BF16), parity))


def dot(left, right, contract):
    return lax.dot_general(left, right, ((contract[:1], contract[1:]), ((), ())), preferred_element_type=F32)


def kernel_call(body, outs, scratch=(), flops=0, grant=32):
    return pl.pallas_call(
        body,
        out_shape=outs,
        scratch_shapes=list(scratch),
        compiler_params=pltpu.CompilerParams(vmem_limit_bytes=grant * 2**20),
        cost_estimate=pl.CostEstimate(flops=flops, bytes_accessed=1 << 20, transcendentals=0),
    )


def dispatch_body(capacity, latent, cotangent, routes, scores, send, first, second):
    experts = send.shape[0]
    slots, rows = first.shape
    width = latent.shape[1]
    slot = lax.broadcasted_iota(jnp.int32, (slots, rows), 0)
    bits = capacity.bit_length() - 1
    expert = slot >> bits
    place = slot & (capacity - 1)
    named_0 = routes[0:1, :] == expert
    named_1 = routes[1:2, :] == expert
    named = jnp.where(named_0 | named_1, 1.0, 0.0)
    upper = lax.broadcasted_iota(jnp.int32, (rows, rows), 0) < lax.broadcasted_iota(
        jnp.int32, (rows, rows), 1
    )
    ranks = dot(named.astype(BF16), jnp.where(upper, 1.0, 0.0).astype(BF16), (1, 0))
    hit = ranks == place.astype(F32)
    one = jnp.where(named_0 & hit, 1.0, 0.0)
    two = jnp.where(named_1 & hit, 1.0, 0.0)
    first[...] = one.astype(BF16)
    second[...] = two.astype(BF16)
    table = (one + two).astype(BF16)
    score = jnp.sum(one * scores[0:1, :] + two * scores[1:2, :], axis=1, keepdims=True)
    placed = dot(table, latent[...], (1, 0)).astype(BF16)
    weighted = (score * dot(table, cotangent[...], (1, 0))).astype(BF16)
    send[:, :capacity, :] = placed.reshape(experts, capacity, width)
    send[:, capacity:, :] = weighted.reshape(experts, capacity, width)


def combine_body(capacity, back, first, second, scores, cotangent, mixed, latent_grad, score_grad):
    slots, rows = first.shape
    width = back.shape[2]
    outs = back[:, :capacity, :].reshape(slots, width)
    tokens = back[:, capacity:, :].reshape(slots, width)
    cot = cotangent[...].astype(F32)
    total = jnp.zeros((rows, width), F32)
    sums = []
    for k, table in enumerate((first, second)):
        picked = dot(table[...], outs, (0, 0))
        score = jnp.broadcast_to(scores[k : k + 1, :], (rows, rows)).T
        total = total + score[:, 0:1] * picked
        own = jnp.sum(cot * picked, axis=1, keepdims=True)
        sums.append(jnp.broadcast_to(own, (rows, rows)).T[0:1, :])
    mixed[...] = total.astype(BF16)
    score_grad[...] = jnp.concatenate(sums, axis=0)
    merged = first[...] + second[...]
    latent_grad[...] = dot(merged, tokens, (0, 0)).astype(BF16)


def expert_body(capacity, last, *refs):
    mine, theirs = refs[:2]
    pieces = refs[2:6]
    refs = refs[6:]
    if last:
        sums, refs = refs[:2], refs[2:]
    grads = refs[:4]
    results = refs[4:6]
    wg, wu, wd, xs, gs, hs, gbs, ubs = refs[6:]
    width = mine.shape[2]
    for i, piece in enumerate(pieces):
        for j in range(2):
            block = slice((2 * i + j) * PAD, (2 * i + j + 1) * PAD)
            for k, weight in enumerate((wg, wu, wd)):
                weight[block, :] = piece[j, k]
    sources = mine.shape[0] // 2
    tile = sources * capacity
    for i in range(4):
        tokens = (mine, theirs)[i // 2]
        part = slice((i % 2) * sources, (i % 2 + 1) * sources)
        rows = slice(i * tile, (i + 1) * tile)
        x = tokens[part, :capacity, :].reshape(tile, width)
        g = tokens[part, capacity:, :].reshape(tile, width)
        xs[rows, :] = x
        gs[rows, :] = g
        gate = dot(x, wg[...], (1, 1))
        up = dot(x, wu[...], (1, 1))
        hidden_grad = dot(g, wd[...], (1, 1))
        sig = jax.nn.sigmoid(gate)
        act = gate * sig
        hidden = (act * up).astype(BF16)
        gate_back = (hidden_grad * up * (sig * (1.0 + gate * (1.0 - sig)))).astype(BF16)
        up_back = (hidden_grad * act).astype(BF16)
        hs[rows, :] = hidden
        gbs[rows, :] = gate_back
        ubs[rows, :] = up_back
        outs = dot(hidden, wd[...], (1, 0)).reshape(sources, capacity, width)
        back = dot(gate_back, wg[...], (1, 0)) + dot(up_back, wu[...], (1, 0))
        back = back.reshape(sources, capacity, width)
        result = results[i // 2]
        if last:
            outs = outs + sums[i // 2][part, :capacity, :]
            back = back + sums[i // 2][part, capacity:, :]
        result[part, :capacity, :] = outs.astype(result.dtype)
        result[part, capacity:, :] = back.astype(result.dtype)
    for k, (left, right) in enumerate(((gbs, xs), (ubs, xs), (hs, gs))):
        term = (dot(left[...], right[...], (0, 0)) * grad_scale).astype(BF16)
        for i, grad in enumerate(grads):
            for j in range(2):
                grad[j, k] = term[(2 * i + j) * PAD : (2 * i + j + 1) * PAD, :]


def expert_call(capacity, mine, theirs, pieces, sums=()):
    last = len(sums) > 0
    both = mine.shape
    width = both[2]
    slots = both[0] * capacity * 2
    hidden = 8 * PAD
    outs = [jax.ShapeDtypeStruct(p.shape, BF16) for p in pieces]
    outs += [jax.ShapeDtypeStruct(both, F32), jax.ShapeDtypeStruct(both, BF16 if last else F32)]
    scratch = [pltpu.VMEM((hidden, width), BF16)] * 3 + [pltpu.VMEM((slots, width), BF16)] * 2
    scratch += [pltpu.VMEM((slots, hidden), BF16)] * 3
    call = kernel_call(
        functools.partial(expert_body, capacity, last), outs, scratch, 18 * slots * hidden * width
    )
    got = call(mine, theirs, *pieces, *sums)
    return got[:4], got[4:]


def shards(latent, routes, scores, cotangent, w_gate, w_up, w_down):
    experts = lax.axis_size("x") * lax.axis_size("yl")
    tok_rows, width = latent.shape
    capacity = 4 * tok_rows // experts
    slots = experts * capacity
    hidden_rows = w_gate.shape[1]
    own = jnp.pad(
        jnp.stack([w_gate[0], w_up[0], w_down[0]]), ((0, 0), (0, PAD - hidden_rows), (0, 0))
    )[None]
    other = swap(own, "yh")

    shape = (experts, 2 * capacity, width)
    table = jax.ShapeDtypeStruct((slots, tok_rows), BF16)
    score_rows = scores.T
    send, first, second = kernel_call(
        functools.partial(dispatch_body, capacity),
        [jax.ShapeDtypeStruct(shape, BF16), table, table],
        grant=56,
    )(latent, cotangent, routes.T, score_rows)

    near_got = swap_z(own, 0)
    other, near_got, send = together((other, near_got, send))
    mine = lax.all_to_all(send, ("x", "yl"), 0, 0, tiled=True)
    near = [jnp.concatenate([own, near_got], axis=0)]
    near.append(swap_z(near[0], 1))
    far_got = swap_z(other, 0)
    near[1], far_got = together((near[1], far_got))
    far = [jnp.concatenate([other, far_got], axis=0)]
    near.append(swap_z(near[1], 0))
    far.append(swap_z(far[0], 1))
    near[2], far[1], mine = together((near[2], far[1], mine))
    near.append(swap_z(near[2], 1))
    far.append(swap_z(far[1], 0))
    theirs = swap(mine, "core")
    near[3], far[2], theirs = together((near[3], far[2], theirs))
    far.append(swap_z(far[2], 1))

    near_terms, sums = expert_call(capacity, mine, theirs, near)
    far_terms, (local, rest) = expert_call(capacity, mine, theirs, far, sums)

    far_sum = sum_z(far_terms, 0).astype(BF16)
    near_sum = sum_z(near_terms, 0)
    back = lax.all_to_all(
        add(local, swap(rest, "core")).astype(BF16), ("x", "yl"), 0, 0, tiled=True
    )
    got = swap(far_sum, "yh")
    row = jax.ShapeDtypeStruct((tok_rows, width), BF16)
    mixed, latent_grad, score_grad = kernel_call(
        functools.partial(combine_body, capacity),
        [row, row, jax.ShapeDtypeStruct((2, tok_rows), F32)],
    )(back, first, second, score_rows, cotangent)
    got, mixed = together((got, mixed))
    grads = (near_sum + got.astype(F32))[0, :, :hidden_rows]
    return (mixed, latent_grad, score_grad.T, grads[0:1], grads[1:2], grads[2:3])


def solution(mesh):
    fine = Mesh(
        mesh.devices.reshape(8, 2, 2, 4, 4), ("z", "yh", "core", "x", "yl")
    )
    fsdp, expert = ("z", "yh", "core"), ("x", "yl")
    rows = P(fsdp + expert, None)
    weight = P(expert, fsdp, None)
    return jax.shard_map(
        shards,
        mesh=fine,
        in_specs=(rows,) * 4 + (weight,) * 3,
        out_specs=(rows,) * 3 + (weight,) * 3,
        check_vma=False,
    )
```

time: 182 us -> 156 us (0.86)
  matrix products: 14.9 us -> 0 us
  Pallas kernels: 0 us -> 13.4 us
  starting transfers between devices: 96.7 us -> 83.9 us
  local copies, waits for them, and re-layouts: 12.2 us -> 3.93 us
  other arithmetic: 9.42 us -> 2.78 us
  waiting for transfers between devices: 46.2 us -> 50.4 us
    dot_general x15 -> x0, matrix products: 14.9 us -> none  [the longest x3 4.94 us: against(): lax.dot_general(left, right, (((1,), (1,)), ((), ())), preferred_element_...]
    pallas_call x0 -> x4, Pallas kernels: none -> 13.4 us  [the longest x2 9.64 us: expert_call(): got = call(mine, theirs, *pieces, *sums)]
    ppermute x16, starting transfers between devices: 65.5 us -> 54.9 us  [swap_z(): return lax.ppermute(rows, 'z', pairs)]
    ppermute x16, waiting for transfers between devices: 36.4 us -> 45.9 us  [swap_z(): return lax.ppermute(rows, 'z', pairs)]
    ppermute x4, waiting for transfers between devices: 9.82 us -> 4.42 us  [swap(): return lax.ppermute(rows, axis, [(0, 1), (1, 0)])]
    all_to_all x2, starting transfers between devices: 17.7 us -> 12.4 us  [the longest x1 6.22 us: shards(): mine = lax.all_to_all(send, ('x', 'yl'), 0, 0, tiled=True)]
    slice x13 -> x3, local copies, waits for them, and re-layouts: 4.41 us -> 0.06 us  [the longest x2 0.04 us: sum_z(): return add(first[:1], swap_z(first[1:].astype(BF16), parity))]
    ppermute x4, starting transfers between devices: 13.5 us -> 16.6 us  [swap(): return lax.ppermute(rows, axis, [(0, 1), (1, 0)])]
  transfers between devices with their start and end apart: 22 -> 22, of which waited for: 11 -> 13; matrix products, arithmetic and copies ran while one was open for 8% -> 1% of each run, Pallas kernels for 0% -> 6%
where the time goes in v2:
time: 156 us; the launch traced here: 155 us
  starting transfers between devices  83.9 us (54%)
  waiting for transfers between devices  50.4 us (32%)
  Pallas kernels  13.4 us (9%)
  local copies, waits for them, and re-layouts  3.93 us (3%)
  other arithmetic  2.78 us (2%)
    ppermute x16, starting transfers between devices, swap_z(): return lax.ppermute(rows, 'z', pairs)  54.9 us
    ppermute x16, waiting for transfers between devices, swap_z(): return lax.ppermute(rows, 'z', pairs)  45.9 us
    ppermute x4, starting transfers between devices, swap(): return lax.ppermute(rows, axis, [(0, 1), (1, 0)])  16.6 us
    pallas_call x2, Pallas kernels, expert_call(): got = call(mine, theirs, *pieces, *sums)  9.64 us
    all_to_all x1, starting transfers between devices, shards(): mine = lax.all_to_all(send, ('x', 'yl'), 0, 0, tiled=True)  6.22 us
    all_to_all x1, starting transfers between devices, shards(): lax.all_to_all(add(local, swap(rest, 'core')).astype(BF16), ('x', 'yl'),...  6.14 us
    ppermute x4, waiting for transfers between devices, swap(): return lax.ppermute(rows, axis, [(0, 1), (1, 0)])  4.42 us
    unnamed x16, local copies, waits for them, and re-layouts  3.85 us
  transfers between devices with their start and end apart: 22, of which 13 were waited for; matrix products, arithmetic and copies ran while one was open for 1% of the time, Pallas kernels for 6%

profile of v2, /device:TPU:2, one launch (start us, length us, event | category | flops | bytes accessed | tf_op | source)
XLA Modules:
  0.0 155.4 jit_solution(12175886654931426925)
XLA Ops:
  1.5 7.7 %collective-permute-start = (bf16[1,3,48,512]{3,2,1,0:T(8,128)(2,1)S(1)}, bf16[1,3,48,512]{3,2,1,0:T(8,128)(2,1)S(1)}, u32[]{:S(2)}, u32[]{:S(2)}) collective-permute-start(bf16[1,3,48,512]{3,2,1,0:T(8,128)(2,1)S(1)} %fusion.7), channel_id=1, source_target_pairs={{0,32},{32,0},{1,33},{33,1},{2,34},{34,2},{3,35},{35,3},{4,36},{36... | collective-permute-start | bytes 442376 | tf_op jit(solution)/shard_map/ppermute | solution.py:23
  9.2 4.3 %collective-permute-start.1 = (bf16[1,3,48,512]{3,2,1,0:T(8,128)(2,1)S(1)}, bf16[1,3,48,512]{3,2,1,0:T(8,128)(2,1)S(1)}, u32[]{:S(2)}, u32[]{:S(2)}) collective-permute-start(bf16[1,3,48,512]{3,2,1,0:T(8,128)(2,1)S(1)} %fusion.7), channel_id=1, source_target_pairs={{0,64},{64,0},{128,192},{192,128},{256,320},{320,256},{384,448},{4... | collective-permute-start | bytes 442376 | tf_op jit(solution)/shard_map/ppermute | solution.py:19
  13.5 2.6 %shard_map.118 = (bf16[16,64,512]{2,1,0:T(8,128)(2,1)}, bf16[512,128]{1,0:T(8,128)(2,1)}, bf16[512,128]{1,0:T(8,128)(2,1)}) custom-call(bf16[128,512]{1,0:T(8,128)(2,1)} %latent.1, bf16[128,512]{1,0:T(8,128)(2,1)} %cotangent.3, s32[2,128]{1,0:T(2,128)} %bitcast.13, f32[2,128]{1,0:T(2,128)} %bitcast.11), custom_call_target="tpu_custom_call" | custom-call | bytes 1048576 | tf_op jit(solution)/shard_map/pallas_call | solution.py:186
  17.1 6.2 %all-to-all-start = ((bf16[16,64,512]{2,1,0:T(8,128)(2,1)}), bf16[16,64,512]{2,1,0:T(8,128)(2,1)S(1)}, u32[]{:S(2)}, u32[]{:S(2)}) async-start(bf16[16,64,512]{2,1,0:T(8,128)(2,1)} %get-tuple-element.42), calls=%async_computation | async-start | bytes 2097152 | tf_op jit(solution)/shard_map/all_to_all | solution.py:194
  23.3 10.9 %collective-permute-start.2 = (bf16[2,3,48,512]{3,2,1,0:T(8,128)(2,1)S(1)}, bf16[2,3,48,512]{3,2,1,0:T(8,128)(2,1)S(1)}, u32[]{:S(2)}, u32[]{:S(2)}) collective-permute-start(bf16[2,3,48,512]{3,2,1,0:T(8,128)(2,1)S(1)} %pad_maximum_fusion.refs_2_), channel_id=1, source_target_pairs={{0,448},{64,128},{128,64},{192,256},{256,192},{320,384},{384,320},... | collective-permute-start | bytes 884744 | tf_op jit(solution)/shard_map/ppermute | solution.py:19
  36.2 5.1 %collective-permute-done.3 = bf16[1,3,48,512]{3,2,1,0:T(8,128)(2,1)S(1)} collective-permute-done((bf16[1,3,48,512]{3,2,1,0:T(8,128)(2,1)S(1)}, bf16[1,3,48,512]{3,2,1,0:T(8,128)(2,1)S(1)}, u32[]{:S(2)}, u32[]{:S(2)}) %collective-permute-start.3) | collective-permute-done | bytes 147488 | tf_op jit(solution)/shard_map/ppermute | solution.py:19
  41.3 4.0 %collective-permute-start.5 = (bf16[2,3,48,512]{3,2,1,0:T(8,128)(2,1)S(1)}, bf16[2,3,48,512]{3,2,1,0:T(8,128)(2,1)S(1)}, u32[]{:S(2)}, u32[]{:S(2)}) collective-permute-start(bf16[2,3,48,512]{3,2,1,0:T(8,128)(2,1)S(1)} %constant_dynamic-update-slice_fusion.refs_2_), channel_id=1, source_target_pairs={{0,448},{64,128},{128,64},{192,256},{256,192},{320,384},{384,320},... | collective-permute-start | bytes 884744 | tf_op jit(solution)/shard_map/ppermute | solution.py:19
  47.3 4.0 %collective-permute-done.5.refs_3_ = bf16[2,3,48,512]{3,2,1,0:T(8,128)(2,1)S(1)} collective-permute-done((bf16[2,3,48,512]{3,2,1,0:T(8,128)(2,1)S(1)}, bf16[2,3,48,512]{3,2,1,0:T(8,128)(2,1)S(1)}, u32[]{:S(2)}, u32[]{:S(2)}) %collective-permute-start.5) | collective-permute-done | bytes 294944 | tf_op jit(solution)/shard_map/ppermute | solution.py:19
  51.3 2.7 %collective-permute-done.4.refs_4_ = bf16[2,3,48,512]{3,2,1,0:T(8,128)(2,1)S(1)} collective-permute-done((bf16[2,3,48,512]{3,2,1,0:T(8,128)(2,1)S(1)}, bf16[2,3,48,512]{3,2,1,0:T(8,128)(2,1)S(1)}, u32[]{:S(2)}, u32[]{:S(2)}) %collective-permute-start.4) | collective-permute-done | bytes 294944 | tf_op jit(solution)/shard_map/ppermute | solution.py:19
  55.9 5.2 %collective-permute-start.6 = (bf16[2,3,48,512]{3,2,1,0:T(8,128)(2,1)S(1)}, bf16[2,3,48,512]{3,2,1,0:T(8,128)(2,1)S(1)}, u32[]{:S(2)}, u32[]{:S(2)}) collective-permute-start(bf16[2,3,48,512]{3,2,1,0:T(8,128)(2,1)S(1)} %collective-permute-done.4.refs_4_), channel_id=1, source_target_pairs={{0,448},{64,128},{128,64},{192,256},{256,192},{320,384},{384,320},... | collective-permute-start | bytes 884744 | tf_op jit(solution)/shard_map/ppermute | solution.py:19
  63.8 5.0 %collective-permute-done.6.refs_5_ = bf16[2,3,48,512]{3,2,1,0:T(8,128)(2,1)S(1)} collective-permute-done((bf16[2,3,48,512]{3,2,1,0:T(8,128)(2,1)S(1)}, bf16[2,3,48,512]{3,2,1,0:T(8,128)(2,1)S(1)}, u32[]{:S(2)}, u32[]{:S(2)}) %collective-permute-start.6) | collective-permute-done | bytes 294944 | tf_op jit(solution)/shard_map/ppermute | solution.py:19
  68.8 4.1 %collective-permute-done.7.refs_4_ = bf16[2,3,48,512]{3,2,1,0:T(8,128)(2,1)S(1)} collective-permute-done((bf16[2,3,48,512]{3,2,1,0:T(8,128)(2,1)S(1)}, bf16[2,3,48,512]{3,2,1,0:T(8,128)(2,1)S(1)}, u32[]{:S(2)}, u32[]{:S(2)}) %collective-permute-start.7) | collective-permute-done | bytes 294944 | tf_op jit(solution)/shard_map/ppermute | solution.py:19
  76.0 4.8 %shard_map.119 = (bf16[2,3,48,512]{3,2,1,0:T(8,128)(2,1)S(1)}, bf16[2,3,48,512]{3,2,1,0:T(8,128)(2,1)S(1)}, bf16[2,3,48,512]{3,2,1,0:T(8,128)(2,1)S(1)}, bf16[2,...) custom-call(bf16[16,64,512]{2,1,0:T(8,128)(2,1)S(1)} %all-to-all-done.refs_0_, ...), custom_call_target="tpu_custom_call" | custom-call | flops 3623878656 | bytes 1048576 | tf_op jit(solution)/shard_map/pallas_call | solution.py:168
  80.8 3.4 %collective-permute-done.9.refs_5_ = bf16[2,3,48,512]{3,2,1,0:T(8,128)(2,1)S(1)} collective-permute-done((bf16[2,3,48,512]{3,2,1,0:T(8,128)(2,1)S(1)}, bf16[2,3,48,512]{3,2,1,0:T(8,128)(2,1)S(1)}, u32[]{:S(2)}, u32[]{:S(2)}) %collective-permute-start.9) | collective-permute-done | bytes 294944 | tf_op jit(solution)/shard_map/ppermute | solution.py:19
  84.3 4.8 %shard_map.120 = (bf16[2,3,48,512]{3,2,1,0:T(8,128)(2,1)S(1)}, bf16[2,3,48,512]{3,2,1,0:T(8,128)(2,1)S(1)}, bf16[2,3,48,512]{3,2,1,0:T(8,128)(2,1)S(1)}, bf16[2,...) custom-call(bf16[16,64,512]{2,1,0:T(8,128)(2,1)S(1)} %all-to-all-done.refs_0_, ...), custom_call_target="tpu_custom_call" | custom-call | flops 3623878656 | bytes 1048576 | tf_op jit(solution)/shard_map/pallas_call | solution.py:168
  93.5 10.0 %collective-permute-done.10 = bf16[2,3,48,512]{3,2,1,0:T(8,128)(2,1)S(1)} collective-permute-done((bf16[2,3,48,512]{3,2,1,0:T(8,128)(2,1)S(1)}, bf16[2,3,48,512]{3,2,1,0:T(8,128)(2,1)S(1)}, u32[]{:S(2)}, u32[]{:S(2)}) %collective-permute-start.10) | collective-permute-done | bytes 294944 | tf_op jit(solution)/shard_map/ppermute | solution.py:19
  106.9 6.1 %all-to-all-start.1 = ((bf16[16,64,512]{2,1,0:T(8,128)(2,1)}), bf16[16,64,512]{2,1,0:T(8,128)(2,1)S(1)}, u32[]{:S(2)}, u32[]{:S(2)}) async-start(bf16[16,64,512]{2,1,0:T(8,128)(2,1)} %add_convert_fusion), calls=%async_computation.1 | async-start | bytes 2097152 | tf_op jit(solution)/shard_map/all_to_all | solution.py:214
  113.0 3.2 %collective-permute-start.16 = (bf16[2,3,48,512]{3,2,1,0:T(8,128)(2,1)S(1)}, bf16[2,3,48,512]{3,2,1,0:T(8,128)(2,1)S(1)}, u32[]{:S(2)}, u32[]{:S(2)}) collective-permute-start(bf16[2,3,48,512]{3,2,1,0:T(8,128)(2,1)S(1)} %get-tuple-element.66), channel_id=1, source_target_pairs={{0,448},{64,128},{128,64},{192,256},{256,192},{320,384},{384,320},... | collective-permute-start | bytes 884744 | tf_op jit(solution)/shard_map/ppermute | solution.py:19
  116.4 3.8 %collective-permute-start.12 = (bf16[2,3,48,512]{3,2,1,0:T(8,128)(2,1)S(1)}, bf16[2,3,48,512]{3,2,1,0:T(8,128)(2,1)S(1)}, u32[]{:S(2)}, u32[]{:S(2)}) collective-permute-start(bf16[2,3,48,512]{3,2,1,0:T(8,128)(2,1)S(1)} %add_convert_fusion.3), channel_id=1, source_target_pairs={{0,448},{64,128},{128,64},{192,256},{256,192},{320,384},{384,320},... | collective-permute-start | bytes 884744 | tf_op jit(solution)/shard_map/ppermute | solution.py:19
  120.2 5.9 %collective-permute-done.16 = bf16[2,3,48,512]{3,2,1,0:T(8,128)(2,1)S(1)} collective-permute-done((bf16[2,3,48,512]{3,2,1,0:T(8,128)(2,1)S(1)}, bf16[2,3,48,512]{3,2,1,0:T(8,128)(2,1)S(1)}, u32[]{:S(2)}, u32[]{:S(2)}) %collective-permute-start.16) | collective-permute-done | bytes 294944 | tf_op jit(solution)/shard_map/ppermute | solution.py:19
  126.2 2.7 %collective-permute-start.17 = (bf16[2,3,48,512]{3,2,1,0:T(8,128)(2,1)S(1)}, bf16[2,3,48,512]{3,2,1,0:T(8,128)(2,1)S(1)}, u32[]{:S(2)}, u32[]{:S(2)}) collective-permute-start(bf16[2,3,48,512]{3,2,1,0:T(8,128)(2,1)S(1)} %add_convert_fusion.2), channel_id=1, source_target_pairs={{0,64},{64,0},{128,192},{192,128},{256,320},{320,256},{384,448},{4... | collective-permute-start | bytes 884744 | tf_op jit(solution)/shard_map/ppermute | solution.py:19
  135.5 3.8 %collective-permute-start.18 = (bf16[2,3,48,512]{3,2,1,0:T(8,128)(2,1)S(1)}, bf16[2,3,48,512]{3,2,1,0:T(8,128)(2,1)S(1)}, u32[]{:S(2)}, u32[]{:S(2)}) collective-permute-start(bf16[2,3,48,512]{3,2,1,0:T(8,128)(2,1)S(1)} %add_convert_fusion.1), channel_id=1, source_target_pairs={{0,448},{64,128},{128,64},{192,256},{256,192},{320,384},{384,320},... | collective-permute-start | bytes 884744 | tf_op jit(solution)/shard_map/ppermute | solution.py:19
  139.4 5.1 %collective-permute-start.14 = (bf16[1,3,48,512]{3,2,1,0:T(8,128)(2,1)S(1)}, bf16[1,3,48,512]{3,2,1,0:T(8,128)(2,1)S(1)}, u32[]{:S(2)}, u32[]{:S(2)}) collective-permute-start(bf16[1,3,48,512]{3,2,1,0:T(8,128)(2,1)S(1)} %fusion.1), channel_id=1, source_target_pairs={{0,32},{32,0},{1,33},{33,1},{2,34},{34,2},{3,35},{35,3},{4,36},{36... | collective-permute-start | bytes 442376 | tf_op jit(solution)/shard_map/ppermute | solution.py:23
  148.7 4.4 %collective-permute-done.14 = bf16[1,3,48,512]{3,2,1,0:T(8,128)(2,1)S(1)} collective-permute-done((bf16[1,3,48,512]{3,2,1,0:T(8,128)(2,1)S(1)}, bf16[1,3,48,512]{3,2,1,0:T(8,128)(2,1)S(1)}, u32[]{:S(2)}, u32[]{:S(2)}) %collective-permute-start.14) | collective-permute-done | bytes 147488 | tf_op jit(solution)/shard_map/ppermute | solution.py:23
  (55 shorter events, 34.4 us)
Async XLA Ops:
  1.5 14.6 %collective-permute-start = (bf16[1,3,48,512]{3,2,1,0:T(8,128)(2,1)S(1)}, bf16[1,3,48,512]{3,2,1,0:T(8,128)(2,1)S(1)}, u32[]{:S(2)}, u32[]{:S(2)}) collective-permute-start(bf16[1,3,48,512]{3,2,1,0:T(8,128)(2,1)S(1)} %fusion.7), channel_id=1, source_target_pairs={{0,32},{32,0},{1,33},{33,1},{2,34},{34,2},{3,35},{35,3},{4,36},{36... | collective-permute-start | bytes 442376 | tf_op jit(solution)/shard_map/ppermute | solution.py:23
  9.2 7.8 %collective-permute-start.1 = (bf16[1,3,48,512]{3,2,1,0:T(8,128)(2,1)S(1)}, bf16[1,3,48,512]{3,2,1,0:T(8,128)(2,1)S(1)}, u32[]{:S(2)}, u32[]{:S(2)}) collective-permute-start(bf16[1,3,48,512]{3,2,1,0:T(8,128)(2,1)S(1)} %fusion.7), channel_id=1, source_target_pairs={{0,64},{64,0},{128,192},{192,128},{256,320},{320,256},{384,448},{4... | collective-permute-start | bytes 442376 | tf_op jit(solution)/shard_map/ppermute | solution.py:19
  17.1 36.9 %all-to-all-start = ((bf16[16,64,512]{2,1,0:T(8,128)(2,1)}), bf16[16,64,512]{2,1,0:T(8,128)(2,1)S(1)}, u32[]{:S(2)}, u32[]{:S(2)}) async-start(bf16[16,64,512]{2,1,0:T(8,128)(2,1)} %get-tuple-element.42), calls=%async_computation | async-start | bytes 2097152 | tf_op jit(solution)/shard_map/all_to_all | solution.py:194
  23.3 18.0 %collective-permute-start.2 = (bf16[2,3,48,512]{3,2,1,0:T(8,128)(2,1)S(1)}, bf16[2,3,48,512]{3,2,1,0:T(8,128)(2,1)S(1)}, u32[]{:S(2)}, u32[]{:S(2)}) collective-permute-start(bf16[2,3,48,512]{3,2,1,0:T(8,128)(2,1)S(1)} %pad_maximum_fusion.refs_2_), channel_id=1, source_target_pairs={{0,448},{64,128},{128,64},{192,256},{256,192},{320,384},{384,320},... | collective-permute-start | bytes 884744 | tf_op jit(solution)/shard_map/ppermute | solution.py:19
  34.3 7.0 %collective-permute-start.3 = (bf16[1,3,48,512]{3,2,1,0:T(8,128)(2,1)S(1)}, bf16[1,3,48,512]{3,2,1,0:T(8,128)(2,1)S(1)}, u32[]{:S(2)}, u32[]{:S(2)}) collective-permute-start(bf16[1,3,48,512]{3,2,1,0:T(8,128)(2,1)S(1)} %collective-permute-done), channel_id=1, source_target_pairs={{0,64},{64,0},{128,192},{192,128},{256,320},{320,256},{384,448},{4... | collective-permute-start | bytes 442376 | tf_op jit(solution)/shard_map/ppermute | solution.py:19
  41.3 9.9 %collective-permute-start.5 = (bf16[2,3,48,512]{3,2,1,0:T(8,128)(2,1)S(1)}, bf16[2,3,48,512]{3,2,1,0:T(8,128)(2,1)S(1)}, u32[]{:S(2)}, u32[]{:S(2)}) collective-permute-start(bf16[2,3,48,512]{3,2,1,0:T(8,128)(2,1)S(1)} %constant_dynamic-update-slice_fusion.refs_2_), channel_id=1, source_target_pairs={{0,448},{64,128},{128,64},{192,256},{256,192},{320,384},{384,320},... | collective-permute-start | bytes 884744 | tf_op jit(solution)/shard_map/ppermute | solution.py:19
  45.4 8.7 %collective-permute-start.4 = (bf16[2,3,48,512]{3,2,1,0:T(8,128)(2,1)S(1)}, bf16[2,3,48,512]{3,2,1,0:T(8,128)(2,1)S(1)}, u32[]{:S(2)}, u32[]{:S(2)}) collective-permute-start(bf16[2,3,48,512]{3,2,1,0:T(8,128)(2,1)S(1)} %collective-permute-done.2.refs_3_), channel_id=1, source_target_pairs={{0,64},{64,0},{128,192},{192,128},{256,320},{320,256},{384,448},{4... | collective-permute-start | bytes 884744 | tf_op jit(solution)/shard_map/ppermute | solution.py:19
  54.0 18.8 %collective-permute-start.8 = (bf16[16,64,512]{2,1,0:T(8,128)(2,1)S(1)}, bf16[16,64,512]{2,1,0:T(8,128)(2,1)S(1)}, u32[]{:S(2)}, u32[]{:S(2)}) collective-permute-start(bf16[16,64,512]{2,1,0:T(8,128)(2,1)S(1)} %all-to-all-done.refs_0_), channel_id=1, source_target_pairs={{0,16},{16,0},{1,17},{17,1},{2,18},{18,2},{3,19},{19,3},{4,20},{20... | collective-permute-start | bytes 3145736 | tf_op jit(solution)/shard_map/ppermute | solution.py:23
  55.9 12.9 %collective-permute-start.6 = (bf16[2,3,48,512]{3,2,1,0:T(8,128)(2,1)S(1)}, bf16[2,3,48,512]{3,2,1,0:T(8,128)(2,1)S(1)}, u32[]{:S(2)}, u32[]{:S(2)}) collective-permute-start(bf16[2,3,48,512]{3,2,1,0:T(8,128)(2,1)S(1)} %collective-permute-done.4.refs_4_), channel_id=1, source_target_pairs={{0,448},{64,128},{128,64},{192,256},{256,192},{320,384},{384,320},... | collective-permute-start | bytes 884744 | tf_op jit(solution)/shard_map/ppermute | solution.py:19
  61.8 11.0 %collective-permute-start.7 = (bf16[2,3,48,512]{3,2,1,0:T(8,128)(2,1)S(1)}, bf16[2,3,48,512]{3,2,1,0:T(8,128)(2,1)S(1)}, u32[]{:S(2)}, u32[]{:S(2)}) collective-permute-start(bf16[2,3,48,512]{3,2,1,0:T(8,128)(2,1)S(1)} %collective-permute-done.5.refs_3_), channel_id=1, source_target_pairs={{0,64},{64,0},{128,192},{192,128},{256,320},{320,256},{384,448},{4... | collective-permute-start | bytes 884744 | tf_op jit(solution)/shard_map/ppermute | solution.py:19
  72.9 11.4 %collective-permute-start.9 = (bf16[2,3,48,512]{3,2,1,0:T(8,128)(2,1)S(1)}, bf16[2,3,48,512]{3,2,1,0:T(8,128)(2,1)S(1)}, u32[]{:S(2)}, u32[]{:S(2)}) collective-permute-start(bf16[2,3,48,512]{3,2,1,0:T(8,128)(2,1)S(1)} %collective-permute-done.7.refs_4_), channel_id=1, source_target_pairs={{0,448},{64,128},{128,64},{192,256},{256,192},{320,384},{384,320},... | collective-permute-start | bytes 884744 | tf_op jit(solution)/shard_map/ppermute | solution.py:19
  89.1 16.5 %collective-permute-start.15 = (bf16[16,64,512]{2,1,0:T(8,128)(2,1)S(1)}, bf16[16,64,512]{2,1,0:T(8,128)(2,1)S(1)}, u32[]{:S(2)}, u32[]{:S(2)}) collective-permute-start(bf16[16,64,512]{2,1,0:T(8,128)(2,1)S(1)} %get-tuple-element.56), channel_id=1, source_target_pairs={{0,16},{16,0},{1,17},{17,1},{2,18},{18,2},{3,19},{19,3},{4,20},{20... | collective-permute-start | bytes 3145736 | tf_op jit(solution)/shard_map/ppermute | solution.py:23
  91.0 12.5 %collective-permute-start.10 = (bf16[2,3,48,512]{3,2,1,0:T(8,128)(2,1)S(1)}, bf16[2,3,48,512]{3,2,1,0:T(8,128)(2,1)S(1)}, u32[]{:S(2)}, u32[]{:S(2)}) collective-permute-start(bf16[2,3,48,512]{3,2,1,0:T(8,128)(2,1)S(1)} %get-tuple-element.54), channel_id=1, source_target_pairs={{0,448},{64,128},{128,64},{192,256},{256,192},{320,384},{384,320},... | collective-permute-start | bytes 884744 | tf_op jit(solution)/shard_map/ppermute | solution.py:19
  103.6 12.7 %collective-permute-start.11 = (bf16[2,3,48,512]{3,2,1,0:T(8,128)(2,1)S(1)}, bf16[2,3,48,512]{3,2,1,0:T(8,128)(2,1)S(1)}, u32[]{:S(2)}, u32[]{:S(2)}) collective-permute-start(bf16[2,3,48,512]{3,2,1,0:T(8,128)(2,1)S(1)} %add_convert_fusion.4), channel_id=1, source_target_pairs={{0,64},{64,0},{128,192},{192,128},{256,320},{320,256},{384,448},{4... | collective-permute-start | bytes 884744 | tf_op jit(solution)/shard_map/ppermute | solution.py:19
  106.9 40.6 %all-to-all-start.1 = ((bf16[16,64,512]{2,1,0:T(8,128)(2,1)}), bf16[16,64,512]{2,1,0:T(8,128)(2,1)S(1)}, u32[]{:S(2)}, u32[]{:S(2)}) async-start(bf16[16,64,512]{2,1,0:T(8,128)(2,1)} %add_convert_fusion), calls=%async_computation.1 | async-start | bytes 2097152 | tf_op jit(solution)/shard_map/all_to_all | solution.py:214
  113.0 13.0 %collective-permute-start.16 = (bf16[2,3,48,512]{3,2,1,0:T(8,128)(2,1)S(1)}, bf16[2,3,48,512]{3,2,1,0:T(8,128)(2,1)S(1)}, u32[]{:S(2)}, u32[]{:S(2)}) collective-permute-start(bf16[2,3,48,512]{3,2,1,0:T(8,128)(2,1)S(1)} %get-tuple-element.66), channel_id=1, source_target_pairs={{0,448},{64,128},{128,64},{192,256},{256,192},{320,384},{384,320},... | collective-permute-start | bytes 884744 | tf_op jit(solution)/shard_map/ppermute | solution.py:19
  116.4 14.4 %collective-permute-start.12 = (bf16[2,3,48,512]{3,2,1,0:T(8,128)(2,1)S(1)}, bf16[2,3,48,512]{3,2,1,0:T(8,128)(2,1)S(1)}, u32[]{:S(2)}, u32[]{:S(2)}) collective-permute-start(bf16[2,3,48,512]{3,2,1,0:T(8,128)(2,1)S(1)} %add_convert_fusion.3), channel_id=1, source_target_pairs={{0,448},{64,128},{128,64},{192,256},{256,192},{320,384},{384,320},... | collective-permute-start | bytes 884744 | tf_op jit(solution)/shard_map/ppermute | solution.py:19
  126.2 9.3 %collective-permute-start.17 = (bf16[2,3,48,512]{3,2,1,0:T(8,128)(2,1)S(1)}, bf16[2,3,48,512]{3,2,1,0:T(8,128)(2,1)S(1)}, u32[]{:S(2)}, u32[]{:S(2)}) collective-permute-start(bf16[2,3,48,512]{3,2,1,0:T(8,128)(2,1)S(1)} %add_convert_fusion.2), channel_id=1, source_target_pairs={{0,64},{64,0},{128,192},{192,128},{256,320},{320,256},{384,448},{4... | collective-permute-start | bytes 884744 | tf_op jit(solution)/shard_map/ppermute | solution.py:19
  130.8 16.7 %copy-start.2 = (bf16[512,128]{1,0:T(8,128)(2,1)S(1)}, bf16[512,128]{1,0:T(8,128)(2,1)}, u32[]{:S(2)}) copy-start(bf16[512,128]{1,0:T(8,128)(2,1)} %get-tuple-element.58.second) | copy-start | bytes 393220
  130.8 16.7 %copy-start.3 = (f32[128,2]{0,1:T(2,128)S(1)}, f32[128,2]{0,1:T(2,128)}, u32[]{:S(2)}) copy-start(f32[128,2]{0,1:T(2,128)} %param.9) | copy-start | bytes 3076
  130.9 8.4 %collective-permute-start.13 = (bf16[1,3,48,512]{3,2,1,0:T(8,128)(2,1)S(1)}, bf16[1,3,48,512]{3,2,1,0:T(8,128)(2,1)S(1)}, u32[]{:S(2)}, u32[]{:S(2)}) collective-permute-start(bf16[1,3,48,512]{3,2,1,0:T(8,128)(2,1)S(1)} %slice.65), channel_id=1, source_target_pairs={{0,64},{64,0},{128,192},{192,128},{256,320},{320,256},{384,448},{4... | collective-permute-start | bytes 442376 | tf_op jit(solution)/shard_map/ppermute | solution.py:19
  135.5 9.8 %collective-permute-start.18 = (bf16[2,3,48,512]{3,2,1,0:T(8,128)(2,1)S(1)}, bf16[2,3,48,512]{3,2,1,0:T(8,128)(2,1)S(1)}, u32[]{:S(2)}, u32[]{:S(2)}) collective-permute-start(bf16[2,3,48,512]{3,2,1,0:T(8,128)(2,1)S(1)} %add_convert_fusion.1), channel_id=1, source_target_pairs={{0,448},{64,128},{128,64},{192,256},{256,192},{320,384},{384,320},... | collective-permute-start | bytes 884744 | tf_op jit(solution)/shard_map/ppermute | solution.py:19
  139.4 13.8 %collective-permute-start.14 = (bf16[1,3,48,512]{3,2,1,0:T(8,128)(2,1)S(1)}, bf16[1,3,48,512]{3,2,1,0:T(8,128)(2,1)S(1)}, u32[]{:S(2)}, u32[]{:S(2)}) collective-permute-start(bf16[1,3,48,512]{3,2,1,0:T(8,128)(2,1)S(1)} %fusion.1), channel_id=1, source_target_pairs={{0,32},{32,0},{1,33},{33,1},{2,34},{34,2},{3,35},{35,3},{4,36},{36... | collective-permute-start | bytes 442376 | tf_op jit(solution)/shard_map/ppermute | solution.py:23
  145.5 7.7 %collective-permute-start.19 = (bf16[1,3,48,512]{3,2,1,0:T(8,128)(2,1)S(1)}, bf16[1,3,48,512]{3,2,1,0:T(8,128)(2,1)S(1)}, u32[]{:S(2)}, u32[]{:S(2)}) collective-permute-start(bf16[1,3,48,512]{3,2,1,0:T(8,128)(2,1)S(1)} %slice.64), channel_id=1, source_target_pairs={{0,64},{64,0},{128,192},{192,128},{256,320},{320,256},{384,448},{4... | collective-permute-start | bytes 442376 | tf_op jit(solution)/shard_map/ppermute | solution.py:19
  (4 other events, 35.0 us)

commit v3 on v2

--- a/solution.py
+++ b/solution.py
@@ -100,21 +100,23 @@
     latent_grad[...] = dot(merged, tokens, (0, 0)).astype(BF16)
 
 
-def expert_body(capacity, last, *refs):
+def expert_body(capacity, count, more, *refs):
     mine, theirs = refs[:2]
-    pieces = refs[2:6]
-    refs = refs[6:]
-    if last:
+    pieces = refs[2 : 2 + count]
+    refs = refs[2 + count :]
+    if more:
         sums, refs = refs[:2], refs[2:]
-    grads = refs[:4]
-    results = refs[4:6]
-    wg, wu, wd, xs, gs, hs, gbs, ubs = refs[6:]
+    grads = refs[:count]
+    results = refs[count : count + 2]
+    wg, wu, wd, xs, gs, hs, gbs, ubs = refs[count + 2 :]
     width = mine.shape[2]
+    own_rows = pieces[0].shape[1] // 3
     for i, piece in enumerate(pieces):
         for j in range(2):
-            block = slice((2 * i + j) * PAD, (2 * i + j + 1) * PAD)
+            start = (2 * i + j) * PAD
             for k, weight in enumerate((wg, wu, wd)):
-                weight[block, :] = piece[j, k]
+                weight[start : start + own_rows, :] = piece[j, k * own_rows : (k + 1) * own_rows, :]
+                weight[start + own_rows : start + PAD, :] = jnp.zeros((PAD - own_rows, width), BF16)
     sources = mine.shape[0] // 2
     tile = sources * capacity
     for i in range(4):
@@ -140,7 +142,7 @@
         back = dot(gate_back, wg[...], (1, 0)) + dot(up_back, wu[...], (1, 0))
         back = back.reshape(sources, capacity, width)
         result = results[i // 2]
-        if last:
+        if more:
             outs = outs + sums[i // 2][part, :capacity, :]
             back = back + sums[i // 2][part, capacity:, :]
         result[part, :capacity, :] = outs.astype(result.dtype)
@@ -149,24 +151,53 @@
         term = (dot(left[...], right[...], (0, 0)) * grad_scale).astype(BF16)
         for i, grad in enumerate(grads):
             for j in range(2):
-                grad[j, k] = term[(2 * i + j) * PAD : (2 * i + j + 1) * PAD, :]
-
-
-def expert_call(capacity, mine, theirs, pieces, sums=()):
-    last = len(sums) > 0
+                start = (2 * i + j) * PAD
+                grad[j, k * own_rows : (k + 1) * own_rows, :] = term[start : start + own_rows, :]
+
+
+def expert_call(capacity, mine, theirs, pieces, sums=(), last=False):
     both = mine.shape
     width = both[2]
     slots = both[0] * capacity * 2
-    hidden = 8 * PAD
+    count = len(pieces)
+    hidden = 2 * count * PAD
     outs = [jax.ShapeDtypeStruct(p.shape, BF16) for p in pieces]
     outs += [jax.ShapeDtypeStruct(both, F32), jax.ShapeDtypeStruct(both, BF16 if last else F32)]
     scratch = [pltpu.VMEM((hidden, width), BF16)] * 3 + [pltpu.VMEM((slots, width), BF16)] * 2
     scratch += [pltpu.VMEM((slots, hidden), BF16)] * 3
-    call = kernel_call(
-        functools.partial(expert_body, capacity, last), outs, scratch, 18 * slots * hidden * width
-    )
+    body = functools.partial(expert_body, capacity, count, len(sums) > 0)
+    call = kernel_call(body, outs, scratch, 18 * slots * hidden * width)
     got = call(mine, theirs, *pieces, *sums)
-    return got[:4], got[4:]
+    return got[:count], got[count:]
+
+
+def pair_body(one, two, out):
+    out[0:1] = one[...]
+    out[1:2] = two[...]
+
+
+def pair(one, two, flops=0):
+    out = jax.ShapeDtypeStruct((2,) + one.shape[1:], one.dtype)
+    return kernel_call(pair_body, out, flops=flops, grant=16)(one, two)
+
+
+def total_body(one, two, out):
+    out[...] = (one[...].astype(F32) + two[...].astype(F32)).astype(out.dtype)
+
+
+def total(one, two, dtype, flops=0):
+    out = jax.ShapeDtypeStruct(one.shape, dtype)
+    return kernel_call(total_body, out, flops=flops, grant=16)(one, two)
+
+
+def finish_body(near, far, *outs):
+    value = near[0] + far[0].astype(F32)
+    rows = value.shape[0] // 3
+    for k, out in enumerate(outs):
+        for j in range(value.shape[1] // 128):
+            out[pl.ds(j, rows, stride=value.shape[1] // 128), :] = value[
+                k * rows : (k + 1) * rows, j * 128 : (j + 1) * 128
+            ]
 
 
 def shards(latent, routes, scores, cotangent, w_gate, w_up, w_down):
@@ -175,11 +206,10 @@
     capacity = 4 * tok_rows // experts
     slots = experts * capacity
     hidden_rows = w_gate.shape[1]
-    own = jnp.pad(
-        jnp.stack([w_gate[0], w_up[0], w_down[0]]), ((0, 0), (0, PAD - hidden_rows), (0, 0))
-    )[None]
+    own = jnp.concatenate([w_gate[0], w_up[0], w_down[0]], axis=0)[None]
     other = swap(own, "yh")
 
+    near_got = swap_z(own, 0)
     shape = (experts, 2 * capacity, width)
     table = jax.ShapeDtypeStruct((slots, tok_rows), BF16)
     score_rows = scores.T
@@ -189,31 +219,41 @@
         grant=56,
     )(latent, cotangent, routes.T, score_rows)
 
-    near_got = swap_z(own, 0)
     other, near_got, send = together((other, near_got, send))
     mine = lax.all_to_all(send, ("x", "yl"), 0, 0, tiled=True)
     near = [jnp.concatenate([own, near_got], axis=0)]
     near.append(swap_z(near[0], 1))
     far_got = swap_z(other, 0)
     near[1], far_got = together((near[1], far_got))
-    far = [jnp.concatenate([other, far_got], axis=0)]
+    far = [pair(other, far_got, 4 * 10**10)]
     near.append(swap_z(near[1], 0))
     far.append(swap_z(far[0], 1))
-    near[2], far[1], mine = together((near[2], far[1], mine))
+    near[2], far[1] = together((near[2], far[1]))
     near.append(swap_z(near[2], 1))
     far.append(swap_z(far[1], 0))
+    near[3], far[2], mine = together((near[3], far[2], mine))
     theirs = swap(mine, "core")
-    near[3], far[2], theirs = together((near[3], far[2], theirs))
     far.append(swap_z(far[2], 1))
 
     near_terms, sums = expert_call(capacity, mine, theirs, near)
-    far_terms, (local, rest) = expert_call(capacity, mine, theirs, far, sums)
-
-    far_sum = sum_z(far_terms, 0).astype(BF16)
-    near_sum = sum_z(near_terms, 0)
-    back = lax.all_to_all(
-        add(local, swap(rest, "core")).astype(BF16), ("x", "yl"), 0, 0, tiled=True
-    )
+    early, sums = expert_call(capacity, mine, theirs, far[:3], sums)
+    late, (local, rest) = expert_call(capacity, mine, theirs, far[3:], sums, True)
+    far_terms = (*early, *late)
+
+    near_got = swap_z(near_terms[3], 1)
+    rest = swap(rest, "core")
+    near_sum = add(near_terms[2], near_got).astype(BF16)
+    near_got, got, rest = together((swap_z(near_sum, 0), swap_z(far_terms[3], 1), rest))
+    far_sum = add(far_terms[2], got).astype(BF16)
+    near_sum = add(near_terms[1], near_got).astype(BF16)
+    back = lax.all_to_all(add(local, rest).astype(BF16), ("x", "yl"), 0, 0, tiled=True)
+    near_got, got = together((swap_z(near_sum, 1), swap_z(far_sum, 0)))
+    far_sum = total(far_terms[1], got, BF16, 4 * 10**10)
+    near_sum = add(near_terms[0], near_got)
+    near_got, got = together((swap_z(near_sum[1:].astype(BF16), 0), swap_z(far_sum, 1)))
+    near_sum = add(near_sum[:1], near_got)
+    far_sum = add(far_terms[0], got)
+    far_sum = add(far_sum[:1], swap_z(far_sum[1:].astype(BF16), 0)).astype(BF16)
     got = swap(far_sum, "yh")
     row = jax.ShapeDtypeStruct((tok_rows, width), BF16)
     mixed, latent_grad, score_grad = kernel_call(
@@ -221,8 +261,11 @@
         [row, row, jax.ShapeDtypeStruct((2, tok_rows), F32)],
     )(back, first, second, score_rows, cotangent)
     got, mixed = together((got, mixed))
-    grads = (near_sum + got.astype(F32))[0, :, :hidden_rows]
-    return (mixed, latent_grad, score_grad.T, grads[0:1], grads[1:2], grads[2:3])
+    lanes = width // 128
+    block = jax.ShapeDtypeStruct((hidden_rows * lanes, 128), F32)
+    grads = kernel_call(finish_body, [block] * 3)(near_sum, got)
+    grads = [grad.reshape(1, hidden_rows, width) for grad in grads]
+    return (mixed, latent_grad, score_grad.T, *grads)
 
 
 def solution(mesh):

time: 156 us -> 147 us (0.942)
  the two profiles are of different devices: /device:TPU:2 before, /device:TPU:8 now
where the time goes in v3:
time: 147 us; the launch traced here: 146 us
  starting transfers between devices  86.5 us (59%)
  waiting for transfers between devices  39.2 us (27%)
  Pallas kernels  16.5 us (11%)
  other arithmetic  2.64 us (2%)
    ppermute x16, starting transfers between devices, swap_z(): return lax.ppermute(rows, 'z', pairs)  55.3 us
    ppermute x16, waiting for transfers between devices, swap_z(): return lax.ppermute(rows, 'z', pairs)  32.7 us
    ppermute x4, starting transfers between devices, swap(): return lax.ppermute(rows, axis, [(0, 1), (1, 0)])  16 us
    pallas_call x3, Pallas kernels, expert_call(): got = call(mine, theirs, *pieces, *sums)  11.9 us
    all_to_all x1, starting transfers between devices, shards(): mine = lax.all_to_all(send, ('x', 'yl'), 0, 0, tiled=True)  7.66 us
    all_to_all x1, starting transfers between devices, shards(): lax.all_to_all(add(local, rest).astype(BF16), ('x', 'yl'), 0, 0, tiled=True)  7.52 us
    ppermute x4, waiting for transfers between devices, swap(): return lax.ppermute(rows, axis, [(0, 1), (1, 0)])  4.71 us
  transfers between devices with their start and end apart: 22, of which 12 were waited for; matrix products, arithmetic and copies ran while one was open for 1% of the time, Pallas kernels for 9%

profile of v3, /device:TPU:8, one launch (start us, length us, event | category | flops | bytes accessed | tf_op | source)
XLA Modules:
  0.0 145.8 jit_solution(4064278576497704990)
XLA Ops:
  1.5 6.8 %collective-permute-start = (bf16[1,126,512]{2,1,0:T(8,128)(2,1)S(1)}, bf16[1,126,512]{2,1,0:T(8,128)(2,1)S(1)}, u32[]{:S(2)}, u32[]{:S(2)}) collective-permute-start(bf16[1,126,512]{2,1,0:T(8,128)(2,1)S(1)} %maximum_bitcast_fusion), channel_id=1, source_target_pairs={{0,32},{32,0},{1,33},{33,1},{2,34},{34,2},{3,35},{35,3},{4,36},{36... | collective-permute-start | bytes 387080 | tf_op jit(solution)/shard_map/ppermute | solution.py:23
  8.4 4.3 %collective-permute-start.1 = (bf16[1,126,512]{2,1,0:T(8,128)(2,1)S(1)}, bf16[1,126,512]{2,1,0:T(8,128)(2,1)S(1)}, u32[]{:S(2)}, u32[]{:S(2)}) collective-permute-start(bf16[1,126,512]{2,1,0:T(8,128)(2,1)S(1)} %maximum_bitcast_fusion), channel_id=1, source_target_pairs={{0,64},{64,0},{128,192},{192,128},{256,320},{320,256},{384,448},{4... | collective-permute-start | bytes 387080 | tf_op jit(solution)/shard_map/ppermute | solution.py:19
  15.9 10.3 %collective-permute-start.2 = (bf16[2,126,512]{2,1,0:T(8,128)(2,1)S(1)}, bf16[2,126,512]{2,1,0:T(8,128)(2,1)S(1)}, u32[]{:S(2)}, u32[]{:S(2)}) collective-permute-start(bf16[2,126,512]{2,1,0:T(8,128)(2,1)S(1)} %pad_maximum_fusion.refs_2_), channel_id=1, source_target_pairs={{0,448},{64,128},{128,64},{192,256},{256,192},{320,384},{384,320},... | collective-permute-start | bytes 774152 | tf_op jit(solution)/shard_map/ppermute | solution.py:19
  28.1 7.7 %all-to-all-start = ((bf16[16,64,512]{2,1,0:T(8,128)(2,1)}), bf16[16,64,512]{2,1,0:T(8,128)(2,1)S(1)}, u32[]{:S(2)}, u32[]{:S(2)}) async-start(bf16[16,64,512]{2,1,0:T(8,128)(2,1)} %get-tuple-element.55), calls=%async_computation | async-start | bytes 2097152 | tf_op jit(solution)/shard_map/all_to_all | solution.py:223
  35.8 3.0 %collective-permute-start.5 = (bf16[2,126,512]{2,1,0:T(8,128)(2,1)S(1)}, bf16[2,126,512]{2,1,0:T(8,128)(2,1)S(1)}, u32[]{:S(2)}, u32[]{:S(2)}) collective-permute-start(bf16[2,126,512]{2,1,0:T(8,128)(2,1)S(1)} %shard_map.119.refs_2_), channel_id=1, source_target_pairs={{0,448},{64,128},{128,64},{192,256},{256,192},{320,384},{384,320},... | collective-permute-start | bytes 774152 | tf_op jit(solution)/shard_map/ppermute | solution.py:19
  38.8 2.8 %collective-permute-start.4 = (bf16[2,126,512]{2,1,0:T(8,128)(2,1)S(1)}, bf16[2,126,512]{2,1,0:T(8,128)(2,1)S(1)}, u32[]{:S(2)}, u32[]{:S(2)}) collective-permute-start(bf16[2,126,512]{2,1,0:T(8,128)(2,1)S(1)} %collective-permute-done.2.refs_3_), channel_id=1, source_target_pairs={{0,64},{64,0},{128,192},{192,128},{256,320},{320,256},{384,448},{4... | collective-permute-start | bytes 774152 | tf_op jit(solution)/shard_map/ppermute | solution.py:19
  41.7 3.9 %collective-permute-done.5.refs_3_ = bf16[2,126,512]{2,1,0:T(8,128)(2,1)S(1)} collective-permute-done((bf16[2,126,512]{2,1,0:T(8,128)(2,1)S(1)}, bf16[2,126,512]{2,1,0:T(8,128)(2,1)S(1)}, u32[]{:S(2)}, u32[]{:S(2)}) %collective-permute-start.5) | collective-permute-done | bytes 258080 | tf_op jit(solution)/shard_map/ppermute | solution.py:19
  47.1 4.0 %collective-permute-start.6 = (bf16[2,126,512]{2,1,0:T(8,128)(2,1)S(1)}, bf16[2,126,512]{2,1,0:T(8,128)(2,1)S(1)}, u32[]{:S(2)}, u32[]{:S(2)}) collective-permute-start(bf16[2,126,512]{2,1,0:T(8,128)(2,1)S(1)} %collective-permute-done.4.refs_4_), channel_id=1, source_target_pairs={{0,448},{64,128},{128,64},{192,256},{256,192},{320,384},{384,320},... | collective-permute-start | bytes 774152 | tf_op jit(solution)/shard_map/ppermute | solution.py:19
  56.6 2.8 %collective-permute-done.7.refs_4_ = bf16[2,126,512]{2,1,0:T(8,128)(2,1)S(1)} collective-permute-done((bf16[2,126,512]{2,1,0:T(8,128)(2,1)S(1)}, bf16[2,126,512]{2,1,0:T(8,128)(2,1)S(1)}, u32[]{:S(2)}, u32[]{:S(2)}) %collective-permute-start.7) | collective-permute-done | bytes 258080 | tf_op jit(solution)/shard_map/ppermute | solution.py:19
  61.3 3.0 %collective-permute-start.11 = (bf16[2,126,512]{2,1,0:T(8,128)(2,1)S(1)}, bf16[2,126,512]{2,1,0:T(8,128)(2,1)S(1)}, u32[]{:S(2)}, u32[]{:S(2)}) collective-permute-start(bf16[2,126,512]{2,1,0:T(8,128)(2,1)S(1)} %collective-permute-done.7.refs_4_), channel_id=1, source_target_pairs={{0,448},{64,128},{128,64},{192,256},{256,192},{320,384},{384,320},... | collective-permute-start | bytes 774152 | tf_op jit(solution)/shard_map/ppermute | solution.py:19
  64.4 4.8 %shard_map.120 = (bf16[2,126,512]{2,1,0:T(8,128)(2,1)S(1)}, bf16[2,126,512]{2,1,0:T(8,128)(2,1)S(1)}, bf16[2,126,512]{2,1,0:T(8,128)(2,1)S(1)}, bf16[2,126,512]{...) custom-call(bf16[16,64,512]{2,1,0:T(8,128)(2,1)S(1)} %all-to-all-done.refs_0_, ...), custom_call_target="tpu_custom_call" | custom-call | flops 3623878656 | bytes 1048576 | tf_op jit(solution)/shard_map/pallas_call | solution.py:170
  69.2 4.5 %shard_map.121 = (bf16[2,126,512]{2,1,0:T(8,128)(2,1)S(1)}, bf16[2,126,512]{2,1,0:T(8,128)(2,1)S(1)}, bf16[2,126,512]{2,1,0:T(8,128)(2,1)S(1)}, f32[16,64,512]{2,1,0:T(8,128)S(1)}, f32[16,64,512]{2,1,0:T(8,128)S(1)}) custom-call(bf16[16,64,512]{2,1,0:T(8,128)(2,1)S(1)} %all-to-all-done.refs_0_, bf16[16,64,512]{2,1,0:T(8,128)(2,1)S(1)} %collective-permute-done.8.refs_1_, ...), custom_call_target="tpu_custom_call" | custom-call | flops 2717908992 | bytes 1048576 | tf_op jit(solution)/shard_map/pallas_call | solution.py:170
  78.5 4.1 %collective-permute-start.9 = (bf16[2,126,512]{2,1,0:T(8,128)(2,1)S(1)}, bf16[2,126,512]{2,1,0:T(8,128)(2,1)S(1)}, u32[]{:S(2)}, u32[]{:S(2)}) collective-permute-start(bf16[2,126,512]{2,1,0:T(8,128)(2,1)S(1)} %get-tuple-element.65), channel_id=1, source_target_pairs={{0,448},{64,128},{128,64},{192,256},{256,192},{320,384},{384,320},... | collective-permute-start | bytes 774152 | tf_op jit(solution)/shard_map/ppermute | solution.py:19
  82.5 3.0 %collective-permute-start.12 = (bf16[2,126,512]{2,1,0:T(8,128)(2,1)S(1)}, bf16[2,126,512]{2,1,0:T(8,128)(2,1)S(1)}, u32[]{:S(2)}, u32[]{:S(2)}) collective-permute-start(bf16[2,126,512]{2,1,0:T(8,128)(2,1)S(1)} %get-tuple-element.68), channel_id=1, source_target_pairs={{0,448},{64,128},{128,64},{192,256},{256,192},{320,384},{384,320},... | collective-permute-start | bytes 774152 | tf_op jit(solution)/shard_map/ppermute | solution.py:19
  85.5 5.2 %collective-permute-done.9 = bf16[2,126,512]{2,1,0:T(8,128)(2,1)S(1)} collective-permute-done((bf16[2,126,512]{2,1,0:T(8,128)(2,1)S(1)}, bf16[2,126,512]{2,1,0:T(8,128)(2,1)S(1)}, u32[]{:S(2)}, u32[]{:S(2)}) %collective-permute-start.9) | collective-permute-done | bytes 258080 | tf_op jit(solution)/shard_map/ppermute | solution.py:19
  92.7 3.0 %collective-permute-done.12 = bf16[2,126,512]{2,1,0:T(8,128)(2,1)S(1)} collective-permute-done((bf16[2,126,512]{2,1,0:T(8,128)(2,1)S(1)}, bf16[2,126,512]{2,1,0:T(8,128)(2,1)S(1)}, u32[]{:S(2)}, u32[]{:S(2)}) %collective-permute-start.12) | collective-permute-done | bytes 258080 | tf_op jit(solution)/shard_map/ppermute | solution.py:19
  95.7 4.0 %collective-permute-done.10 = bf16[2,126,512]{2,1,0:T(8,128)(2,1)S(1)} collective-permute-done((bf16[2,126,512]{2,1,0:T(8,128)(2,1)S(1)}, bf16[2,126,512]{2,1,0:T(8,128)(2,1)S(1)}, u32[]{:S(2)}, u32[]{:S(2)}) %collective-permute-start.10) | collective-permute-done | bytes 258080 | tf_op jit(solution)/shard_map/ppermute | solution.py:19
  102.1 4.0 %collective-permute-start.14 = (bf16[2,126,512]{2,1,0:T(8,128)(2,1)S(1)}, bf16[2,126,512]{2,1,0:T(8,128)(2,1)S(1)}, u32[]{:S(2)}, u32[]{:S(2)}) collective-permute-start(bf16[2,126,512]{2,1,0:T(8,128)(2,1)S(1)} %add_convert_fusion.2), channel_id=1, source_target_pairs={{0,448},{64,128},{128,64},{192,256},{256,192},{320,384},{384,320},... | collective-permute-start | bytes 774152 | tf_op jit(solution)/shard_map/ppermute | solution.py:19
  107.5 7.5 %all-to-all-start.1 = ((bf16[16,64,512]{2,1,0:T(8,128)(2,1)}), bf16[16,64,512]{2,1,0:T(8,128)(2,1)S(1)}, u32[]{:S(2)}, u32[]{:S(2)}) async-start(bf16[16,64,512]{2,1,0:T(8,128)(2,1)} %add_convert_fusion), calls=%async_computation.1 | async-start | bytes 2097152 | tf_op jit(solution)/shard_map/all_to_all | solution.py:249
  115.1 3.1 %collective-permute-start.17 = (bf16[2,126,512]{2,1,0:T(8,128)(2,1)S(1)}, bf16[2,126,512]{2,1,0:T(8,128)(2,1)S(1)}, u32[]{:S(2)}, u32[]{:S(2)}) collective-permute-start(bf16[2,126,512]{2,1,0:T(8,128)(2,1)S(1)} %shard_map.123), channel_id=1, source_target_pairs={{0,448},{64,128},{128,64},{192,256},{256,192},{320,384},{384,320},... | collective-permute-start | bytes 774152 | tf_op jit(solution)/shard_map/ppermute | solution.py:19
  120.8 4.4 %collective-permute-done.16 = bf16[1,126,512]{2,1,0:T(8,128)(2,1)S(1)} collective-permute-done((bf16[1,126,512]{2,1,0:T(8,128)(2,1)S(1)}, bf16[1,126,512]{2,1,0:T(8,128)(2,1)S(1)}, u32[]{:S(2)}, u32[]{:S(2)}) %collective-permute-start.16) | collective-permute-done | bytes 129056 | tf_op jit(solution)/shard_map/ppermute | solution.py:19
  127.8 4.4 %collective-permute-done.18 = bf16[1,126,512]{2,1,0:T(8,128)(2,1)S(1)} collective-permute-done((bf16[1,126,512]{2,1,0:T(8,128)(2,1)S(1)}, bf16[1,126,512]{2,1,0:T(8,128)(2,1)S(1)}, u32[]{:S(2)}, u32[]{:S(2)}) %collective-permute-start.18) | collective-permute-done | bytes 129056 | tf_op jit(solution)/shard_map/ppermute | solution.py:19
  132.3 5.1 %collective-permute-start.19 = (bf16[1,126,512]{2,1,0:T(8,128)(2,1)S(1)}, bf16[1,126,512]{2,1,0:T(8,128)(2,1)S(1)}, u32[]{:S(2)}, u32[]{:S(2)}) collective-permute-start(bf16[1,126,512]{2,1,0:T(8,128)(2,1)S(1)} %fusion), channel_id=1, source_target_pairs={{0,32},{32,0},{1,33},{33,1},{2,34},{34,2},{3,35},{35,3},{4,36},{36... | collective-permute-start | bytes 387080 | tf_op jit(solution)/shard_map/ppermute | solution.py:23
  140.4 4.7 %collective-permute-done.19.far = bf16[1,126,512]{2,1,0:T(8,128)(2,1)S(1)} collective-permute-done((bf16[1,126,512]{2,1,0:T(8,128)(2,1)S(1)}, bf16[1,126,512]{2,1,0:T(8,128)(2,1)S(1)}, u32[]{:S(2)}, u32[]{:S(2)}) %collective-permute-start.19) | collective-permute-done | bytes 129056 | tf_op jit(solution)/shard_map/ppermute | solution.py:23
  (48 shorter events, 34.2 us)
Async XLA Ops:
  1.5 13.7 %collective-permute-start = (bf16[1,126,512]{2,1,0:T(8,128)(2,1)S(1)}, bf16[1,126,512]{2,1,0:T(8,128)(2,1)S(1)}, u32[]{:S(2)}, u32[]{:S(2)}) collective-permute-start(bf16[1,126,512]{2,1,0:T(8,128)(2,1)S(1)} %maximum_bitcast_fusion), channel_id=1, source_target_pairs={{0,32},{32,0},{1,33},{33,1},{2,34},{34,2},{3,35},{35,3},{4,36},{36... | collective-permute-start | bytes 387080 | tf_op jit(solution)/shard_map/ppermute | solution.py:23
  8.4 7.5 %collective-permute-start.1 = (bf16[1,126,512]{2,1,0:T(8,128)(2,1)S(1)}, bf16[1,126,512]{2,1,0:T(8,128)(2,1)S(1)}, u32[]{:S(2)}, u32[]{:S(2)}) collective-permute-start(bf16[1,126,512]{2,1,0:T(8,128)(2,1)S(1)} %maximum_bitcast_fusion), channel_id=1, source_target_pairs={{0,64},{64,0},{128,192},{192,128},{256,320},{320,256},{384,448},{4... | collective-permute-start | bytes 387080 | tf_op jit(solution)/shard_map/ppermute | solution.py:19
  15.9 19.9 %collective-permute-start.2 = (bf16[2,126,512]{2,1,0:T(8,128)(2,1)S(1)}, bf16[2,126,512]{2,1,0:T(8,128)(2,1)S(1)}, u32[]{:S(2)}, u32[]{:S(2)}) collective-permute-start(bf16[2,126,512]{2,1,0:T(8,128)(2,1)S(1)} %pad_maximum_fusion.refs_2_), channel_id=1, source_target_pairs={{0,448},{64,128},{128,64},{192,256},{256,192},{320,384},{384,320},... | collective-permute-start | bytes 774152 | tf_op jit(solution)/shard_map/ppermute | solution.py:19
  26.2 9.6 %collective-permute-start.3 = (bf16[1,126,512]{2,1,0:T(8,128)(2,1)S(1)}, bf16[1,126,512]{2,1,0:T(8,128)(2,1)S(1)}, u32[]{:S(2)}, u32[]{:S(2)}) collective-permute-start(bf16[1,126,512]{2,1,0:T(8,128)(2,1)S(1)} %collective-permute-done.one), channel_id=1, source_target_pairs={{0,64},{64,0},{128,192},{192,128},{256,320},{320,256},{384,448},{4... | collective-permute-start | bytes 387080 | tf_op jit(solution)/shard_map/ppermute | solution.py:19
  28.1 31.3 %all-to-all-start = ((bf16[16,64,512]{2,1,0:T(8,128)(2,1)}), bf16[16,64,512]{2,1,0:T(8,128)(2,1)S(1)}, u32[]{:S(2)}, u32[]{:S(2)}) async-start(bf16[16,64,512]{2,1,0:T(8,128)(2,1)} %get-tuple-element.55), calls=%async_computation | async-start | bytes 2097152 | tf_op jit(solution)/shard_map/all_to_all | solution.py:223
  35.8 9.7 %collective-permute-start.5 = (bf16[2,126,512]{2,1,0:T(8,128)(2,1)S(1)}, bf16[2,126,512]{2,1,0:T(8,128)(2,1)S(1)}, u32[]{:S(2)}, u32[]{:S(2)}) collective-permute-start(bf16[2,126,512]{2,1,0:T(8,128)(2,1)S(1)} %shard_map.119.refs_2_), channel_id=1, source_target_pairs={{0,448},{64,128},{128,64},{192,256},{256,192},{320,384},{384,320},... | collective-permute-start | bytes 774152 | tf_op jit(solution)/shard_map/ppermute | solution.py:19
  38.8 8.3 %collective-permute-start.4 = (bf16[2,126,512]{2,1,0:T(8,128)(2,1)S(1)}, bf16[2,126,512]{2,1,0:T(8,128)(2,1)S(1)}, u32[]{:S(2)}, u32[]{:S(2)}) collective-permute-start(bf16[2,126,512]{2,1,0:T(8,128)(2,1)S(1)} %collective-permute-done.2.refs_3_), channel_id=1, source_target_pairs={{0,64},{64,0},{128,192},{192,128},{256,320},{320,256},{384,448},{4... | collective-permute-start | bytes 774152 | tf_op jit(solution)/shard_map/ppermute | solution.py:19
  47.1 9.5 %collective-permute-start.6 = (bf16[2,126,512]{2,1,0:T(8,128)(2,1)S(1)}, bf16[2,126,512]{2,1,0:T(8,128)(2,1)S(1)}, u32[]{:S(2)}, u32[]{:S(2)}) collective-permute-start(bf16[2,126,512]{2,1,0:T(8,128)(2,1)S(1)} %collective-permute-done.4.refs_4_), channel_id=1, source_target_pairs={{0,448},{64,128},{128,64},{192,256},{256,192},{320,384},{384,320},... | collective-permute-start | bytes 774152 | tf_op jit(solution)/shard_map/ppermute | solution.py:19
  51.2 8.3 %collective-permute-start.7 = (bf16[2,126,512]{2,1,0:T(8,128)(2,1)S(1)}, bf16[2,126,512]{2,1,0:T(8,128)(2,1)S(1)}, u32[]{:S(2)}, u32[]{:S(2)}) collective-permute-start(bf16[2,126,512]{2,1,0:T(8,128)(2,1)S(1)} %collective-permute-done.5.refs_3_), channel_id=1, source_target_pairs={{0,64},{64,0},{128,192},{192,128},{256,320},{320,256},{384,448},{4... | collective-permute-start | bytes 774152 | tf_op jit(solution)/shard_map/ppermute | solution.py:19
  59.4 4.9 %collective-permute-start.8 = (bf16[16,64,512]{2,1,0:T(8,128)(2,1)S(1)}, bf16[16,64,512]{2,1,0:T(8,128)(2,1)S(1)}, u32[]{:S(2)}, u32[]{:S(2)}) collective-permute-start(bf16[16,64,512]{2,1,0:T(8,128)(2,1)S(1)} %all-to-all-done.refs_0_), channel_id=1, source_target_pairs={{0,16},{16,0},{1,17},{17,1},{2,18},{18,2},{3,19},{19,3},{4,20},{20... | collective-permute-start | bytes 3145736 | tf_op jit(solution)/shard_map/ppermute | solution.py:23
  61.3 12.4 %collective-permute-start.11 = (bf16[2,126,512]{2,1,0:T(8,128)(2,1)S(1)}, bf16[2,126,512]{2,1,0:T(8,128)(2,1)S(1)}, u32[]{:S(2)}, u32[]{:S(2)}) collective-permute-start(bf16[2,126,512]{2,1,0:T(8,128)(2,1)S(1)} %collective-permute-done.7.refs_4_), channel_id=1, source_target_pairs={{0,448},{64,128},{128,64},{192,256},{256,192},{320,384},{384,320},... | collective-permute-start | bytes 774152 | tf_op jit(solution)/shard_map/ppermute | solution.py:19
  76.3 23.4 %collective-permute-start.13 = (bf16[16,64,512]{2,1,0:T(8,128)(2,1)S(1)}, bf16[16,64,512]{2,1,0:T(8,128)(2,1)S(1)}, u32[]{:S(2)}, u32[]{:S(2)}) collective-permute-start(bf16[16,64,512]{2,1,0:T(8,128)(2,1)S(1)} %get-tuple-element.69), channel_id=1, source_target_pairs={{0,16},{16,0},{1,17},{17,1},{2,18},{18,2},{3,19},{19,3},{4,20},{20... | collective-permute-start | bytes 3145736 | tf_op jit(solution)/shard_map/ppermute | solution.py:23
  78.5 12.2 %collective-permute-start.9 = (bf16[2,126,512]{2,1,0:T(8,128)(2,1)S(1)}, bf16[2,126,512]{2,1,0:T(8,128)(2,1)S(1)}, u32[]{:S(2)}, u32[]{:S(2)}) collective-permute-start(bf16[2,126,512]{2,1,0:T(8,128)(2,1)S(1)} %get-tuple-element.65), channel_id=1, source_target_pairs={{0,448},{64,128},{128,64},{192,256},{256,192},{320,384},{384,320},... | collective-permute-start | bytes 774152 | tf_op jit(solution)/shard_map/ppermute | solution.py:19
  82.5 13.2 %collective-permute-start.12 = (bf16[2,126,512]{2,1,0:T(8,128)(2,1)S(1)}, bf16[2,126,512]{2,1,0:T(8,128)(2,1)S(1)}, u32[]{:S(2)}, u32[]{:S(2)}) collective-permute-start(bf16[2,126,512]{2,1,0:T(8,128)(2,1)S(1)} %get-tuple-element.68), channel_id=1, source_target_pairs={{0,448},{64,128},{128,64},{192,256},{256,192},{320,384},{384,320},... | collective-permute-start | bytes 774152 | tf_op jit(solution)/shard_map/ppermute | solution.py:19
  90.8 9.0 %collective-permute-start.10 = (bf16[2,126,512]{2,1,0:T(8,128)(2,1)S(1)}, bf16[2,126,512]{2,1,0:T(8,128)(2,1)S(1)}, u32[]{:S(2)}, u32[]{:S(2)}) collective-permute-start(bf16[2,126,512]{2,1,0:T(8,128)(2,1)S(1)} %add_convert_fusion.3), channel_id=1, source_target_pairs={{0,64},{64,0},{128,192},{192,128},{256,320},{320,256},{384,448},{4... | collective-permute-start | bytes 774152 | tf_op jit(solution)/shard_map/ppermute | solution.py:19
  99.8 15.2 %collective-permute-start.15 = (bf16[2,126,512]{2,1,0:T(8,128)(2,1)S(1)}, bf16[2,126,512]{2,1,0:T(8,128)(2,1)S(1)}, u32[]{:S(2)}, u32[]{:S(2)}) collective-permute-start(bf16[2,126,512]{2,1,0:T(8,128)(2,1)S(1)} %add_convert_fusion.1), channel_id=1, source_target_pairs={{0,64},{64,0},{128,192},{192,128},{256,320},{320,256},{384,448},{4... | collective-permute-start | bytes 774152 | tf_op jit(solution)/shard_map/ppermute | solution.py:19
  102.1 12.9 %collective-permute-start.14 = (bf16[2,126,512]{2,1,0:T(8,128)(2,1)S(1)}, bf16[2,126,512]{2,1,0:T(8,128)(2,1)S(1)}, u32[]{:S(2)}, u32[]{:S(2)}) collective-permute-start(bf16[2,126,512]{2,1,0:T(8,128)(2,1)S(1)} %add_convert_fusion.2), channel_id=1, source_target_pairs={{0,448},{64,128},{128,64},{192,256},{256,192},{320,384},{384,320},... | collective-permute-start | bytes 774152 | tf_op jit(solution)/shard_map/ppermute | solution.py:19
  107.5 31.7 %all-to-all-start.1 = ((bf16[16,64,512]{2,1,0:T(8,128)(2,1)}), bf16[16,64,512]{2,1,0:T(8,128)(2,1)S(1)}, u32[]{:S(2)}, u32[]{:S(2)}) async-start(bf16[16,64,512]{2,1,0:T(8,128)(2,1)} %add_convert_fusion), calls=%async_computation.1 | async-start | bytes 2097152 | tf_op jit(solution)/shard_map/all_to_all | solution.py:249
  115.1 24.1 %copy-start = (bf16[128,512]{1,0:T(8,128)(2,1)S(1)}, bf16[128,512]{1,0:T(8,128)(2,1)}, u32[]{:S(2)}) copy-start(bf16[128,512]{1,0:T(8,128)(2,1)} %cotangent.3) | copy-start | bytes 393220
  115.1 24.1 %copy-start.1 = (bf16[512,128]{1,0:T(8,128)(2,1)S(1)}, bf16[512,128]{1,0:T(8,128)(2,1)}, u32[]{:S(2)}) copy-start(bf16[512,128]{1,0:T(8,128)(2,1)} %get-tuple-element.79.first) | copy-start | bytes 393220
  115.1 10.1 %collective-permute-start.17 = (bf16[2,126,512]{2,1,0:T(8,128)(2,1)S(1)}, bf16[2,126,512]{2,1,0:T(8,128)(2,1)S(1)}, u32[]{:S(2)}, u32[]{:S(2)}) collective-permute-start(bf16[2,126,512]{2,1,0:T(8,128)(2,1)S(1)} %shard_map.123), channel_id=1, source_target_pairs={{0,448},{64,128},{128,64},{192,256},{256,192},{320,384},{384,320},... | collective-permute-start | bytes 774152 | tf_op jit(solution)/shard_map/ppermute | solution.py:19
  118.4 6.9 %collective-permute-start.16 = (bf16[1,126,512]{2,1,0:T(8,128)(2,1)S(1)}, bf16[1,126,512]{2,1,0:T(8,128)(2,1)S(1)}, u32[]{:S(2)}, u32[]{:S(2)}) collective-permute-start(bf16[1,126,512]{2,1,0:T(8,128)(2,1)S(1)} %slice.29), channel_id=1, source_target_pairs={{0,64},{64,0},{128,192},{192,128},{256,320},{320,256},{384,448},{4... | collective-permute-start | bytes 387080 | tf_op jit(solution)/shard_map/ppermute | solution.py:19
  125.4 6.9 %collective-permute-start.18 = (bf16[1,126,512]{2,1,0:T(8,128)(2,1)S(1)}, bf16[1,126,512]{2,1,0:T(8,128)(2,1)S(1)}, u32[]{:S(2)}, u32[]{:S(2)}) collective-permute-start(bf16[1,126,512]{2,1,0:T(8,128)(2,1)S(1)} %slice.28), channel_id=1, source_target_pairs={{0,64},{64,0},{128,192},{192,128},{256,320},{320,256},{384,448},{4... | collective-permute-start | bytes 387080 | tf_op jit(solution)/shard_map/ppermute | solution.py:19
  132.3 12.9 %collective-permute-start.19 = (bf16[1,126,512]{2,1,0:T(8,128)(2,1)S(1)}, bf16[1,126,512]{2,1,0:T(8,128)(2,1)S(1)}, u32[]{:S(2)}, u32[]{:S(2)}) collective-permute-start(bf16[1,126,512]{2,1,0:T(8,128)(2,1)S(1)} %fusion), channel_id=1, source_target_pairs={{0,32},{32,0},{1,33},{33,1},{2,34},{34,2},{3,35},{35,3},{4,36},{36... | collective-permute-start | bytes 387080 | tf_op jit(solution)/shard_map/ppermute | solution.py:23
  (2 other events, 48.2 us)

commit v4 on v3

--- a/solution.py
+++ b/solution.py
@@ -42,7 +42,7 @@
     return lax.dot_general(left, right, ((contract[:1], contract[1:]), ((), ())), preferred_element_type=F32)
 
 
-def kernel_call(body, outs, scratch=(), flops=0, grant=32):
+def kernel_call(body, outs, scratch=(), flops=0, grant=24):
     return pl.pallas_call(
         body,
         out_shape=outs,
@@ -190,8 +190,20 @@
     return kernel_call(total_body, out, flops=flops, grant=16)(one, two)
 
 
-def finish_body(near, far, *outs):
-    value = near[0] + far[0].astype(F32)
+def split_body(one, two, keep, send):
+    value = one[...].astype(F32) + two[...].astype(F32)
+    keep[...] = value[0:1]
+    send[...] = value[1:2].astype(send.dtype)
+
+
+def split(one, two, flops=0):
+    shape = (1,) + one.shape[1:]
+    outs = [jax.ShapeDtypeStruct(shape, F32), jax.ShapeDtypeStruct(shape, BF16)]
+    return kernel_call(split_body, outs, flops=flops, grant=16)(one, two)
+
+
+def finish_body(near, near_far, far, *outs):
+    value = near[0] + near_far[0].astype(F32) + far[0].astype(F32)
     rows = value.shape[0] // 3
     for k, out in enumerate(outs):
         for j in range(value.shape[1] // 128):
@@ -222,9 +234,8 @@
     other, near_got, send = together((other, near_got, send))
     mine = lax.all_to_all(send, ("x", "yl"), 0, 0, tiled=True)
     near = [jnp.concatenate([own, near_got], axis=0)]
+    far_got = swap_z(other, 0)
     near.append(swap_z(near[0], 1))
-    far_got = swap_z(other, 0)
-    near[1], far_got = together((near[1], far_got))
     far = [pair(other, far_got, 4 * 10**10)]
     near.append(swap_z(near[1], 0))
     far.append(swap_z(far[0], 1))
@@ -240,20 +251,24 @@
     late, (local, rest) = expert_call(capacity, mine, theirs, far[3:], sums, True)
     far_terms = (*early, *late)
 
-    near_got = swap_z(near_terms[3], 1)
     rest = swap(rest, "core")
-    near_sum = add(near_terms[2], near_got).astype(BF16)
-    near_got, got, rest = together((swap_z(near_sum, 0), swap_z(far_terms[3], 1), rest))
-    far_sum = add(far_terms[2], got).astype(BF16)
-    near_sum = add(near_terms[1], near_got).astype(BF16)
+    got = swap_z(far_terms[3], 1)
+    far_sum = total(far_terms[2], got, BF16, 4 * 10**10)
+    far_sum, rest = together((far_sum, rest))
     back = lax.all_to_all(add(local, rest).astype(BF16), ("x", "yl"), 0, 0, tiled=True)
-    near_got, got = together((swap_z(near_sum, 1), swap_z(far_sum, 0)))
-    far_sum = total(far_terms[1], got, BF16, 4 * 10**10)
-    near_sum = add(near_terms[0], near_got)
-    near_got, got = together((swap_z(near_sum[1:].astype(BF16), 0), swap_z(far_sum, 1)))
-    near_sum = add(near_sum[:1], near_got)
-    far_sum = add(far_terms[0], got)
-    far_sum = add(far_sum[:1], swap_z(far_sum[1:].astype(BF16), 0)).astype(BF16)
+    got, near_got = together((swap_z(far_sum, 0), swap_z(near_terms[3], 1)))
+    far_sum = total(far_terms[1], got, BF16, 0)
+    far_sum, near_got = together((far_sum, near_got))
+    near_sum = total(near_terms[2], near_got, BF16, 4 * 10**9)
+    got, near_got = together((swap_z(far_sum, 1), swap_z(near_sum, 0)))
+    far_keep, far_send = split(far_terms[0], got)
+    far_send, near_got = together((far_send, near_got))
+    near_sum = total(near_terms[1], near_got, BF16, 4 * 10**9)
+    got, near_got = together((swap_z(far_send, 0), swap_z(near_sum, 1)))
+    far_sum = total(far_keep, got, BF16)
+    far_sum, near_got = together((far_sum, near_got))
+    near_keep, near_send = split(near_terms[0], near_got, 4 * 10**9)
+    near_got = swap_z(near_send, 0)
     got = swap(far_sum, "yh")
     row = jax.ShapeDtypeStruct((tok_rows, width), BF16)
     mixed, latent_grad, score_grad = kernel_call(
@@ -263,7 +278,7 @@
     got, mixed = together((got, mixed))
     lanes = width // 128
     block = jax.ShapeDtypeStruct((hidden_rows * lanes, 128), F32)
-    grads = kernel_call(finish_body, [block] * 3)(near_sum, got)
+    grads = kernel_call(finish_body, [block] * 3)(near_keep, near_got, got)
     grads = [grad.reshape(1, hidden_rows, width) for grad in grads]
     return (mixed, latent_grad, score_grad.T, *grads)
 

time: 147 us -> 139 us (0.946)
  the two profiles are of different devices: /device:TPU:8 before, /device:TPU:2 now
where the time goes in v4:
time: 139 us
  starting transfers between devices  88.2 us (63%)
  waiting for transfers between devices  29.5 us (21%)
  Pallas kernels  16.9 us (12%)
  other arithmetic  2.24 us (2%)
    ppermute x16, starting transfers between devices, swap_z(): return lax.ppermute(rows, 'z', pairs)  57.4 us
    ppermute x16, waiting for transfers between devices, swap_z(): return lax.ppermute(rows, 'z', pairs)  26.4 us
    ppermute x4, starting transfers between devices, swap(): return lax.ppermute(rows, axis, [(0, 1), (1, 0)])  16.7 us
    pallas_call x3, Pallas kernels, expert_call(): got = call(mine, theirs, *pieces, *sums)  11.9 us
    all_to_all x1, starting transfers between devices, shards(): lax.all_to_all(add(local, rest).astype(BF16), ('x', 'yl'), 0, 0, tiled=True)  7.27 us
    all_to_all x1, starting transfers between devices, shards(): mine = lax.all_to_all(send, ('x', 'yl'), 0, 0, tiled=True)  6.84 us
  transfers between devices with their start and end apart: 22, of which 12 were waited for; matrix products, arithmetic and copies ran while one was open for 1% of the time, Pallas kernels for 10%

profile of v4, /device:TPU:2, one launch (start us, length us, event | category | flops | bytes accessed | tf_op | source)
XLA Modules:
  0.0 138.5 jit_solution(6186518252864733114)
XLA Ops:
  1.5 7.7 %collective-permute-start = (bf16[1,126,512]{2,1,0:T(8,128)(2,1)S(1)}, bf16[1,126,512]{2,1,0:T(8,128)(2,1)S(1)}, u32[]{:S(2)}, u32[]{:S(2)}) collective-permute-start(bf16[1,126,512]{2,1,0:T(8,128)(2,1)S(1)} %maximum_bitcast_fusion), channel_id=1, source_target_pairs={{0,32},{32,0},{1,33},{33,1},{2,34},{34,2},{3,35},{35,3},{4,36},{36... | collective-permute-start | bytes 387080 | tf_op jit(solution)/shard_map/ppermute | solution.py:23
  9.3 4.3 %collective-permute-start.1 = (bf16[1,126,512]{2,1,0:T(8,128)(2,1)S(1)}, bf16[1,126,512]{2,1,0:T(8,128)(2,1)S(1)}, u32[]{:S(2)}, u32[]{:S(2)}) collective-permute-start(bf16[1,126,512]{2,1,0:T(8,128)(2,1)S(1)} %maximum_bitcast_fusion), channel_id=1, source_target_pairs={{0,64},{64,0},{128,192},{192,128},{256,320},{320,256},{384,448},{4... | collective-permute-start | bytes 387080 | tf_op jit(solution)/shard_map/ppermute | solution.py:19
  13.5 2.6 %shard_map.118 = (bf16[16,64,512]{2,1,0:T(8,128)(2,1)}, bf16[512,128]{1,0:T(8,128)(2,1)}, bf16[512,128]{1,0:T(8,128)(2,1)}) custom-call(bf16[128,512]{1,0:T(8,128)(2,1)} %latent.1, bf16[128,512]{1,0:T(8,128)(2,1)} %cotangent.3, s32[2,128]{1,0:T(2,128)} %bitcast.16, f32[2,128]{1,0:T(2,128)} %bitcast.11), custom_call_target="tpu_custom_call" | custom-call | bytes 1048576 | tf_op jit(solution)/shard_map/pallas_call | solution.py:228
  16.7 3.6 %collective-permute-start.4 = (bf16[1,126,512]{2,1,0:T(8,128)(2,1)S(1)}, bf16[1,126,512]{2,1,0:T(8,128)(2,1)S(1)}, u32[]{:S(2)}, u32[]{:S(2)}) collective-permute-start(bf16[1,126,512]{2,1,0:T(8,128)(2,1)S(1)} %collective-permute-done.one), channel_id=1, source_target_pairs={{0,64},{64,0},{128,192},{192,128},{256,320},{320,256},{384,448},{4... | collective-permute-start | bytes 387080 | tf_op jit(solution)/shard_map/ppermute | solution.py:19
  20.4 9.1 %collective-permute-start.2 = (bf16[2,126,512]{2,1,0:T(8,128)(2,1)S(1)}, bf16[2,126,512]{2,1,0:T(8,128)(2,1)S(1)}, u32[]{:S(2)}, u32[]{:S(2)}) collective-permute-start(bf16[2,126,512]{2,1,0:T(8,128)(2,1)S(1)} %pad_maximum_fusion.refs_2_), channel_id=1, source_target_pairs={{0,448},{64,128},{128,64},{192,256},{256,192},{320,384},{384,320},... | collective-permute-start | bytes 774152 | tf_op jit(solution)/shard_map/ppermute | solution.py:19
  29.6 6.8 %all-to-all-start = ((bf16[16,64,512]{2,1,0:T(8,128)(2,1)}), bf16[16,64,512]{2,1,0:T(8,128)(2,1)S(1)}, u32[]{:S(2)}, u32[]{:S(2)}) async-start(bf16[16,64,512]{2,1,0:T(8,128)(2,1)} %get-tuple-element.62), calls=%async_computation | async-start | bytes 2097152 | tf_op jit(solution)/shard_map/all_to_all | solution.py:235
  40.3 5.6 %collective-permute-done.5.refs_3_ = bf16[2,126,512]{2,1,0:T(8,128)(2,1)S(1)} collective-permute-done((bf16[2,126,512]{2,1,0:T(8,128)(2,1)S(1)}, bf16[2,126,512]{2,1,0:T(8,128)(2,1)S(1)}, u32[]{:S(2)}, u32[]{:S(2)}) %collective-permute-start.5) | collective-permute-done | bytes 258080 | tf_op jit(solution)/shard_map/ppermute | solution.py:19
  46.6 5.1 %collective-permute-start.6 = (bf16[2,126,512]{2,1,0:T(8,128)(2,1)S(1)}, bf16[2,126,512]{2,1,0:T(8,128)(2,1)S(1)}, u32[]{:S(2)}, u32[]{:S(2)}) collective-permute-start(bf16[2,126,512]{2,1,0:T(8,128)(2,1)S(1)} %collective-permute-done.3.refs_4_), channel_id=1, source_target_pairs={{0,448},{64,128},{128,64},{192,256},{256,192},{320,384},{384,320},... | collective-permute-start | bytes 774152 | tf_op jit(solution)/shard_map/ppermute | solution.py:19
  53.7 2.4 %collective-permute-done.6.refs_5_ = bf16[2,126,512]{2,1,0:T(8,128)(2,1)S(1)} collective-permute-done((bf16[2,126,512]{2,1,0:T(8,128)(2,1)S(1)}, bf16[2,126,512]{2,1,0:T(8,128)(2,1)S(1)}, u32[]{:S(2)}, u32[]{:S(2)}) %collective-permute-start.6) | collective-permute-done | bytes 258080 | tf_op jit(solution)/shard_map/ppermute | solution.py:19
  56.1 3.9 %collective-permute-done.7.refs_4_ = bf16[2,126,512]{2,1,0:T(8,128)(2,1)S(1)} collective-permute-done((bf16[2,126,512]{2,1,0:T(8,128)(2,1)S(1)}, bf16[2,126,512]{2,1,0:T(8,128)(2,1)S(1)}, u32[]{:S(2)}, u32[]{:S(2)}) %collective-permute-start.7) | collective-permute-done | bytes 258080 | tf_op jit(solution)/shard_map/ppermute | solution.py:19
  65.0 4.8 %shard_map.120 = (bf16[2,126,512]{2,1,0:T(8,128)(2,1)S(1)}, bf16[2,126,512]{2,1,0:T(8,128)(2,1)S(1)}, bf16[2,126,512]{2,1,0:T(8,128)(2,1)S(1)}, bf16[2,126,512]{...) custom-call(bf16[16,64,512]{2,1,0:T(8,128)(2,1)S(1)} %all-to-all-done.refs_0_, ...), custom_call_target="tpu_custom_call" | custom-call | flops 3623878656 | bytes 1048576 | tf_op jit(solution)/shard_map/pallas_call | solution.py:170
  70.5 4.5 %shard_map.121 = (bf16[2,126,512]{2,1,0:T(8,128)(2,1)S(1)}, bf16[2,126,512]{2,1,0:T(8,128)(2,1)S(1)}, bf16[2,126,512]{2,1,0:T(8,128)(2,1)S(1)}, f32[16,64,512]{2,1,0:T(8,128)S(1)}, f32[16,64,512]{2,1,0:T(8,128)S(1)}) custom-call(bf16[16,64,512]{2,1,0:T(8,128)(2,1)S(1)} %all-to-all-done.refs_0_, bf16[16,64,512]{2,1,0:T(8,128)(2,1)S(1)} %collective-permute-done.8.refs_1_, ...), custom_call_target="tpu_custom_call" | custom-call | flops 2717908992 | bytes 1048576 | tf_op jit(solution)/shard_map/pallas_call | solution.py:170
  75.0 2.6 %shard_map.122 = (bf16[2,126,512]{2,1,0:T(8,128)(2,1)S(1)}, f32[16,64,512]{2,1,0:T(8,128)S(1)}, bf16[16,64,512]{2,1,0:T(8,128)(2,1)S(1)}) custom-call(bf16[16,64,512]{2,1,0:T(8,128)(2,1)S(1)} %all-to-all-done.refs_0_, bf16[16,64,512]{2,1,0:T(8,128)(2,1)S(1)} %collective-permute-done.8.refs_1_, bf16[2,126,512]{2,1,0:T(8,128)(2,1)S(1)} %collective-permute-done.9.refs_2_, ...), custom_call_target="tpu_custom_call" | custom-call | flops 905969664 | bytes 1048576 | tf_op jit(solution)/shard_map/pallas_call | solution.py:170
  77.7 4.4 %collective-permute-start.10 = (bf16[2,126,512]{2,1,0:T(8,128)(2,1)S(1)}, bf16[2,126,512]{2,1,0:T(8,128)(2,1)S(1)}, u32[]{:S(2)}, u32[]{:S(2)}) collective-permute-start(bf16[2,126,512]{2,1,0:T(8,128)(2,1)S(1)} %get-tuple-element.73), channel_id=1, source_target_pairs={{0,448},{64,128},{128,64},{192,256},{256,192},{320,384},{384,320},... | collective-permute-start | bytes 774152 | tf_op jit(solution)/shard_map/ppermute | solution.py:19
  84.0 2.6 %collective-permute-start.13 = (bf16[2,126,512]{2,1,0:T(8,128)(2,1)S(1)}, bf16[2,126,512]{2,1,0:T(8,128)(2,1)S(1)}, u32[]{:S(2)}, u32[]{:S(2)}) collective-permute-start(bf16[2,126,512]{2,1,0:T(8,128)(2,1)S(1)} %get-tuple-element.76), channel_id=1, source_target_pairs={{0,448},{64,128},{128,64},{192,256},{256,192},{320,384},{384,320},... | collective-permute-start | bytes 774152 | tf_op jit(solution)/shard_map/ppermute | solution.py:19
  86.7 2.4 %collective-permute-done.10.two = bf16[2,126,512]{2,1,0:T(8,128)(2,1)S(1)} collective-permute-done((bf16[2,126,512]{2,1,0:T(8,128)(2,1)S(1)}, bf16[2,126,512]{2,1,0:T(8,128)(2,1)S(1)}, u32[]{:S(2)}, u32[]{:S(2)}) %collective-permute-start.10) | collective-permute-done | bytes 258080 | tf_op jit(solution)/shard_map/ppermute | solution.py:19
  92.5 7.3 %all-to-all-start.1 = ((bf16[16,64,512]{2,1,0:T(8,128)(2,1)}), bf16[16,64,512]{2,1,0:T(8,128)(2,1)S(1)}, u32[]{:S(2)}, u32[]{:S(2)}) async-start(bf16[16,64,512]{2,1,0:T(8,128)(2,1)} %add_convert_fusion), calls=%async_computation.1 | async-start | bytes 2097152 | tf_op jit(solution)/shard_map/all_to_all | solution.py:258
  99.9 3.9 %collective-permute-start.15 = (bf16[2,126,512]{2,1,0:T(8,128)(2,1)S(1)}, bf16[2,126,512]{2,1,0:T(8,128)(2,1)S(1)}, u32[]{:S(2)}, u32[]{:S(2)}) collective-permute-start(bf16[2,126,512]{2,1,0:T(8,128)(2,1)S(1)} %shard_map.125), channel_id=1, source_target_pairs={{0,64},{64,0},{128,192},{192,128},{256,320},{320,256},{384,448},{4... | collective-permute-start | bytes 774152 | tf_op jit(solution)/shard_map/ppermute | solution.py:19
  103.8 5.2 %collective-permute-start.14 = (bf16[2,126,512]{2,1,0:T(8,128)(2,1)S(1)}, bf16[2,126,512]{2,1,0:T(8,128)(2,1)S(1)}, u32[]{:S(2)}, u32[]{:S(2)}) collective-permute-start(bf16[2,126,512]{2,1,0:T(8,128)(2,1)S(1)} %shard_map.124), channel_id=1, source_target_pairs={{0,448},{64,128},{128,64},{192,256},{256,192},{320,384},{384,320},... | collective-permute-start | bytes 774152 | tf_op jit(solution)/shard_map/ppermute | solution.py:19
  109.1 4.3 %collective-permute-done.14.two = bf16[2,126,512]{2,1,0:T(8,128)(2,1)S(1)} collective-permute-done((bf16[2,126,512]{2,1,0:T(8,128)(2,1)S(1)}, bf16[2,126,512]{2,1,0:T(8,128)(2,1)S(1)}, u32[]{:S(2)}, u32[]{:S(2)}) %collective-permute-start.14) | collective-permute-done | bytes 258080 | tf_op jit(solution)/shard_map/ppermute | solution.py:19
  113.6 5.1 %collective-permute-start.17 = (bf16[2,126,512]{2,1,0:T(8,128)(2,1)S(1)}, bf16[2,126,512]{2,1,0:T(8,128)(2,1)S(1)}, u32[]{:S(2)}, u32[]{:S(2)}) collective-permute-start(bf16[2,126,512]{2,1,0:T(8,128)(2,1)S(1)} %shard_map.127), channel_id=1, source_target_pairs={{0,448},{64,128},{128,64},{192,256},{256,192},{320,384},{384,320},... | collective-permute-start | bytes 774152 | tf_op jit(solution)/shard_map/ppermute | solution.py:19
  120.6 4.9 %collective-permute-done.16.two = bf16[1,126,512]{2,1,0:T(8,128)(2,1)S(1)} collective-permute-done((bf16[1,126,512]{2,1,0:T(8,128)(2,1)S(1)}, bf16[1,126,512]{2,1,0:T(8,128)(2,1)S(1)}, u32[]{:S(2)}, u32[]{:S(2)}) %collective-permute-start.16) | collective-permute-done | bytes 129056 | tf_op jit(solution)/shard_map/ppermute | solution.py:19
  125.6 5.1 %collective-permute-start.18 = (bf16[1,126,512]{2,1,0:T(8,128)(2,1)S(1)}, bf16[1,126,512]{2,1,0:T(8,128)(2,1)S(1)}, u32[]{:S(2)}, u32[]{:S(2)}) collective-permute-start(bf16[1,126,512]{2,1,0:T(8,128)(2,1)S(1)} %shard_map.128), channel_id=1, source_target_pairs={{0,32},{32,0},{1,33},{33,1},{2,34},{34,2},{3,35},{35,3},{4,36},{36... | collective-permute-start | bytes 387080 | tf_op jit(solution)/shard_map/ppermute | solution.py:23
  134.1 2.3 %collective-permute-done.18.far = bf16[1,126,512]{2,1,0:T(8,128)(2,1)S(1)} collective-permute-done((bf16[1,126,512]{2,1,0:T(8,128)(2,1)S(1)}, bf16[1,126,512]{2,1,0:T(8,128)(2,1)S(1)}, u32[]{:S(2)}, u32[]{:S(2)}) %collective-permute-start.18) | collective-permute-done | bytes 129056 | tf_op jit(solution)/shard_map/ppermute | solution.py:23
  (53 shorter events, 26.5 us)
Async XLA Ops:
  1.5 14.6 %collective-permute-start = (bf16[1,126,512]{2,1,0:T(8,128)(2,1)S(1)}, bf16[1,126,512]{2,1,0:T(8,128)(2,1)S(1)}, u32[]{:S(2)}, u32[]{:S(2)}) collective-permute-start(bf16[1,126,512]{2,1,0:T(8,128)(2,1)S(1)} %maximum_bitcast_fusion), channel_id=1, source_target_pairs={{0,32},{32,0},{1,33},{33,1},{2,34},{34,2},{3,35},{35,3},{4,36},{36... | collective-permute-start | bytes 387080 | tf_op jit(solution)/shard_map/ppermute | solution.py:23
  9.3 7.5 %collective-permute-start.1 = (bf16[1,126,512]{2,1,0:T(8,128)(2,1)S(1)}, bf16[1,126,512]{2,1,0:T(8,128)(2,1)S(1)}, u32[]{:S(2)}, u32[]{:S(2)}) collective-permute-start(bf16[1,126,512]{2,1,0:T(8,128)(2,1)S(1)} %maximum_bitcast_fusion), channel_id=1, source_target_pairs={{0,64},{64,0},{128,192},{192,128},{256,320},{320,256},{384,448},{4... | collective-permute-start | bytes 387080 | tf_op jit(solution)/shard_map/ppermute | solution.py:19
  16.7 19.7 %collective-permute-start.4 = (bf16[1,126,512]{2,1,0:T(8,128)(2,1)S(1)}, bf16[1,126,512]{2,1,0:T(8,128)(2,1)S(1)}, u32[]{:S(2)}, u32[]{:S(2)}) collective-permute-start(bf16[1,126,512]{2,1,0:T(8,128)(2,1)S(1)} %collective-permute-done.one), channel_id=1, source_target_pairs={{0,64},{64,0},{128,192},{192,128},{256,320},{320,256},{384,448},{4... | collective-permute-start | bytes 387080 | tf_op jit(solution)/shard_map/ppermute | solution.py:19
  20.4 17.9 %collective-permute-start.2 = (bf16[2,126,512]{2,1,0:T(8,128)(2,1)S(1)}, bf16[2,126,512]{2,1,0:T(8,128)(2,1)S(1)}, u32[]{:S(2)}, u32[]{:S(2)}) collective-permute-start(bf16[2,126,512]{2,1,0:T(8,128)(2,1)S(1)} %pad_maximum_fusion.refs_2_), channel_id=1, source_target_pairs={{0,448},{64,128},{128,64},{192,256},{256,192},{320,384},{384,320},... | collective-permute-start | bytes 774152 | tf_op jit(solution)/shard_map/ppermute | solution.py:19
  29.6 30.9 %all-to-all-start = ((bf16[16,64,512]{2,1,0:T(8,128)(2,1)}), bf16[16,64,512]{2,1,0:T(8,128)(2,1)S(1)}, u32[]{:S(2)}, u32[]{:S(2)}) async-start(bf16[16,64,512]{2,1,0:T(8,128)(2,1)} %get-tuple-element.62), calls=%async_computation | async-start | bytes 2097152 | tf_op jit(solution)/shard_map/all_to_all | solution.py:235
  36.4 9.5 %collective-permute-start.5 = (bf16[2,126,512]{2,1,0:T(8,128)(2,1)S(1)}, bf16[2,126,512]{2,1,0:T(8,128)(2,1)S(1)}, u32[]{:S(2)}, u32[]{:S(2)}) collective-permute-start(bf16[2,126,512]{2,1,0:T(8,128)(2,1)S(1)} %shard_map.119.refs_2_), channel_id=1, source_target_pairs={{0,448},{64,128},{128,64},{192,256},{256,192},{320,384},{384,320},... | collective-permute-start | bytes 774152 | tf_op jit(solution)/shard_map/ppermute | solution.py:19
  38.4 8.3 %collective-permute-start.3 = (bf16[2,126,512]{2,1,0:T(8,128)(2,1)S(1)}, bf16[2,126,512]{2,1,0:T(8,128)(2,1)S(1)}, u32[]{:S(2)}, u32[]{:S(2)}) collective-permute-start(bf16[2,126,512]{2,1,0:T(8,128)(2,1)S(1)} %collective-permute-done.2.refs_3_), channel_id=1, source_target_pairs={{0,64},{64,0},{128,192},{192,128},{256,320},{320,256},{384,448},{4... | collective-permute-start | bytes 774152 | tf_op jit(solution)/shard_map/ppermute | solution.py:19
  46.6 9.5 %collective-permute-start.6 = (bf16[2,126,512]{2,1,0:T(8,128)(2,1)S(1)}, bf16[2,126,512]{2,1,0:T(8,128)(2,1)S(1)}, u32[]{:S(2)}, u32[]{:S(2)}) collective-permute-start(bf16[2,126,512]{2,1,0:T(8,128)(2,1)S(1)} %collective-permute-done.3.refs_4_), channel_id=1, source_target_pairs={{0,448},{64,128},{128,64},{192,256},{256,192},{320,384},{384,320},... | collective-permute-start | bytes 774152 | tf_op jit(solution)/shard_map/ppermute | solution.py:19
  51.8 8.3 %collective-permute-start.7 = (bf16[2,126,512]{2,1,0:T(8,128)(2,1)S(1)}, bf16[2,126,512]{2,1,0:T(8,128)(2,1)S(1)}, u32[]{:S(2)}, u32[]{:S(2)}) collective-permute-start(bf16[2,126,512]{2,1,0:T(8,128)(2,1)S(1)} %collective-permute-done.5.refs_3_), channel_id=1, source_target_pairs={{0,64},{64,0},{128,192},{192,128},{256,320},{320,256},{384,448},{4... | collective-permute-start | bytes 774152 | tf_op jit(solution)/shard_map/ppermute | solution.py:19
  60.4 4.5 %collective-permute-start.8 = (bf16[16,64,512]{2,1,0:T(8,128)(2,1)S(1)}, bf16[16,64,512]{2,1,0:T(8,128)(2,1)S(1)}, u32[]{:S(2)}, u32[]{:S(2)}) collective-permute-start(bf16[16,64,512]{2,1,0:T(8,128)(2,1)S(1)} %all-to-all-done.refs_0_), channel_id=1, source_target_pairs={{0,16},{16,0},{1,17},{17,1},{2,18},{18,2},{3,19},{19,3},{4,20},{20... | collective-permute-start | bytes 3145736 | tf_op jit(solution)/shard_map/ppermute | solution.py:23
  62.4 12.7 %collective-permute-start.9 = (bf16[2,126,512]{2,1,0:T(8,128)(2,1)S(1)}, bf16[2,126,512]{2,1,0:T(8,128)(2,1)S(1)}, u32[]{:S(2)}, u32[]{:S(2)}) collective-permute-start(bf16[2,126,512]{2,1,0:T(8,128)(2,1)S(1)} %collective-permute-done.7.refs_4_), channel_id=1, source_target_pairs={{0,448},{64,128},{128,64},{192,256},{256,192},{320,384},{384,320},... | collective-permute-start | bytes 774152 | tf_op jit(solution)/shard_map/ppermute | solution.py:19
  77.7 11.4 %collective-permute-start.10 = (bf16[2,126,512]{2,1,0:T(8,128)(2,1)S(1)}, bf16[2,126,512]{2,1,0:T(8,128)(2,1)S(1)}, u32[]{:S(2)}, u32[]{:S(2)}) collective-permute-start(bf16[2,126,512]{2,1,0:T(8,128)(2,1)S(1)} %get-tuple-element.73), channel_id=1, source_target_pairs={{0,448},{64,128},{128,64},{192,256},{256,192},{320,384},{384,320},... | collective-permute-start | bytes 774152 | tf_op jit(solution)/shard_map/ppermute | solution.py:19
  82.1 7.1 %collective-permute-start.11 = (bf16[16,64,512]{2,1,0:T(8,128)(2,1)S(1)}, bf16[16,64,512]{2,1,0:T(8,128)(2,1)S(1)}, u32[]{:S(2)}, u32[]{:S(2)}) collective-permute-start(bf16[16,64,512]{2,1,0:T(8,128)(2,1)S(1)} %get-tuple-element.74), channel_id=1, source_target_pairs={{0,16},{16,0},{1,17},{17,1},{2,18},{18,2},{3,19},{19,3},{4,20},{20... | collective-permute-start | bytes 3145736 | tf_op jit(solution)/shard_map/ppermute | solution.py:23
  84.0 15.7 %collective-permute-start.13 = (bf16[2,126,512]{2,1,0:T(8,128)(2,1)S(1)}, bf16[2,126,512]{2,1,0:T(8,128)(2,1)S(1)}, u32[]{:S(2)}, u32[]{:S(2)}) collective-permute-start(bf16[2,126,512]{2,1,0:T(8,128)(2,1)S(1)} %get-tuple-element.76), channel_id=1, source_target_pairs={{0,448},{64,128},{128,64},{192,256},{256,192},{320,384},{384,320},... | collective-permute-start | bytes 774152 | tf_op jit(solution)/shard_map/ppermute | solution.py:19
  89.2 10.5 %collective-permute-start.12 = (bf16[2,126,512]{2,1,0:T(8,128)(2,1)S(1)}, bf16[2,126,512]{2,1,0:T(8,128)(2,1)S(1)}, u32[]{:S(2)}, u32[]{:S(2)}) collective-permute-start(bf16[2,126,512]{2,1,0:T(8,128)(2,1)S(1)} %shard_map.123), channel_id=1, source_target_pairs={{0,64},{64,0},{128,192},{192,128},{256,320},{320,256},{384,448},{4... | collective-permute-start | bytes 774152 | tf_op jit(solution)/shard_map/ppermute | solution.py:19
  92.5 7.4 %copy-start.7 = (bf16[2,126,512]{2,1,0:T(8,128)(2,1)S(1)}, bf16[2,126,512]{2,1,0:T(8,128)(2,1)}, u32[]{:S(2)}) copy-start(bf16[2,126,512]{2,1,0:T(8,128)(2,1)} %copy-done.6) | copy-start | bytes 774148
  92.5 40.4 %all-to-all-start.1 = ((bf16[16,64,512]{2,1,0:T(8,128)(2,1)}), bf16[16,64,512]{2,1,0:T(8,128)(2,1)S(1)}, u32[]{:S(2)}, u32[]{:S(2)}) async-start(bf16[16,64,512]{2,1,0:T(8,128)(2,1)} %add_convert_fusion), calls=%async_computation.1 | async-start | bytes 2097152 | tf_op jit(solution)/shard_map/all_to_all | solution.py:258
  99.8 13.7 %copy-start.5 = (bf16[2,126,512]{2,1,0:T(8,128)(2,1)S(1)}, bf16[2,126,512]{2,1,0:T(8,128)(2,1)}, u32[]{:S(2)}) copy-start(bf16[2,126,512]{2,1,0:T(8,128)(2,1)} %copy-done.4) | copy-start | bytes 774148
  99.9 9.2 %collective-permute-start.15 = (bf16[2,126,512]{2,1,0:T(8,128)(2,1)S(1)}, bf16[2,126,512]{2,1,0:T(8,128)(2,1)S(1)}, u32[]{:S(2)}, u32[]{:S(2)}) collective-permute-start(bf16[2,126,512]{2,1,0:T(8,128)(2,1)S(1)} %shard_map.125), channel_id=1, source_target_pairs={{0,64},{64,0},{128,192},{192,128},{256,320},{320,256},{384,448},{4... | collective-permute-start | bytes 774152 | tf_op jit(solution)/shard_map/ppermute | solution.py:19
  103.8 9.6 %collective-permute-start.14 = (bf16[2,126,512]{2,1,0:T(8,128)(2,1)S(1)}, bf16[2,126,512]{2,1,0:T(8,128)(2,1)S(1)}, u32[]{:S(2)}, u32[]{:S(2)}) collective-permute-start(bf16[2,126,512]{2,1,0:T(8,128)(2,1)S(1)} %shard_map.124), channel_id=1, source_target_pairs={{0,448},{64,128},{128,64},{192,256},{256,192},{320,384},{384,320},... | collective-permute-start | bytes 774152 | tf_op jit(solution)/shard_map/ppermute | solution.py:19
  113.6 12.0 %collective-permute-start.17 = (bf16[2,126,512]{2,1,0:T(8,128)(2,1)S(1)}, bf16[2,126,512]{2,1,0:T(8,128)(2,1)S(1)}, u32[]{:S(2)}, u32[]{:S(2)}) collective-permute-start(bf16[2,126,512]{2,1,0:T(8,128)(2,1)S(1)} %shard_map.127), channel_id=1, source_target_pairs={{0,448},{64,128},{128,64},{192,256},{256,192},{320,384},{384,320},... | collective-permute-start | bytes 774152 | tf_op jit(solution)/shard_map/ppermute | solution.py:19
  118.7 6.9 %collective-permute-start.16 = (bf16[1,126,512]{2,1,0:T(8,128)(2,1)S(1)}, bf16[1,126,512]{2,1,0:T(8,128)(2,1)S(1)}, u32[]{:S(2)}, u32[]{:S(2)}) collective-permute-start(bf16[1,126,512]{2,1,0:T(8,128)(2,1)S(1)} %get-tuple-element.86), channel_id=1, source_target_pairs={{0,64},{64,0},{128,192},{192,128},{256,320},{320,256},{384,448},{4... | collective-permute-start | bytes 387080 | tf_op jit(solution)/shard_map/ppermute | solution.py:19
  125.6 10.9 %collective-permute-start.18 = (bf16[1,126,512]{2,1,0:T(8,128)(2,1)S(1)}, bf16[1,126,512]{2,1,0:T(8,128)(2,1)S(1)}, u32[]{:S(2)}, u32[]{:S(2)}) collective-permute-start(bf16[1,126,512]{2,1,0:T(8,128)(2,1)S(1)} %shard_map.128), channel_id=1, source_target_pairs={{0,32},{32,0},{1,33},{33,1},{2,34},{34,2},{3,35},{35,3},{4,36},{36... | collective-permute-start | bytes 387080 | tf_op jit(solution)/shard_map/ppermute | solution.py:23
  130.8 7.0 %collective-permute-start.19 = (bf16[1,126,512]{2,1,0:T(8,128)(2,1)S(1)}, bf16[1,126,512]{2,1,0:T(8,128)(2,1)S(1)}, u32[]{:S(2)}, u32[]{:S(2)}) collective-permute-start(bf16[1,126,512]{2,1,0:T(8,128)(2,1)S(1)} %get-tuple-element.103), channel_id=1, source_target_pairs={{0,64},{64,0},{128,192},{192,128},{256,320},{320,256},{384,448},{4... | collective-permute-start | bytes 387080 | tf_op jit(solution)/shard_map/ppermute | solution.py:19
  (6 other events, 14.0 us)

commit v5 on v4

--- a/solution.py
+++ b/solution.py
@@ -239,7 +239,6 @@
     far = [pair(other, far_got, 4 * 10**10)]
     near.append(swap_z(near[1], 0))
     far.append(swap_z(far[0], 1))
-    near[2], far[1] = together((near[2], far[1]))
     near.append(swap_z(near[2], 1))
     far.append(swap_z(far[1], 0))
     near[3], far[2], mine = together((near[3], far[2], mine))

time: 139 us -> 139 us (level)
  starting transfers between devices: 88.2 us -> 86.2 us
    ppermute x16, starting transfers between devices: 57.4 us -> 54.4 us  [swap_z(): return lax.ppermute(rows, 'z', pairs)]
    all_to_all x1, waiting for transfers between devices: 0.39 us -> 2.63 us  [shards(): mine = lax.all_to_all(send, ('x', 'yl'), 0, 0, tiled=True)]
where the time goes in v5:
time: 139 us; the launch traced here: 138 us
  starting transfers between devices  86.2 us (62%)
  waiting for transfers between devices  30.6 us (22%)
  Pallas kernels  16.9 us (12%)
  other arithmetic  2.24 us (2%)
    ppermute x16, starting transfers between devices, swap_z(): return lax.ppermute(rows, 'z', pairs)  54.4 us
    ppermute x16, waiting for transfers between devices, swap_z(): return lax.ppermute(rows, 'z', pairs)  25.6 us
    ppermute x4, starting transfers between devices, swap(): return lax.ppermute(rows, axis, [(0, 1), (1, 0)])  16.8 us
    pallas_call x3, Pallas kernels, expert_call(): got = call(mine, theirs, *pieces, *sums)  11.9 us
    all_to_all x1, starting transfers between devices, shards(): lax.all_to_all(add(local, rest).astype(BF16), ('x', 'yl'), 0, 0, tiled=True)  8.23 us
    all_to_all x1, starting transfers between devices, shards(): mine = lax.all_to_all(send, ('x', 'yl'), 0, 0, tiled=True)  6.84 us
  transfers between devices with their start and end apart: 22, of which 12 were waited for; matrix products, arithmetic and copies ran while one was open for 1% of the time, Pallas kernels for 10%

profile of v5, /device:TPU:2, one launch (start us, length us, event | category | flops | bytes accessed | tf_op | source)
XLA Modules:
  0.0 137.6 jit_solution(4288817444146981052)
XLA Ops:
  1.5 7.7 %collective-permute-start = (bf16[1,126,512]{2,1,0:T(8,128)(2,1)S(1)}, bf16[1,126,512]{2,1,0:T(8,128)(2,1)S(1)}, u32[]{:S(2)}, u32[]{:S(2)}) collective-permute-start(bf16[1,126,512]{2,1,0:T(8,128)(2,1)S(1)} %maximum_bitcast_fusion), channel_id=1, source_target_pairs={{0,32},{32,0},{1,33},{33,1},{2,34},{34,2},{3,35},{35,3},{4,36},{36... | collective-permute-start | bytes 387080 | tf_op jit(solution)/shard_map/ppermute | solution.py:23
  9.3 4.3 %collective-permute-start.1 = (bf16[1,126,512]{2,1,0:T(8,128)(2,1)S(1)}, bf16[1,126,512]{2,1,0:T(8,128)(2,1)S(1)}, u32[]{:S(2)}, u32[]{:S(2)}) collective-permute-start(bf16[1,126,512]{2,1,0:T(8,128)(2,1)S(1)} %maximum_bitcast_fusion), channel_id=1, source_target_pairs={{0,64},{64,0},{128,192},{192,128},{256,320},{320,256},{384,448},{4... | collective-permute-start | bytes 387080 | tf_op jit(solution)/shard_map/ppermute | solution.py:19
  13.5 2.6 %shard_map.118 = (bf16[16,64,512]{2,1,0:T(8,128)(2,1)}, bf16[512,128]{1,0:T(8,128)(2,1)}, bf16[512,128]{1,0:T(8,128)(2,1)}) custom-call(bf16[128,512]{1,0:T(8,128)(2,1)} %latent.1, bf16[128,512]{1,0:T(8,128)(2,1)} %cotangent.3, s32[2,128]{1,0:T(2,128)} %bitcast.16, f32[2,128]{1,0:T(2,128)} %bitcast.11), custom_call_target="tpu_custom_call" | custom-call | bytes 1048576 | tf_op jit(solution)/shard_map/pallas_call | solution.py:228
  16.7 3.6 %collective-permute-start.5 = (bf16[1,126,512]{2,1,0:T(8,128)(2,1)S(1)}, bf16[1,126,512]{2,1,0:T(8,128)(2,1)S(1)}, u32[]{:S(2)}, u32[]{:S(2)}) collective-permute-start(bf16[1,126,512]{2,1,0:T(8,128)(2,1)S(1)} %collective-permute-done.one), channel_id=1, source_target_pairs={{0,64},{64,0},{128,192},{192,128},{256,320},{320,256},{384,448},{4... | collective-permute-start | bytes 387080 | tf_op jit(solution)/shard_map/ppermute | solution.py:19
  20.4 9.1 %collective-permute-start.2 = (bf16[2,126,512]{2,1,0:T(8,128)(2,1)S(1)}, bf16[2,126,512]{2,1,0:T(8,128)(2,1)S(1)}, u32[]{:S(2)}, u32[]{:S(2)}) collective-permute-start(bf16[2,126,512]{2,1,0:T(8,128)(2,1)S(1)} %pad_maximum_fusion.refs_2_), channel_id=1, source_target_pairs={{0,448},{64,128},{128,64},{192,256},{256,192},{320,384},{384,320},... | collective-permute-start | bytes 774152 | tf_op jit(solution)/shard_map/ppermute | solution.py:19
  29.6 6.8 %all-to-all-start = ((bf16[16,64,512]{2,1,0:T(8,128)(2,1)}), bf16[16,64,512]{2,1,0:T(8,128)(2,1)S(1)}, u32[]{:S(2)}, u32[]{:S(2)}) async-start(bf16[16,64,512]{2,1,0:T(8,128)(2,1)} %get-tuple-element.58), calls=%async_computation | async-start | bytes 2097152 | tf_op jit(solution)/shard_map/all_to_all | solution.py:235
  40.3 5.6 %collective-permute-done.6.refs_3_ = bf16[2,126,512]{2,1,0:T(8,128)(2,1)S(1)} collective-permute-done((bf16[2,126,512]{2,1,0:T(8,128)(2,1)S(1)}, bf16[2,126,512]{2,1,0:T(8,128)(2,1)S(1)}, u32[]{:S(2)}, u32[]{:S(2)}) %collective-permute-start.6) | collective-permute-done | bytes 258080 | tf_op jit(solution)/shard_map/ppermute | solution.py:19
  47.8 5.6 %collective-permute-start.4 = (bf16[2,126,512]{2,1,0:T(8,128)(2,1)S(1)}, bf16[2,126,512]{2,1,0:T(8,128)(2,1)S(1)}, u32[]{:S(2)}, u32[]{:S(2)}) collective-permute-start(bf16[2,126,512]{2,1,0:T(8,128)(2,1)S(1)} %collective-permute-done.3.refs_4_), channel_id=1, source_target_pairs={{0,448},{64,128},{128,64},{192,256},{256,192},{320,384},{384,320},... | collective-permute-start | bytes 774152 | tf_op jit(solution)/shard_map/ppermute | solution.py:19
  54.2 3.6 %collective-permute-done.4.refs_5_ = bf16[2,126,512]{2,1,0:T(8,128)(2,1)S(1)} collective-permute-done((bf16[2,126,512]{2,1,0:T(8,128)(2,1)S(1)}, bf16[2,126,512]{2,1,0:T(8,128)(2,1)S(1)}, u32[]{:S(2)}, u32[]{:S(2)}) %collective-permute-start.4) | collective-permute-done | bytes 258080 | tf_op jit(solution)/shard_map/ppermute | solution.py:19
  57.8 2.6 %all-to-all-done.refs_0_ = bf16[16,64,512]{2,1,0:T(8,128)(2,1)S(1)} async-done(((bf16[16,64,512]{2,1,0:T(8,128)(2,1)}), bf16[16,64,512]{2,1,0:T(8,128)(2,1)S(1)}, u32[]{:S(2)}, u32[]{:S(2)}) %all-to-all-start) | async-done | bytes 1048608 | tf_op jit(solution)/shard_map/all_to_all | solution.py:235
  62.4 2.5 %collective-permute-start.9 = (bf16[2,126,512]{2,1,0:T(8,128)(2,1)S(1)}, bf16[2,126,512]{2,1,0:T(8,128)(2,1)S(1)}, u32[]{:S(2)}, u32[]{:S(2)}) collective-permute-start(bf16[2,126,512]{2,1,0:T(8,128)(2,1)S(1)} %collective-permute-done.7.refs_4_), channel_id=1, source_target_pairs={{0,448},{64,128},{128,64},{192,256},{256,192},{320,384},{384,320},... | collective-permute-start | bytes 774152 | tf_op jit(solution)/shard_map/ppermute | solution.py:19
  65.0 4.8 %shard_map.120 = (bf16[2,126,512]{2,1,0:T(8,128)(2,1)S(1)}, bf16[2,126,512]{2,1,0:T(8,128)(2,1)S(1)}, bf16[2,126,512]{2,1,0:T(8,128)(2,1)S(1)}, bf16[2,126,512]{...) custom-call(bf16[16,64,512]{2,1,0:T(8,128)(2,1)S(1)} %all-to-all-done.refs_0_, ...), custom_call_target="tpu_custom_call" | custom-call | flops 3623878656 | bytes 1048576 | tf_op jit(solution)/shard_map/pallas_call | solution.py:170
  70.5 4.5 %shard_map.121 = (bf16[2,126,512]{2,1,0:T(8,128)(2,1)S(1)}, bf16[2,126,512]{2,1,0:T(8,128)(2,1)S(1)}, bf16[2,126,512]{2,1,0:T(8,128)(2,1)S(1)}, f32[16,64,512]{2,1,0:T(8,128)S(1)}, f32[16,64,512]{2,1,0:T(8,128)S(1)}) custom-call(bf16[16,64,512]{2,1,0:T(8,128)(2,1)S(1)} %all-to-all-done.refs_0_, bf16[16,64,512]{2,1,0:T(8,128)(2,1)S(1)} %collective-permute-done.8.refs_1_, ...), custom_call_target="tpu_custom_call" | custom-call | flops 2717908992 | bytes 1048576 | tf_op jit(solution)/shard_map/pallas_call | solution.py:170
  75.0 2.6 %shard_map.122 = (bf16[2,126,512]{2,1,0:T(8,128)(2,1)S(1)}, f32[16,64,512]{2,1,0:T(8,128)S(1)}, bf16[16,64,512]{2,1,0:T(8,128)(2,1)S(1)}) custom-call(bf16[16,64,512]{2,1,0:T(8,128)(2,1)S(1)} %all-to-all-done.refs_0_, bf16[16,64,512]{2,1,0:T(8,128)(2,1)S(1)} %collective-permute-done.8.refs_1_, bf16[2,126,512]{2,1,0:T(8,128)(2,1)S(1)} %collective-permute-done.9.refs_2_, ...), custom_call_target="tpu_custom_call" | custom-call | flops 905969664 | bytes 1048576 | tf_op jit(solution)/shard_map/pallas_call | solution.py:170
  77.7 4.4 %collective-permute-start.10 = (bf16[2,126,512]{2,1,0:T(8,128)(2,1)S(1)}, bf16[2,126,512]{2,1,0:T(8,128)(2,1)S(1)}, u32[]{:S(2)}, u32[]{:S(2)}) collective-permute-start(bf16[2,126,512]{2,1,0:T(8,128)(2,1)S(1)} %get-tuple-element.69), channel_id=1, source_target_pairs={{0,448},{64,128},{128,64},{192,256},{256,192},{320,384},{384,320},... | collective-permute-start | bytes 774152 | tf_op jit(solution)/shard_map/ppermute | solution.py:19
  84.0 2.6 %collective-permute-start.13 = (bf16[2,126,512]{2,1,0:T(8,128)(2,1)S(1)}, bf16[2,126,512]{2,1,0:T(8,128)(2,1)S(1)}, u32[]{:S(2)}, u32[]{:S(2)}) collective-permute-start(bf16[2,126,512]{2,1,0:T(8,128)(2,1)S(1)} %get-tuple-element.72), channel_id=1, source_target_pairs={{0,448},{64,128},{128,64},{192,256},{256,192},{320,384},{384,320},... | collective-permute-start | bytes 774152 | tf_op jit(solution)/shard_map/ppermute | solution.py:19
  86.7 2.4 %collective-permute-done.10.two = bf16[2,126,512]{2,1,0:T(8,128)(2,1)S(1)} collective-permute-done((bf16[2,126,512]{2,1,0:T(8,128)(2,1)S(1)}, bf16[2,126,512]{2,1,0:T(8,128)(2,1)S(1)}, u32[]{:S(2)}, u32[]{:S(2)}) %collective-permute-start.10) | collective-permute-done | bytes 258080 | tf_op jit(solution)/shard_map/ppermute | solution.py:19
  92.5 8.2 %all-to-all-start.1 = ((bf16[16,64,512]{2,1,0:T(8,128)(2,1)}), bf16[16,64,512]{2,1,0:T(8,128)(2,1)S(1)}, u32[]{:S(2)}, u32[]{:S(2)}) async-start(bf16[16,64,512]{2,1,0:T(8,128)(2,1)} %add_convert_fusion), calls=%async_computation.1 | async-start | bytes 2097152 | tf_op jit(solution)/shard_map/all_to_all | solution.py:257
  100.9 3.9 %collective-permute-start.15 = (bf16[2,126,512]{2,1,0:T(8,128)(2,1)S(1)}, bf16[2,126,512]{2,1,0:T(8,128)(2,1)S(1)}, u32[]{:S(2)}, u32[]{:S(2)}) collective-permute-start(bf16[2,126,512]{2,1,0:T(8,128)(2,1)S(1)} %shard_map.125), channel_id=1, source_target_pairs={{0,64},{64,0},{128,192},{192,128},{256,320},{320,256},{384,448},{4... | collective-permute-start | bytes 774152 | tf_op jit(solution)/shard_map/ppermute | solution.py:19
  104.8 3.3 %collective-permute-start.14 = (bf16[2,126,512]{2,1,0:T(8,128)(2,1)S(1)}, bf16[2,126,512]{2,1,0:T(8,128)(2,1)S(1)}, u32[]{:S(2)}, u32[]{:S(2)}) collective-permute-start(bf16[2,126,512]{2,1,0:T(8,128)(2,1)S(1)} %shard_map.124), channel_id=1, source_target_pairs={{0,448},{64,128},{128,64},{192,256},{256,192},{320,384},{384,320},... | collective-permute-start | bytes 774152 | tf_op jit(solution)/shard_map/ppermute | solution.py:19
  109.2 5.0 %collective-permute-done.14.two = bf16[2,126,512]{2,1,0:T(8,128)(2,1)S(1)} collective-permute-done((bf16[2,126,512]{2,1,0:T(8,128)(2,1)S(1)}, bf16[2,126,512]{2,1,0:T(8,128)(2,1)S(1)}, u32[]{:S(2)}, u32[]{:S(2)}) %collective-permute-start.14) | collective-permute-done | bytes 258080 | tf_op jit(solution)/shard_map/ppermute | solution.py:19
  114.4 3.3 %collective-permute-start.17 = (bf16[2,126,512]{2,1,0:T(8,128)(2,1)S(1)}, bf16[2,126,512]{2,1,0:T(8,128)(2,1)S(1)}, u32[]{:S(2)}, u32[]{:S(2)}) collective-permute-start(bf16[2,126,512]{2,1,0:T(8,128)(2,1)S(1)} %shard_map.127), channel_id=1, source_target_pairs={{0,448},{64,128},{128,64},{192,256},{256,192},{320,384},{384,320},... | collective-permute-start | bytes 774152 | tf_op jit(solution)/shard_map/ppermute | solution.py:19
  119.6 4.9 %collective-permute-done.16.two = bf16[1,126,512]{2,1,0:T(8,128)(2,1)S(1)} collective-permute-done((bf16[1,126,512]{2,1,0:T(8,128)(2,1)S(1)}, bf16[1,126,512]{2,1,0:T(8,128)(2,1)S(1)}, u32[]{:S(2)}, u32[]{:S(2)}) %collective-permute-start.16) | collective-permute-done | bytes 129056 | tf_op jit(solution)/shard_map/ppermute | solution.py:19
  124.6 5.2 %collective-permute-start.18 = (bf16[1,126,512]{2,1,0:T(8,128)(2,1)S(1)}, bf16[1,126,512]{2,1,0:T(8,128)(2,1)S(1)}, u32[]{:S(2)}, u32[]{:S(2)}) collective-permute-start(bf16[1,126,512]{2,1,0:T(8,128)(2,1)S(1)} %shard_map.128), channel_id=1, source_target_pairs={{0,32},{32,0},{1,33},{33,1},{2,34},{34,2},{3,35},{35,3},{4,36},{36... | collective-permute-start | bytes 387080 | tf_op jit(solution)/shard_map/ppermute | solution.py:23
  (53 shorter events, 27.1 us)
Async XLA Ops:
  1.5 14.6 %collective-permute-start = (bf16[1,126,512]{2,1,0:T(8,128)(2,1)S(1)}, bf16[1,126,512]{2,1,0:T(8,128)(2,1)S(1)}, u32[]{:S(2)}, u32[]{:S(2)}) collective-permute-start(bf16[1,126,512]{2,1,0:T(8,128)(2,1)S(1)} %maximum_bitcast_fusion), channel_id=1, source_target_pairs={{0,32},{32,0},{1,33},{33,1},{2,34},{34,2},{3,35},{35,3},{4,36},{36... | collective-permute-start | bytes 387080 | tf_op jit(solution)/shard_map/ppermute | solution.py:23
  9.3 7.5 %collective-permute-start.1 = (bf16[1,126,512]{2,1,0:T(8,128)(2,1)S(1)}, bf16[1,126,512]{2,1,0:T(8,128)(2,1)S(1)}, u32[]{:S(2)}, u32[]{:S(2)}) collective-permute-start(bf16[1,126,512]{2,1,0:T(8,128)(2,1)S(1)} %maximum_bitcast_fusion), channel_id=1, source_target_pairs={{0,64},{64,0},{128,192},{192,128},{256,320},{320,256},{384,448},{4... | collective-permute-start | bytes 387080 | tf_op jit(solution)/shard_map/ppermute | solution.py:19
  16.7 19.7 %collective-permute-start.5 = (bf16[1,126,512]{2,1,0:T(8,128)(2,1)S(1)}, bf16[1,126,512]{2,1,0:T(8,128)(2,1)S(1)}, u32[]{:S(2)}, u32[]{:S(2)}) collective-permute-start(bf16[1,126,512]{2,1,0:T(8,128)(2,1)S(1)} %collective-permute-done.one), channel_id=1, source_target_pairs={{0,64},{64,0},{128,192},{192,128},{256,320},{320,256},{384,448},{4... | collective-permute-start | bytes 387080 | tf_op jit(solution)/shard_map/ppermute | solution.py:19
  20.4 17.9 %collective-permute-start.2 = (bf16[2,126,512]{2,1,0:T(8,128)(2,1)S(1)}, bf16[2,126,512]{2,1,0:T(8,128)(2,1)S(1)}, u32[]{:S(2)}, u32[]{:S(2)}) collective-permute-start(bf16[2,126,512]{2,1,0:T(8,128)(2,1)S(1)} %pad_maximum_fusion.refs_2_), channel_id=1, source_target_pairs={{0,448},{64,128},{128,64},{192,256},{256,192},{320,384},{384,320},... | collective-permute-start | bytes 774152 | tf_op jit(solution)/shard_map/ppermute | solution.py:19
  29.6 30.9 %all-to-all-start = ((bf16[16,64,512]{2,1,0:T(8,128)(2,1)}), bf16[16,64,512]{2,1,0:T(8,128)(2,1)S(1)}, u32[]{:S(2)}, u32[]{:S(2)}) async-start(bf16[16,64,512]{2,1,0:T(8,128)(2,1)} %get-tuple-element.58), calls=%async_computation | async-start | bytes 2097152 | tf_op jit(solution)/shard_map/all_to_all | solution.py:235
  36.4 9.5 %collective-permute-start.6 = (bf16[2,126,512]{2,1,0:T(8,128)(2,1)S(1)}, bf16[2,126,512]{2,1,0:T(8,128)(2,1)S(1)}, u32[]{:S(2)}, u32[]{:S(2)}) collective-permute-start(bf16[2,126,512]{2,1,0:T(8,128)(2,1)S(1)} %shard_map.119.refs_2_), channel_id=1, source_target_pairs={{0,448},{64,128},{128,64},{192,256},{256,192},{320,384},{384,320},... | collective-permute-start | bytes 774152 | tf_op jit(solution)/shard_map/ppermute | solution.py:19
  38.4 9.5 %collective-permute-start.3 = (bf16[2,126,512]{2,1,0:T(8,128)(2,1)S(1)}, bf16[2,126,512]{2,1,0:T(8,128)(2,1)S(1)}, u32[]{:S(2)}, u32[]{:S(2)}) collective-permute-start(bf16[2,126,512]{2,1,0:T(8,128)(2,1)S(1)} %collective-permute-done.2.refs_3_), channel_id=1, source_target_pairs={{0,64},{64,0},{128,192},{192,128},{256,320},{320,256},{384,448},{4... | collective-permute-start | bytes 774152 | tf_op jit(solution)/shard_map/ppermute | solution.py:19
  45.9 8.3 %collective-permute-start.7 = (bf16[2,126,512]{2,1,0:T(8,128)(2,1)S(1)}, bf16[2,126,512]{2,1,0:T(8,128)(2,1)S(1)}, u32[]{:S(2)}, u32[]{:S(2)}) collective-permute-start(bf16[2,126,512]{2,1,0:T(8,128)(2,1)S(1)} %collective-permute-done.6.refs_3_), channel_id=1, source_target_pairs={{0,64},{64,0},{128,192},{192,128},{256,320},{320,256},{384,448},{4... | collective-permute-start | bytes 774152 | tf_op jit(solution)/shard_map/ppermute | solution.py:19
  47.8 10.0 %collective-permute-start.4 = (bf16[2,126,512]{2,1,0:T(8,128)(2,1)S(1)}, bf16[2,126,512]{2,1,0:T(8,128)(2,1)S(1)}, u32[]{:S(2)}, u32[]{:S(2)}) collective-permute-start(bf16[2,126,512]{2,1,0:T(8,128)(2,1)S(1)} %collective-permute-done.3.refs_4_), channel_id=1, source_target_pairs={{0,448},{64,128},{128,64},{192,256},{256,192},{320,384},{384,320},... | collective-permute-start | bytes 774152 | tf_op jit(solution)/shard_map/ppermute | solution.py:19
  60.4 4.5 %collective-permute-start.8 = (bf16[16,64,512]{2,1,0:T(8,128)(2,1)S(1)}, bf16[16,64,512]{2,1,0:T(8,128)(2,1)S(1)}, u32[]{:S(2)}, u32[]{:S(2)}) collective-permute-start(bf16[16,64,512]{2,1,0:T(8,128)(2,1)S(1)} %all-to-all-done.refs_0_), channel_id=1, source_target_pairs={{0,16},{16,0},{1,17},{17,1},{2,18},{18,2},{3,19},{19,3},{4,20},{20... | collective-permute-start | bytes 3145736 | tf_op jit(solution)/shard_map/ppermute | solution.py:23
  62.4 12.7 %collective-permute-start.9 = (bf16[2,126,512]{2,1,0:T(8,128)(2,1)S(1)}, bf16[2,126,512]{2,1,0:T(8,128)(2,1)S(1)}, u32[]{:S(2)}, u32[]{:S(2)}) collective-permute-start(bf16[2,126,512]{2,1,0:T(8,128)(2,1)S(1)} %collective-permute-done.7.refs_4_), channel_id=1, source_target_pairs={{0,448},{64,128},{128,64},{192,256},{256,192},{320,384},{384,320},... | collective-permute-start | bytes 774152 | tf_op jit(solution)/shard_map/ppermute | solution.py:19
  77.7 11.4 %collective-permute-start.10 = (bf16[2,126,512]{2,1,0:T(8,128)(2,1)S(1)}, bf16[2,126,512]{2,1,0:T(8,128)(2,1)S(1)}, u32[]{:S(2)}, u32[]{:S(2)}) collective-permute-start(bf16[2,126,512]{2,1,0:T(8,128)(2,1)S(1)} %get-tuple-element.69), channel_id=1, source_target_pairs={{0,448},{64,128},{128,64},{192,256},{256,192},{320,384},{384,320},... | collective-permute-start | bytes 774152 | tf_op jit(solution)/shard_map/ppermute | solution.py:19
  82.1 7.1 %collective-permute-start.11 = (bf16[16,64,512]{2,1,0:T(8,128)(2,1)S(1)}, bf16[16,64,512]{2,1,0:T(8,128)(2,1)S(1)}, u32[]{:S(2)}, u32[]{:S(2)}) collective-permute-start(bf16[16,64,512]{2,1,0:T(8,128)(2,1)S(1)} %get-tuple-element.70), channel_id=1, source_target_pairs={{0,16},{16,0},{1,17},{17,1},{2,18},{18,2},{3,19},{19,3},{4,20},{20... | collective-permute-start | bytes 3145736 | tf_op jit(solution)/shard_map/ppermute | solution.py:23
  84.0 16.6 %collective-permute-start.13 = (bf16[2,126,512]{2,1,0:T(8,128)(2,1)S(1)}, bf16[2,126,512]{2,1,0:T(8,128)(2,1)S(1)}, u32[]{:S(2)}, u32[]{:S(2)}) collective-permute-start(bf16[2,126,512]{2,1,0:T(8,128)(2,1)S(1)} %get-tuple-element.72), channel_id=1, source_target_pairs={{0,448},{64,128},{128,64},{192,256},{256,192},{320,384},{384,320},... | collective-permute-start | bytes 774152 | tf_op jit(solution)/shard_map/ppermute | solution.py:19
  89.2 11.5 %collective-permute-start.12 = (bf16[2,126,512]{2,1,0:T(8,128)(2,1)S(1)}, bf16[2,126,512]{2,1,0:T(8,128)(2,1)S(1)}, u32[]{:S(2)}, u32[]{:S(2)}) collective-permute-start(bf16[2,126,512]{2,1,0:T(8,128)(2,1)S(1)} %shard_map.123), channel_id=1, source_target_pairs={{0,64},{64,0},{128,192},{192,128},{256,320},{320,256},{384,448},{4... | collective-permute-start | bytes 774152 | tf_op jit(solution)/shard_map/ppermute | solution.py:19
  92.5 8.3 %copy-start.7 = (bf16[2,126,512]{2,1,0:T(8,128)(2,1)S(1)}, bf16[2,126,512]{2,1,0:T(8,128)(2,1)}, u32[]{:S(2)}) copy-start(bf16[2,126,512]{2,1,0:T(8,128)(2,1)} %copy-done.6) | copy-start | bytes 774148
  92.5 39.5 %all-to-all-start.1 = ((bf16[16,64,512]{2,1,0:T(8,128)(2,1)}), bf16[16,64,512]{2,1,0:T(8,128)(2,1)S(1)}, u32[]{:S(2)}, u32[]{:S(2)}) async-start(bf16[16,64,512]{2,1,0:T(8,128)(2,1)} %add_convert_fusion), calls=%async_computation.1 | async-start | bytes 2097152 | tf_op jit(solution)/shard_map/all_to_all | solution.py:257
  100.8 13.6 %copy-start.5 = (bf16[2,126,512]{2,1,0:T(8,128)(2,1)S(1)}, bf16[2,126,512]{2,1,0:T(8,128)(2,1)}, u32[]{:S(2)}) copy-start(bf16[2,126,512]{2,1,0:T(8,128)(2,1)} %copy-done.4) | copy-start | bytes 774148
  100.9 8.4 %collective-permute-start.15 = (bf16[2,126,512]{2,1,0:T(8,128)(2,1)S(1)}, bf16[2,126,512]{2,1,0:T(8,128)(2,1)S(1)}, u32[]{:S(2)}, u32[]{:S(2)}) collective-permute-start(bf16[2,126,512]{2,1,0:T(8,128)(2,1)S(1)} %shard_map.125), channel_id=1, source_target_pairs={{0,64},{64,0},{128,192},{192,128},{256,320},{320,256},{384,448},{4... | collective-permute-start | bytes 774152 | tf_op jit(solution)/shard_map/ppermute | solution.py:19
  104.8 9.5 %collective-permute-start.14 = (bf16[2,126,512]{2,1,0:T(8,128)(2,1)S(1)}, bf16[2,126,512]{2,1,0:T(8,128)(2,1)S(1)}, u32[]{:S(2)}, u32[]{:S(2)}) collective-permute-start(bf16[2,126,512]{2,1,0:T(8,128)(2,1)S(1)} %shard_map.124), channel_id=1, source_target_pairs={{0,448},{64,128},{128,64},{192,256},{256,192},{320,384},{384,320},... | collective-permute-start | bytes 774152 | tf_op jit(solution)/shard_map/ppermute | solution.py:19
  114.4 10.2 %collective-permute-start.17 = (bf16[2,126,512]{2,1,0:T(8,128)(2,1)S(1)}, bf16[2,126,512]{2,1,0:T(8,128)(2,1)S(1)}, u32[]{:S(2)}, u32[]{:S(2)}) collective-permute-start(bf16[2,126,512]{2,1,0:T(8,128)(2,1)S(1)} %shard_map.127), channel_id=1, source_target_pairs={{0,448},{64,128},{128,64},{192,256},{256,192},{320,384},{384,320},... | collective-permute-start | bytes 774152 | tf_op jit(solution)/shard_map/ppermute | solution.py:19
  117.7 6.9 %collective-permute-start.16 = (bf16[1,126,512]{2,1,0:T(8,128)(2,1)S(1)}, bf16[1,126,512]{2,1,0:T(8,128)(2,1)S(1)}, u32[]{:S(2)}, u32[]{:S(2)}) collective-permute-start(bf16[1,126,512]{2,1,0:T(8,128)(2,1)S(1)} %get-tuple-element.82), channel_id=1, source_target_pairs={{0,64},{64,0},{128,192},{192,128},{256,320},{320,256},{384,448},{4... | collective-permute-start | bytes 387080 | tf_op jit(solution)/shard_map/ppermute | solution.py:19
  124.6 10.9 %collective-permute-start.18 = (bf16[1,126,512]{2,1,0:T(8,128)(2,1)S(1)}, bf16[1,126,512]{2,1,0:T(8,128)(2,1)S(1)}, u32[]{:S(2)}, u32[]{:S(2)}) collective-permute-start(bf16[1,126,512]{2,1,0:T(8,128)(2,1)S(1)} %shard_map.128), channel_id=1, source_target_pairs={{0,32},{32,0},{1,33},{33,1},{2,34},{34,2},{3,35},{35,3},{4,36},{36... | collective-permute-start | bytes 387080 | tf_op jit(solution)/shard_map/ppermute | solution.py:23
  129.9 7.0 %collective-permute-start.19 = (bf16[1,126,512]{2,1,0:T(8,128)(2,1)S(1)}, bf16[1,126,512]{2,1,0:T(8,128)(2,1)S(1)}, u32[]{:S(2)}, u32[]{:S(2)}) collective-permute-start(bf16[1,126,512]{2,1,0:T(8,128)(2,1)S(1)} %get-tuple-element.99), channel_id=1, source_target_pairs={{0,64},{64,0},{128,192},{192,128},{256,320},{320,256},{384,448},{4... | collective-permute-start | bytes 387080 | tf_op jit(solution)/shard_map/ppermute | solution.py:19
  (6 other events, 14.0 us)

commit v6 on v5

--- a/solution.py
+++ b/solution.py
@@ -259,13 +259,11 @@
     far_sum = total(far_terms[1], got, BF16, 0)
     far_sum, near_got = together((far_sum, near_got))
     near_sum = total(near_terms[2], near_got, BF16, 4 * 10**9)
-    got, near_got = together((swap_z(far_sum, 1), swap_z(near_sum, 0)))
+    got, near_got = swap_z(far_sum, 1), swap_z(near_sum, 0)
     far_keep, far_send = split(far_terms[0], got)
-    far_send, near_got = together((far_send, near_got))
     near_sum = total(near_terms[1], near_got, BF16, 4 * 10**9)
-    got, near_got = together((swap_z(far_send, 0), swap_z(near_sum, 1)))
+    got, near_got = swap_z(far_send, 0), swap_z(near_sum, 1)
     far_sum = total(far_keep, got, BF16)
-    far_sum, near_got = together((far_sum, near_got))
     near_keep, near_send = split(near_terms[0], near_got, 4 * 10**9)
     near_got = swap_z(near_send, 0)
     got = swap(far_sum, "yh")

time: 139 us -> 137 us (0.986)
  the two profiles are of different devices: /device:TPU:2 before, /device:TPU:18 now
where the time goes in v6:
time: 137 us; the launch traced here: 136 us
  starting transfers between devices  85.7 us (63%)
  waiting for transfers between devices  29.3 us (21%)
  Pallas kernels  16.8 us (12%)
  other arithmetic  2.24 us (2%)
    ppermute x16, starting transfers between devices, swap_z(): return lax.ppermute(rows, 'z', pairs)  57 us
    ppermute x16, waiting for transfers between devices, swap_z(): return lax.ppermute(rows, 'z', pairs)  22.6 us
    ppermute x4, starting transfers between devices, swap(): return lax.ppermute(rows, axis, [(0, 1), (1, 0)])  13.8 us
    pallas_call x3, Pallas kernels, expert_call(): got = call(mine, theirs, *pieces, *sums)  12 us
    all_to_all x1, starting transfers between devices, shards(): lax.all_to_all(add(local, rest).astype(BF16), ('x', 'yl'), 0, 0, tiled=True)  7.67 us
    all_to_all x1, starting transfers between devices, shards(): mine = lax.all_to_all(send, ('x', 'yl'), 0, 0, tiled=True)  7.31 us
    ppermute x4, waiting for transfers between devices, swap(): return lax.ppermute(rows, axis, [(0, 1), (1, 0)])  5.84 us
  transfers between devices with their start and end apart: 22, of which 10 were waited for; matrix products, arithmetic and copies ran while one was open for 1% of the time, Pallas kernels for 10%

profile of v6, /device:TPU:18, one launch (start us, length us, event | category | flops | bytes accessed | tf_op | source)
XLA Modules:
  0.0 135.9 jit_solution(16232212005853116047)
XLA Ops:
  1.5 5.9 %collective-permute-start = (bf16[1,126,512]{2,1,0:T(8,128)(2,1)S(1)}, bf16[1,126,512]{2,1,0:T(8,128)(2,1)S(1)}, u32[]{:S(2)}, u32[]{:S(2)}) collective-permute-start(bf16[1,126,512]{2,1,0:T(8,128)(2,1)S(1)} %maximum_bitcast_fusion), channel_id=1, source_target_pairs={{0,32},{32,0},{1,33},{33,1},{2,34},{34,2},{3,35},{35,3},{4,36},{36... | collective-permute-start | bytes 387080 | tf_op jit(solution)/shard_map/ppermute | solution.py:23
  7.5 4.3 %collective-permute-start.1 = (bf16[1,126,512]{2,1,0:T(8,128)(2,1)S(1)}, bf16[1,126,512]{2,1,0:T(8,128)(2,1)S(1)}, u32[]{:S(2)}, u32[]{:S(2)}) collective-permute-start(bf16[1,126,512]{2,1,0:T(8,128)(2,1)S(1)} %maximum_bitcast_fusion), channel_id=1, source_target_pairs={{0,64},{64,0},{128,192},{192,128},{256,320},{320,256},{384,448},{4... | collective-permute-start | bytes 387080 | tf_op jit(solution)/shard_map/ppermute | solution.py:19
  11.7 2.6 %shard_map.118 = (bf16[16,64,512]{2,1,0:T(8,128)(2,1)}, bf16[512,128]{1,0:T(8,128)(2,1)}, bf16[512,128]{1,0:T(8,128)(2,1)}) custom-call(bf16[128,512]{1,0:T(8,128)(2,1)} %latent.1, bf16[128,512]{1,0:T(8,128)(2,1)} %cotangent.3, s32[2,128]{1,0:T(2,128)} %bitcast.16, f32[2,128]{1,0:T(2,128)} %bitcast.11), custom_call_target="tpu_custom_call" | custom-call | bytes 1048576 | tf_op jit(solution)/shard_map/pallas_call | solution.py:228
  15.4 4.3 %collective-permute-start.5 = (bf16[1,126,512]{2,1,0:T(8,128)(2,1)S(1)}, bf16[1,126,512]{2,1,0:T(8,128)(2,1)S(1)}, u32[]{:S(2)}, u32[]{:S(2)}) collective-permute-start(bf16[1,126,512]{2,1,0:T(8,128)(2,1)S(1)} %collective-permute-done.one), channel_id=1, source_target_pairs={{0,64},{64,0},{128,192},{192,128},{256,320},{320,256},{384,448},{4... | collective-permute-start | bytes 387080 | tf_op jit(solution)/shard_map/ppermute | solution.py:19
  19.7 9.1 %collective-permute-start.2 = (bf16[2,126,512]{2,1,0:T(8,128)(2,1)S(1)}, bf16[2,126,512]{2,1,0:T(8,128)(2,1)S(1)}, u32[]{:S(2)}, u32[]{:S(2)}) collective-permute-start(bf16[2,126,512]{2,1,0:T(8,128)(2,1)S(1)} %pad_maximum_fusion.refs_2_), channel_id=1, source_target_pairs={{0,448},{64,128},{128,64},{192,256},{256,192},{320,384},{384,320},... | collective-permute-start | bytes 774152 | tf_op jit(solution)/shard_map/ppermute | solution.py:19
  28.9 7.3 %all-to-all-start = ((bf16[16,64,512]{2,1,0:T(8,128)(2,1)}), bf16[16,64,512]{2,1,0:T(8,128)(2,1)S(1)}, u32[]{:S(2)}, u32[]{:S(2)}) async-start(bf16[16,64,512]{2,1,0:T(8,128)(2,1)} %get-tuple-element.50), calls=%async_computation | async-start | bytes 2097152 | tf_op jit(solution)/shard_map/all_to_all | solution.py:235
  40.1 5.6 %collective-permute-done.6.refs_3_ = bf16[2,126,512]{2,1,0:T(8,128)(2,1)S(1)} collective-permute-done((bf16[2,126,512]{2,1,0:T(8,128)(2,1)S(1)}, bf16[2,126,512]{2,1,0:T(8,128)(2,1)S(1)}, u32[]{:S(2)}, u32[]{:S(2)}) %collective-permute-start.6) | collective-permute-done | bytes 258080 | tf_op jit(solution)/shard_map/ppermute | solution.py:19
  47.6 5.6 %collective-permute-start.4 = (bf16[2,126,512]{2,1,0:T(8,128)(2,1)S(1)}, bf16[2,126,512]{2,1,0:T(8,128)(2,1)S(1)}, u32[]{:S(2)}, u32[]{:S(2)}) collective-permute-start(bf16[2,126,512]{2,1,0:T(8,128)(2,1)S(1)} %collective-permute-done.3.refs_4_), channel_id=1, source_target_pairs={{0,448},{64,128},{128,64},{192,256},{256,192},{320,384},{384,320},... | collective-permute-start | bytes 774152 | tf_op jit(solution)/shard_map/ppermute | solution.py:19
  53.9 3.6 %collective-permute-done.4.refs_5_ = bf16[2,126,512]{2,1,0:T(8,128)(2,1)S(1)} collective-permute-done((bf16[2,126,512]{2,1,0:T(8,128)(2,1)S(1)}, bf16[2,126,512]{2,1,0:T(8,128)(2,1)S(1)}, u32[]{:S(2)}, u32[]{:S(2)}) %collective-permute-start.4) | collective-permute-done | bytes 258080 | tf_op jit(solution)/shard_map/ppermute | solution.py:19
  60.3 4.3 %collective-permute-start.9 = (bf16[2,126,512]{2,1,0:T(8,128)(2,1)S(1)}, bf16[2,126,512]{2,1,0:T(8,128)(2,1)S(1)}, u32[]{:S(2)}, u32[]{:S(2)}) collective-permute-start(bf16[2,126,512]{2,1,0:T(8,128)(2,1)S(1)} %collective-permute-done.7.refs_4_), channel_id=1, source_target_pairs={{0,448},{64,128},{128,64},{192,256},{256,192},{320,384},{384,320},... | collective-permute-start | bytes 774152 | tf_op jit(solution)/shard_map/ppermute | solution.py:19
  64.6 4.8 %shard_map.120 = (bf16[2,126,512]{2,1,0:T(8,128)(2,1)S(1)}, bf16[2,126,512]{2,1,0:T(8,128)(2,1)S(1)}, bf16[2,126,512]{2,1,0:T(8,128)(2,1)S(1)}, bf16[2,126,512]{...) custom-call(bf16[16,64,512]{2,1,0:T(8,128)(2,1)S(1)} %all-to-all-done.refs_0_, ...), custom_call_target="tpu_custom_call" | custom-call | flops 3623878656 | bytes 1048576 | tf_op jit(solution)/shard_map/pallas_call | solution.py:170
  70.2 4.5 %shard_map.121 = (bf16[2,126,512]{2,1,0:T(8,128)(2,1)S(1)}, bf16[2,126,512]{2,1,0:T(8,128)(2,1)S(1)}, bf16[2,126,512]{2,1,0:T(8,128)(2,1)S(1)}, f32[16,64,512]{2,1,0:T(8,128)S(1)}, f32[16,64,512]{2,1,0:T(8,128)S(1)}) custom-call(bf16[16,64,512]{2,1,0:T(8,128)(2,1)S(1)} %all-to-all-done.refs_0_, bf16[16,64,512]{2,1,0:T(8,128)(2,1)S(1)} %collective-permute-done.8.refs_1_, ...), custom_call_target="tpu_custom_call" | custom-call | flops 2717908992 | bytes 1048576 | tf_op jit(solution)/shard_map/pallas_call | solution.py:170
  74.7 2.6 %shard_map.122 = (bf16[2,126,512]{2,1,0:T(8,128)(2,1)S(1)}, f32[16,64,512]{2,1,0:T(8,128)S(1)}, bf16[16,64,512]{2,1,0:T(8,128)(2,1)S(1)}) custom-call(bf16[16,64,512]{2,1,0:T(8,128)(2,1)S(1)} %all-to-all-done.refs_0_, bf16[16,64,512]{2,1,0:T(8,128)(2,1)S(1)} %collective-permute-done.8.refs_1_, bf16[2,126,512]{2,1,0:T(8,128)(2,1)S(1)} %collective-permute-done.9.refs_2_, ...), custom_call_target="tpu_custom_call" | custom-call | flops 905969664 | bytes 1048576 | tf_op jit(solution)/shard_map/pallas_call | solution.py:170
  77.3 2.8 %collective-permute-start.10 = (bf16[2,126,512]{2,1,0:T(8,128)(2,1)S(1)}, bf16[2,126,512]{2,1,0:T(8,128)(2,1)S(1)}, u32[]{:S(2)}, u32[]{:S(2)}) collective-permute-start(bf16[2,126,512]{2,1,0:T(8,128)(2,1)S(1)} %get-tuple-element.61), channel_id=1, source_target_pairs={{0,448},{64,128},{128,64},{192,256},{256,192},{320,384},{384,320},... | collective-permute-start | bytes 774152 | tf_op jit(solution)/shard_map/ppermute | solution.py:19
  82.0 4.3 %collective-permute-start.13 = (bf16[2,126,512]{2,1,0:T(8,128)(2,1)S(1)}, bf16[2,126,512]{2,1,0:T(8,128)(2,1)S(1)}, u32[]{:S(2)}, u32[]{:S(2)}) collective-permute-start(bf16[2,126,512]{2,1,0:T(8,128)(2,1)S(1)} %get-tuple-element.64), channel_id=1, source_target_pairs={{0,448},{64,128},{128,64},{192,256},{256,192},{320,384},{384,320},... | collective-permute-start | bytes 774152 | tf_op jit(solution)/shard_map/ppermute | solution.py:19
  86.3 3.1 %collective-permute-done.10.two = bf16[2,126,512]{2,1,0:T(8,128)(2,1)S(1)} collective-permute-done((bf16[2,126,512]{2,1,0:T(8,128)(2,1)S(1)}, bf16[2,126,512]{2,1,0:T(8,128)(2,1)S(1)}, u32[]{:S(2)}, u32[]{:S(2)}) %collective-permute-start.10) | collective-permute-done | bytes 258080 | tf_op jit(solution)/shard_map/ppermute | solution.py:19
  92.8 7.7 %all-to-all-start.1 = ((bf16[16,64,512]{2,1,0:T(8,128)(2,1)}), bf16[16,64,512]{2,1,0:T(8,128)(2,1)S(1)}, u32[]{:S(2)}, u32[]{:S(2)}) async-start(bf16[16,64,512]{2,1,0:T(8,128)(2,1)} %add_convert_fusion), calls=%async_computation.1 | async-start | bytes 2097152 | tf_op jit(solution)/shard_map/all_to_all | solution.py:257
  100.6 3.9 %collective-permute-start.17 = (bf16[2,126,512]{2,1,0:T(8,128)(2,1)S(1)}, bf16[2,126,512]{2,1,0:T(8,128)(2,1)S(1)}, u32[]{:S(2)}, u32[]{:S(2)}) collective-permute-start(bf16[2,126,512]{2,1,0:T(8,128)(2,1)S(1)} %shard_map.128), channel_id=1, source_target_pairs={{0,64},{64,0},{128,192},{192,128},{256,320},{320,256},{384,448},{4... | collective-permute-start | bytes 774152 | tf_op jit(solution)/shard_map/ppermute | solution.py:19
  104.6 3.3 %collective-permute-start.14 = (bf16[2,126,512]{2,1,0:T(8,128)(2,1)S(1)}, bf16[2,126,512]{2,1,0:T(8,128)(2,1)S(1)}, u32[]{:S(2)}, u32[]{:S(2)}) collective-permute-start(bf16[2,126,512]{2,1,0:T(8,128)(2,1)S(1)} %shard_map.124), channel_id=1, source_target_pairs={{0,448},{64,128},{128,64},{192,256},{256,192},{320,384},{384,320},... | collective-permute-start | bytes 774152 | tf_op jit(solution)/shard_map/ppermute | solution.py:19
  109.1 3.5 %collective-permute-start.18 = (bf16[2,126,512]{2,1,0:T(8,128)(2,1)S(1)}, bf16[2,126,512]{2,1,0:T(8,128)(2,1)S(1)}, u32[]{:S(2)}, u32[]{:S(2)}) collective-permute-start(bf16[2,126,512]{2,1,0:T(8,128)(2,1)S(1)} %shard_map.129), channel_id=1, source_target_pairs={{0,448},{64,128},{128,64},{192,256},{256,192},{320,384},{384,320},... | collective-permute-start | bytes 774152 | tf_op jit(solution)/shard_map/ppermute | solution.py:19
  112.5 3.5 %collective-permute-done.14.two = bf16[2,126,512]{2,1,0:T(8,128)(2,1)S(1)} collective-permute-done((bf16[2,126,512]{2,1,0:T(8,128)(2,1)S(1)}, bf16[2,126,512]{2,1,0:T(8,128)(2,1)S(1)}, u32[]{:S(2)}, u32[]{:S(2)}) %collective-permute-start.14) | collective-permute-done | bytes 258080 | tf_op jit(solution)/shard_map/ppermute | solution.py:19
  118.0 4.9 %collective-permute-done.15.two = bf16[1,126,512]{2,1,0:T(8,128)(2,1)S(1)} collective-permute-done((bf16[1,126,512]{2,1,0:T(8,128)(2,1)S(1)}, bf16[1,126,512]{2,1,0:T(8,128)(2,1)S(1)}, u32[]{:S(2)}, u32[]{:S(2)}) %collective-permute-start.15) | collective-permute-done | bytes 129056 | tf_op jit(solution)/shard_map/ppermute | solution.py:19
  123.0 4.0 %collective-permute-start.16 = (bf16[1,126,512]{2,1,0:T(8,128)(2,1)S(1)}, bf16[1,126,512]{2,1,0:T(8,128)(2,1)S(1)}, u32[]{:S(2)}, u32[]{:S(2)}) collective-permute-start(bf16[1,126,512]{2,1,0:T(8,128)(2,1)S(1)} %shard_map.126), channel_id=1, source_target_pairs={{0,32},{32,0},{1,33},{33,1},{2,34},{34,2},{3,35},{35,3},{4,36},{36... | collective-permute-start | bytes 387080 | tf_op jit(solution)/shard_map/ppermute | solution.py:23
  130.4 4.7 %collective-permute-done.16.far = bf16[1,126,512]{2,1,0:T(8,128)(2,1)S(1)} collective-permute-done((bf16[1,126,512]{2,1,0:T(8,128)(2,1)S(1)}, bf16[1,126,512]{2,1,0:T(8,128)(2,1)S(1)}, u32[]{:S(2)}, u32[]{:S(2)}) %collective-permute-start.16) | collective-permute-done | bytes 129056 | tf_op jit(solution)/shard_map/ppermute | solution.py:23
  (53 shorter events, 24.6 us)
Async XLA Ops:
  1.5 13.9 %collective-permute-start = (bf16[1,126,512]{2,1,0:T(8,128)(2,1)S(1)}, bf16[1,126,512]{2,1,0:T(8,128)(2,1)S(1)}, u32[]{:S(2)}, u32[]{:S(2)}) collective-permute-start(bf16[1,126,512]{2,1,0:T(8,128)(2,1)S(1)} %maximum_bitcast_fusion), channel_id=1, source_target_pairs={{0,32},{32,0},{1,33},{33,1},{2,34},{34,2},{3,35},{35,3},{4,36},{36... | collective-permute-start | bytes 387080 | tf_op jit(solution)/shard_map/ppermute | solution.py:23
  7.5 8.0 %collective-permute-start.1 = (bf16[1,126,512]{2,1,0:T(8,128)(2,1)S(1)}, bf16[1,126,512]{2,1,0:T(8,128)(2,1)S(1)}, u32[]{:S(2)}, u32[]{:S(2)}) collective-permute-start(bf16[1,126,512]{2,1,0:T(8,128)(2,1)S(1)} %maximum_bitcast_fusion), channel_id=1, source_target_pairs={{0,64},{64,0},{128,192},{192,128},{256,320},{320,256},{384,448},{4... | collective-permute-start | bytes 387080 | tf_op jit(solution)/shard_map/ppermute | solution.py:19
  15.4 20.8 %collective-permute-start.5 = (bf16[1,126,512]{2,1,0:T(8,128)(2,1)S(1)}, bf16[1,126,512]{2,1,0:T(8,128)(2,1)S(1)}, u32[]{:S(2)}, u32[]{:S(2)}) collective-permute-start(bf16[1,126,512]{2,1,0:T(8,128)(2,1)S(1)} %collective-permute-done.one), channel_id=1, source_target_pairs={{0,64},{64,0},{128,192},{192,128},{256,320},{320,256},{384,448},{4... | collective-permute-start | bytes 387080 | tf_op jit(solution)/shard_map/ppermute | solution.py:19
  19.7 18.4 %collective-permute-start.2 = (bf16[2,126,512]{2,1,0:T(8,128)(2,1)S(1)}, bf16[2,126,512]{2,1,0:T(8,128)(2,1)S(1)}, u32[]{:S(2)}, u32[]{:S(2)}) collective-permute-start(bf16[2,126,512]{2,1,0:T(8,128)(2,1)S(1)} %pad_maximum_fusion.refs_2_), channel_id=1, source_target_pairs={{0,448},{64,128},{128,64},{192,256},{256,192},{320,384},{384,320},... | collective-permute-start | bytes 774152 | tf_op jit(solution)/shard_map/ppermute | solution.py:19
  28.9 29.5 %all-to-all-start = ((bf16[16,64,512]{2,1,0:T(8,128)(2,1)}), bf16[16,64,512]{2,1,0:T(8,128)(2,1)S(1)}, u32[]{:S(2)}, u32[]{:S(2)}) async-start(bf16[16,64,512]{2,1,0:T(8,128)(2,1)} %get-tuple-element.50), calls=%async_computation | async-start | bytes 2097152 | tf_op jit(solution)/shard_map/all_to_all | solution.py:235
  36.2 9.5 %collective-permute-start.6 = (bf16[2,126,512]{2,1,0:T(8,128)(2,1)S(1)}, bf16[2,126,512]{2,1,0:T(8,128)(2,1)S(1)}, u32[]{:S(2)}, u32[]{:S(2)}) collective-permute-start(bf16[2,126,512]{2,1,0:T(8,128)(2,1)S(1)} %shard_map.119.refs_2_), channel_id=1, source_target_pairs={{0,448},{64,128},{128,64},{192,256},{256,192},{320,384},{384,320},... | collective-permute-start | bytes 774152 | tf_op jit(solution)/shard_map/ppermute | solution.py:19
  38.2 9.5 %collective-permute-start.3 = (bf16[2,126,512]{2,1,0:T(8,128)(2,1)S(1)}, bf16[2,126,512]{2,1,0:T(8,128)(2,1)S(1)}, u32[]{:S(2)}, u32[]{:S(2)}) collective-permute-start(bf16[2,126,512]{2,1,0:T(8,128)(2,1)S(1)} %collective-permute-done.2.refs_3_), channel_id=1, source_target_pairs={{0,64},{64,0},{128,192},{192,128},{256,320},{320,256},{384,448},{4... | collective-permute-start | bytes 774152 | tf_op jit(solution)/shard_map/ppermute | solution.py:19
  45.7 8.3 %collective-permute-start.7 = (bf16[2,126,512]{2,1,0:T(8,128)(2,1)S(1)}, bf16[2,126,512]{2,1,0:T(8,128)(2,1)S(1)}, u32[]{:S(2)}, u32[]{:S(2)}) collective-permute-start(bf16[2,126,512]{2,1,0:T(8,128)(2,1)S(1)} %collective-permute-done.6.refs_3_), channel_id=1, source_target_pairs={{0,64},{64,0},{128,192},{192,128},{256,320},{320,256},{384,448},{4... | collective-permute-start | bytes 774152 | tf_op jit(solution)/shard_map/ppermute | solution.py:19
  47.6 10.0 %collective-permute-start.4 = (bf16[2,126,512]{2,1,0:T(8,128)(2,1)S(1)}, bf16[2,126,512]{2,1,0:T(8,128)(2,1)S(1)}, u32[]{:S(2)}, u32[]{:S(2)}) collective-permute-start(bf16[2,126,512]{2,1,0:T(8,128)(2,1)S(1)} %collective-permute-done.3.refs_4_), channel_id=1, source_target_pairs={{0,448},{64,128},{128,64},{192,256},{256,192},{320,384},{384,320},... | collective-permute-start | bytes 774152 | tf_op jit(solution)/shard_map/ppermute | solution.py:19
  58.4 6.2 %collective-permute-start.8 = (bf16[16,64,512]{2,1,0:T(8,128)(2,1)S(1)}, bf16[16,64,512]{2,1,0:T(8,128)(2,1)S(1)}, u32[]{:S(2)}, u32[]{:S(2)}) collective-permute-start(bf16[16,64,512]{2,1,0:T(8,128)(2,1)S(1)} %all-to-all-done.refs_0_), channel_id=1, source_target_pairs={{0,16},{16,0},{1,17},{17,1},{2,18},{18,2},{3,19},{19,3},{4,20},{20... | collective-permute-start | bytes 3145736 | tf_op jit(solution)/shard_map/ppermute | solution.py:23
  60.3 14.4 %collective-permute-start.9 = (bf16[2,126,512]{2,1,0:T(8,128)(2,1)S(1)}, bf16[2,126,512]{2,1,0:T(8,128)(2,1)S(1)}, u32[]{:S(2)}, u32[]{:S(2)}) collective-permute-start(bf16[2,126,512]{2,1,0:T(8,128)(2,1)S(1)} %collective-permute-done.7.refs_4_), channel_id=1, source_target_pairs={{0,448},{64,128},{128,64},{192,256},{256,192},{320,384},{384,320},... | collective-permute-start | bytes 774152 | tf_op jit(solution)/shard_map/ppermute | solution.py:19
  77.3 12.1 %collective-permute-start.10 = (bf16[2,126,512]{2,1,0:T(8,128)(2,1)S(1)}, bf16[2,126,512]{2,1,0:T(8,128)(2,1)S(1)}, u32[]{:S(2)}, u32[]{:S(2)}) collective-permute-start(bf16[2,126,512]{2,1,0:T(8,128)(2,1)S(1)} %get-tuple-element.61), channel_id=1, source_target_pairs={{0,448},{64,128},{128,64},{192,256},{256,192},{320,384},{384,320},... | collective-permute-start | bytes 774152 | tf_op jit(solution)/shard_map/ppermute | solution.py:19
  80.1 9.4 %collective-permute-start.11 = (bf16[16,64,512]{2,1,0:T(8,128)(2,1)S(1)}, bf16[16,64,512]{2,1,0:T(8,128)(2,1)S(1)}, u32[]{:S(2)}, u32[]{:S(2)}) collective-permute-start(bf16[16,64,512]{2,1,0:T(8,128)(2,1)S(1)} %get-tuple-element.62), channel_id=1, source_target_pairs={{0,16},{16,0},{1,17},{17,1},{2,18},{18,2},{3,19},{19,3},{4,20},{20... | collective-permute-start | bytes 3145736 | tf_op jit(solution)/shard_map/ppermute | solution.py:23
  82.0 18.4 %collective-permute-start.13 = (bf16[2,126,512]{2,1,0:T(8,128)(2,1)S(1)}, bf16[2,126,512]{2,1,0:T(8,128)(2,1)S(1)}, u32[]{:S(2)}, u32[]{:S(2)}) collective-permute-start(bf16[2,126,512]{2,1,0:T(8,128)(2,1)S(1)} %get-tuple-element.64), channel_id=1, source_target_pairs={{0,448},{64,128},{128,64},{192,256},{256,192},{320,384},{384,320},... | collective-permute-start | bytes 774152 | tf_op jit(solution)/shard_map/ppermute | solution.py:19
  89.5 10.9 %collective-permute-start.12 = (bf16[2,126,512]{2,1,0:T(8,128)(2,1)S(1)}, bf16[2,126,512]{2,1,0:T(8,128)(2,1)S(1)}, u32[]{:S(2)}, u32[]{:S(2)}) collective-permute-start(bf16[2,126,512]{2,1,0:T(8,128)(2,1)S(1)} %shard_map.123), channel_id=1, source_target_pairs={{0,64},{64,0},{128,192},{192,128},{256,320},{320,256},{384,448},{4... | collective-permute-start | bytes 774152 | tf_op jit(solution)/shard_map/ppermute | solution.py:19
  92.8 7.8 %copy-start.7 = (bf16[2,126,512]{2,1,0:T(8,128)(2,1)S(1)}, bf16[2,126,512]{2,1,0:T(8,128)(2,1)}, u32[]{:S(2)}) copy-start(bf16[2,126,512]{2,1,0:T(8,128)(2,1)} %copy-done.6) | copy-start | bytes 774148
  92.8 36.4 %all-to-all-start.1 = ((bf16[16,64,512]{2,1,0:T(8,128)(2,1)}), bf16[16,64,512]{2,1,0:T(8,128)(2,1)S(1)}, u32[]{:S(2)}, u32[]{:S(2)}) async-start(bf16[16,64,512]{2,1,0:T(8,128)(2,1)} %add_convert_fusion), calls=%async_computation.1 | async-start | bytes 2097152 | tf_op jit(solution)/shard_map/all_to_all | solution.py:257
  100.6 8.4 %copy-start.5 = (bf16[2,126,512]{2,1,0:T(8,128)(2,1)S(1)}, bf16[2,126,512]{2,1,0:T(8,128)(2,1)}, u32[]{:S(2)}) copy-start(bf16[2,126,512]{2,1,0:T(8,128)(2,1)} %copy-done.4) | copy-start | bytes 774148
  100.6 8.4 %collective-permute-start.17 = (bf16[2,126,512]{2,1,0:T(8,128)(2,1)S(1)}, bf16[2,126,512]{2,1,0:T(8,128)(2,1)S(1)}, u32[]{:S(2)}, u32[]{:S(2)}) collective-permute-start(bf16[2,126,512]{2,1,0:T(8,128)(2,1)S(1)} %shard_map.128), channel_id=1, source_target_pairs={{0,64},{64,0},{128,192},{192,128},{256,320},{320,256},{384,448},{4... | collective-permute-start | bytes 774152 | tf_op jit(solution)/shard_map/ppermute | solution.py:19
  104.6 11.4 %collective-permute-start.14 = (bf16[2,126,512]{2,1,0:T(8,128)(2,1)S(1)}, bf16[2,126,512]{2,1,0:T(8,128)(2,1)S(1)}, u32[]{:S(2)}, u32[]{:S(2)}) collective-permute-start(bf16[2,126,512]{2,1,0:T(8,128)(2,1)S(1)} %shard_map.124), channel_id=1, source_target_pairs={{0,448},{64,128},{128,64},{192,256},{256,192},{320,384},{384,320},... | collective-permute-start | bytes 774152 | tf_op jit(solution)/shard_map/ppermute | solution.py:19
  109.1 17.9 %collective-permute-start.18 = (bf16[2,126,512]{2,1,0:T(8,128)(2,1)S(1)}, bf16[2,126,512]{2,1,0:T(8,128)(2,1)S(1)}, u32[]{:S(2)}, u32[]{:S(2)}) collective-permute-start(bf16[2,126,512]{2,1,0:T(8,128)(2,1)S(1)} %shard_map.129), channel_id=1, source_target_pairs={{0,448},{64,128},{128,64},{192,256},{256,192},{320,384},{384,320},... | collective-permute-start | bytes 774152 | tf_op jit(solution)/shard_map/ppermute | solution.py:19
  116.1 6.9 %collective-permute-start.15 = (bf16[1,126,512]{2,1,0:T(8,128)(2,1)S(1)}, bf16[1,126,512]{2,1,0:T(8,128)(2,1)S(1)}, u32[]{:S(2)}, u32[]{:S(2)}) collective-permute-start(bf16[1,126,512]{2,1,0:T(8,128)(2,1)S(1)} %get-tuple-element.69), channel_id=1, source_target_pairs={{0,64},{64,0},{128,192},{192,128},{256,320},{320,256},{384,448},{4... | collective-permute-start | bytes 387080 | tf_op jit(solution)/shard_map/ppermute | solution.py:19
  123.0 12.2 %collective-permute-start.16 = (bf16[1,126,512]{2,1,0:T(8,128)(2,1)S(1)}, bf16[1,126,512]{2,1,0:T(8,128)(2,1)S(1)}, u32[]{:S(2)}, u32[]{:S(2)}) collective-permute-start(bf16[1,126,512]{2,1,0:T(8,128)(2,1)S(1)} %shard_map.126), channel_id=1, source_target_pairs={{0,32},{32,0},{1,33},{33,1},{2,34},{34,2},{3,35},{35,3},{4,36},{36... | collective-permute-start | bytes 387080 | tf_op jit(solution)/shard_map/ppermute | solution.py:23
  127.1 8.0 %collective-permute-start.19 = (bf16[1,126,512]{2,1,0:T(8,128)(2,1)S(1)}, bf16[1,126,512]{2,1,0:T(8,128)(2,1)S(1)}, u32[]{:S(2)}, u32[]{:S(2)}) collective-permute-start(bf16[1,126,512]{2,1,0:T(8,128)(2,1)S(1)} %get-tuple-element.83), channel_id=1, source_target_pairs={{0,64},{64,0},{128,192},{192,128},{256,320},{320,256},{384,448},{4... | collective-permute-start | bytes 387080 | tf_op jit(solution)/shard_map/ppermute | solution.py:19
  (6 other events, 14.0 us)
